TPU v7x, 32 devices: a whole 2x2x4 slice. The times are simulated.
32 devices in a mesh: dp: 2 (over x), seq: 16 (over z, y, core).
Axes of the slice: x: 2, y: 2, z: 4, core: 2. Of those that a mesh axis runs over, the one named last changes fastest.
Arguments:
- queries: bfloat16 [2, 2048, 1024], P('dp', 'seq'), may hold values from -6 to 6
- keys: bfloat16 [2, 2048, 1024], P('dp', 'seq'), may hold values from -6 to 6
- values: bfloat16 [2, 2048, 1024], P('dp', 'seq'), may hold values from -6 to 6
- grad_out: bfloat16 [2, 2048, 1024], P('dp', 'seq'), may hold values from -6 to 6
- mem_keys: bfloat16 [16, 512, 1024], P('dp', 'seq'), may hold values from -6 to 6
- mem_values: bfloat16 [16, 512, 1024], P('dp', 'seq'), may hold values from -6 to 6
- seq_lengths: int32 [2], replicated, may hold values from 256 to 2048, as said below
- mem_counts: int32 [2], replicated, may hold values from 1 to 4, as said below
- block_lists: int32 [2, 4], replicated, may hold values from 0 to 15, as said below
- block_slots: int32 [16], replicated, may hold values from 0 to 15, each once
Outputs:
- grad_queries: bfloat16 [2, 2048, 1024], P('dp', 'seq')
- grad_keys: bfloat16 [2, 2048, 1024], P('dp', 'seq')
- grad_values: bfloat16 [2, 2048, 1024], P('dp', 'seq')
Inputs may be any that keep to these rules, and one draw needn't show every extreme that they name: `seq_lengths`: some user has all 2048 events. `mem_counts`: some user attends to all 4 listed blocks. `block_lists`: the 4 ids of one user are distinct. `block_slots`: A permutation of the block ids.
All inputs are finite; a program needn't handle non-finite values.
Results may differ from a plain program's by a relative error of at most 0.0063.
Values may be sent and summed in bfloat16 or wider, within the bound.
No kernel may reach another device: no remote copies, remote signals or barrier semaphores. Data moves between devices by JAX's collectives and lax.ppermute only.
A program may use at most 128 MiB of HBM per device.

v0:
```python
import functools
import math

import jax
import jax.numpy as jnp
from jax import lax
from jax.experimental import pallas as pl
from jax.experimental.pallas import tpu as pltpu
from jax.sharding import PartitionSpec as P

H = 8
WINDOW = 512
TILE = 256
NEG = -1e30
LOG2E = 1.4426950408889634
VMEM_LIMIT = 48 * 1024 * 1024
VMEM_WHOLE = 64 * 1024 * 1024 - 256 * 1024

NT = (((1,), (1,)), ((), ()))
TN = (((0,), (0,)), ((), ()))


def dot_nt(a, b):
    return lax.dot_general(a, b, NT, preferred_element_type=jnp.float32)


def dot_tn(a, b):
    return lax.dot_general(a, b, TN, preferred_element_type=jnp.float32)


def dot_nn(a, b):
    return jnp.dot(a, b, preferred_element_type=jnp.float32)


def call(body, limit=VMEM_LIMIT, **kw):
    return pl.pallas_call(
        body, compiler_params=pltpu.CompilerParams(vmem_limit_bytes=limit), **kw
    )


def load_listed(user, slots_ref, lists_ref, mk_ref, mv_ref, buffer, sems):
    copies = []
    for block in range(buffer.shape[0]):
        index = lax.rem(slots_ref[lists_ref[user, block]], mk_ref.shape[0])
        for part, pool in enumerate((mk_ref, mv_ref)):
            copies.append(
                pltpu.make_async_copy(
                    pool.at[index], buffer.at[block, part], sems.at[block, part]
                )
            )
    for copy in copies:
        copy.start()
    return copies


def split_parity(buffer, same_ref, other_ref):
    blocks, parts, depth, width = buffer.shape
    hd = width // H
    odd = lax.rem(lax.axis_index("seq"), 2) == 1
    for block in range(blocks):
        rows = slice(block * depth, (block + 1) * depth)
        for part in range(parts):
            for pair in range(H // 2):
                first = buffer[block, part, :, 2 * pair * hd : (2 * pair + 1) * hd]
                second = buffer[block, part, :, (2 * pair + 1) * hd : (2 * pair + 2) * hd]
                same_ref[pair, part, rows] = jnp.where(odd, second, first)
                other_ref[pair, part, rows] = jnp.where(odd, first, second)


def pack_body(users, slots_ref, lists_ref, *refs):
    (q_ref, k_ref, v_ref, g_ref, mk_ref, mv_ref), refs = refs[:6], refs[6:]
    same, other, edge_ref = refs[:users], refs[users : 2 * users], refs[2 * users]
    buffer, sems, edge_sems = refs[2 * users + 1 :]
    user = lax.axis_index("dp")
    early = lax.rem(lax.axis_index("seq"), H) < WINDOW // q_ref.shape[1]
    loads = [
        load_listed(
            lax.rem(user + step, users),
            slots_ref,
            lists_ref,
            mk_ref,
            mv_ref,
            buffer.at[step],
            sems.at[step],
        )
        for step in range(users)
    ]

    @pl.when(early)
    def _():
        for part, ref in enumerate((q_ref, g_ref)):
            pltpu.make_async_copy(ref.at[0], edge_ref.at[part], edge_sems.at[part]).start()

    @pl.when(jnp.logical_not(early))
    def _():
        for part, ref in enumerate((k_ref, v_ref)):
            pltpu.make_async_copy(ref.at[0], edge_ref.at[part], edge_sems.at[part]).start()

    for step in range(users):
        for copy in loads[step]:
            copy.wait()
        split_parity(buffer.at[step], same[step], other[step])
    for part in range(2):
        pltpu.make_async_copy(q_ref.at[0], edge_ref.at[part], edge_sems.at[part]).wait()


def pack(users, block_slots, block_lists, events, mem_keys, mem_values):
    _, depth, width = mem_keys.shape
    blocks = block_lists.shape[1]
    rows = events[0].shape[1]
    dtype = mem_keys.dtype
    smem = pl.BlockSpec(memory_space=pltpu.SMEM)
    hbm = pl.BlockSpec(memory_space=pltpu.HBM)
    pieces = jax.ShapeDtypeStruct((H // 2, 2, blocks * depth, width // H), dtype)
    return call(
        functools.partial(pack_body, users),
        limit=VMEM_WHOLE,
        in_specs=[smem] * 2 + [hbm] * 6,
        out_specs=[pl.BlockSpec(memory_space=pltpu.VMEM)] * (2 * users + 1),
        out_shape=[pieces] * (2 * users) + [jax.ShapeDtypeStruct((2, rows, width), dtype)],
        scratch_shapes=[
            pltpu.VMEM((users, blocks, 2, depth, width), dtype),
            pltpu.SemaphoreType.DMA((users, blocks, 2)),
            pltpu.SemaphoreType.DMA((2,)),
        ],
    )(block_slots, block_lists, *events, mem_keys, mem_values)


def split_body(hd, length_ref, *refs):
    sources, (_, out_ref, buffer, sems) = refs[:4], refs[4:]
    rows = buffer.shape[1]
    copies = [
        pltpu.make_async_copy(source.at[0], buffer.at[part], sems.at[part])
        for part, source in enumerate(sources)
    ]
    for copy in copies:
        copy.start()
    live = length_ref[lax.axis_index("dp")] - lax.axis_index("seq") * rows
    position = lax.broadcasted_iota(jnp.int32, (rows, hd), 0)
    for part, copy in enumerate(copies):
        copy.wait()
        for head in range(H):
            block = buffer[part, :, head * hd : (head + 1) * hd]
            if part == 3:
                block = jnp.where(position < live, block.astype(jnp.float32), 0.0)
            out_ref[head, part] = block.astype(out_ref.dtype)


def split_heads(seq_lengths, arrays, later_than):
    _, rows, width = arrays[0].shape
    parts = len(arrays)
    hbm = pl.BlockSpec(memory_space=pltpu.HBM)
    return call(
        functools.partial(split_body, width // H),
        limit=VMEM_WHOLE,
        in_specs=[pl.BlockSpec(memory_space=pltpu.SMEM)]
        + [hbm] * parts
        + [pl.BlockSpec(memory_space=pl.ANY)],
        out_specs=pl.BlockSpec(memory_space=pltpu.VMEM),
        out_shape=jax.ShapeDtypeStruct((H, parts, rows, width // H), arrays[0].dtype),
        scratch_shapes=[
            pltpu.VMEM((parts, rows, width), arrays[0].dtype),
            pltpu.SemaphoreType.DMA((parts,)),
        ],
    )(seq_lengths, *arrays, later_than)


def edge_body(hd, length_ref, in_ref, *refs):
    out_ref = refs[-1]
    rows = in_ref.shape[1]
    reach = WINDOW // rows
    shard = lax.axis_index("seq")
    beyond = length_ref[lax.axis_index("dp")] - (shard + reach) * rows
    live = jnp.where(lax.rem(shard, H) < reach, rows, beyond)
    position = lax.broadcasted_iota(jnp.int32, (rows, hd), 0)
    for head in range(H):
        cols = slice(head * hd, (head + 1) * hd)
        out_ref[head, 0] = in_ref[0, :, cols]
        grad = in_ref[1, :, cols].astype(jnp.float32)
        out_ref[head, 1] = jnp.where(position < live, grad, 0.0).astype(out_ref.dtype)


def split_edge(seq_lengths, edge, *later_than):
    _, rows, width = edge.shape
    hd = width // H
    vmem = pl.BlockSpec(memory_space=pltpu.VMEM)
    return call(
        functools.partial(edge_body, hd),
        in_specs=[pl.BlockSpec(memory_space=pltpu.SMEM), vmem]
        + [pl.BlockSpec(memory_space=pl.ANY)] * len(later_than),
        out_specs=vmem,
        out_shape=jax.ShapeDtypeStruct((H, 2, rows, hd), edge.dtype),
    )(seq_lengths, edge, *later_than)


def memory_body(held, depth, slots_ref, lists_ref, _, *refs):
    outs = refs[-(H // 2) :]
    sources = refs[: -(H // 2)]
    users = len(sources) // 2
    user = lax.axis_index("dp")
    pair = lax.rem(lax.axis_index("seq") // 2, H // 2)
    for block in range(lists_ref.shape[1]):
        slot = slots_ref[lists_ref[user, block]]
        source = lax.rem(user - slot // held + users, users)
        rows = slice(block * depth, (block + 1) * depth)
        for step, out_ref in enumerate(outs):
            for side in range(2):
                for part in range(2):
                    value = sources[side][pair ^ step, part, rows]
                    for other in range(1, users):
                        value = jnp.where(
                            source == other, sources[2 * other + side][pair ^ step, part, rows], value
                        )
                    out_ref[part, side, rows] = value


def memory_pieces(held, depth, block_slots, block_lists, sources, later_than):
    _, parts, rows, hd = sources[0].shape
    smem = pl.BlockSpec(memory_space=pltpu.SMEM)
    vmem = pl.BlockSpec(memory_space=pltpu.VMEM)
    return call(
        functools.partial(memory_body, held, depth),
        in_specs=[smem] * 2 + [pl.BlockSpec(memory_space=pl.ANY)] + [vmem] * len(sources),
        out_specs=[vmem] * (H // 2),
        out_shape=[jax.ShapeDtypeStruct((parts, 2, rows, hd), sources[0].dtype)] * (H // 2),
    )(block_slots, block_lists, later_than, *sources)


def attend_body(
    scale,
    depth,
    half,
    memories,
    length_ref,
    count_ref,
    ev_ref,
    edge_ref,
    *refs,
):
    mem_refs, (gq_ref, gk_ref, gv_ref) = refs[:memories], refs[memories : memories + 3]
    k_all, v_all, mk_all, mv_all = refs[-4:]
    step = pl.program_id(0)
    hd = ev_ref.shape[-1]
    rows = ev_ref.shape[2]
    reach = WINDOW // rows
    user = lax.axis_index("dp")
    length, count = length_ref[user], count_ref[user]
    base = (lax.axis_index("seq") // H) * (H * rows) + half * WINDOW
    slope = scale * LOG2E
    blocks_per_tile = TILE // rows

    @pl.when(step == 0)
    def _():
        if half == 0:
            k_all[:WINDOW] = edge_ref[:reach, 0].reshape(WINDOW, hd)
            v_all[:WINDOW] = edge_ref[:reach, 1].reshape(WINDOW, hd)
        else:
            k_all[:WINDOW] = ev_ref[:reach, 1].reshape(WINDOW, hd)
            v_all[:WINDOW] = ev_ref[:reach, 2].reshape(WINDOW, hd)
        own = slice(half * reach, (half + 1) * reach)
        k_all[WINDOW:] = ev_ref[own, 1].reshape(WINDOW, hd)
        v_all[WINDOW:] = ev_ref[own, 2].reshape(WINDOW, hd)
        gk_ref[...] = jnp.zeros_like(gk_ref)
        gv_ref[...] = jnp.zeros_like(gv_ref)
        size = mk_all.shape[0] // memories
        for i, mem_ref in enumerate(mem_refs):
            mk_all[i * size : (i + 1) * size] = mem_ref[0].reshape(size, hd)
            mv_all[i * size : (i + 1) * size] = mem_ref[1].reshape(size, hd)

    span = WINDOW + TILE
    here = pl.ds(half * reach + step * blocks_per_tile, blocks_per_tile)
    q = ev_ref[here, 0].reshape(TILE, hd)
    g = ev_ref[here, 3].reshape(TILE, hd)
    start = pl.multiple_of(step * TILE, TILE)
    kw = k_all[pl.ds(start, span)]
    vw = v_all[pl.ds(start, span)]
    mk = mk_all[...]
    mv = mv_all[...]

    qpos = base + start + lax.broadcasted_iota(jnp.int32, (TILE, span), 0)
    kpos = base + start - WINDOW + lax.broadcasted_iota(jnp.int32, (TILE, span), 1)
    allowed = (
        (kpos <= qpos)
        & (qpos - kpos < WINDOW)
        & (kpos >= 0)
        & ((kpos < length) | (kpos == qpos))
    )
    per_source = mem_refs[0].shape[2]
    memory = mk.shape[0]
    which = lax.rem(lax.broadcasted_iota(jnp.int32, (1, memory), 1), per_source) // depth
    live = which < count

    sw = jnp.where(allowed, dot_nt(q, kw), NEG)
    sm = jnp.where(live, dot_nt(q, mk), NEG)
    top = jnp.maximum(
        jnp.max(sw, axis=1, keepdims=True), jnp.max(sm, axis=1, keepdims=True)
    )
    ew = jnp.exp2((sw - top) * slope)
    em = jnp.exp2((sm - top) * slope)
    dw = dot_nt(g, vw)
    dm = dot_nt(g, mv)
    total = jnp.sum(ew, axis=1, keepdims=True) + jnp.sum(em, axis=1, keepdims=True)
    inv = 1.0 / total
    delta = (
        jnp.sum(ew * dw, axis=1, keepdims=True) + jnp.sum(em * dm, axis=1, keepdims=True)
    ) * inv
    pw = ew * inv
    dsw = (pw * (dw - delta)).astype(jnp.bfloat16)
    dsm = (em * (dm - delta)).astype(jnp.bfloat16)
    gq = (dot_nn(dsw, kw) + dot_nn(dsm, mk) * inv) * scale
    gq_ref[pl.ds(step * blocks_per_tile, blocks_per_tile)] = gq.astype(gq_ref.dtype).reshape(
        blocks_per_tile, rows, hd
    )
    gk_ref[pl.ds(start, span)] += dot_tn(dsw, q) * scale
    gv_ref[pl.ds(start, span)] += dot_tn(pw.astype(jnp.bfloat16), g)
    if half == 0:
        stats_ref = refs[memories + 3]
        lane = lax.broadcasted_iota(jnp.int32, (TILE, hd), 1)
        both = jnp.where(lane == 0, top * slope + jnp.log2(total), delta)
        stats_ref[step] = both.T[:8]


def attend(scale, depth, half, seq_lengths, mem_counts, events, edge, memory):
    _, _, rows, hd = events.shape
    reach = WINDOW // rows
    memories = memory[0].shape[1] * memory[0].shape[2] * len(memory)
    keys = WINDOW + memories
    whole = lambda shape: pl.BlockSpec(shape, lambda t: (0,) * len(shape))
    smem = pl.BlockSpec(memory_space=pltpu.SMEM)
    outs = [((reach, rows, hd), jnp.bfloat16)] + [((2 * WINDOW, hd), jnp.float32)] * 2
    if half == 0:
        outs.append(((WINDOW // TILE, 8, TILE), jnp.float32))
    return call(
        functools.partial(attend_body, scale, depth, half, len(memory)),
        grid=(WINDOW // TILE,),
        in_specs=[smem, smem, whole(events.shape), whole(edge.shape)]
        + [whole(piece.shape) for piece in memory],
        out_specs=[whole(shape) for shape, _ in outs],
        out_shape=[jax.ShapeDtypeStruct(shape, dtype) for shape, dtype in outs],
        scratch_shapes=[pltpu.VMEM((2 * WINDOW, hd), jnp.bfloat16)] * 2
        + [pltpu.VMEM((memories, hd), jnp.bfloat16)] * 2,
        cost_estimate=pl.CostEstimate(
            flops=10 * WINDOW * keys * hd,
            bytes_accessed=4 * keys * hd,
            transcendentals=WINDOW * keys,
        ),
    )(seq_lengths, mem_counts, events, edge, *memory)


def finish_body(scale, length_ref, ev_ref, edge_ref, stats_ref, *refs):
    (gq0, gk0, gv0, gq1, gk1, gv1), out_ref = refs[:-1], refs[-1]
    group, _, rows, hd = ev_ref.shape
    reach = WINDOW // rows
    early = group - reach
    number = lax.axis_index("seq") // H
    length = length_ref[lax.axis_index("dp")]
    follows = number + 1 < lax.axis_size("seq") // H
    base = number * (H * rows)
    slope = scale * LOG2E
    span = group * rows

    def put(where, part, value):
        out_ref[where, part] = value.astype(out_ref.dtype).reshape(reach, rows, hd)

    first, last = slice(0, early), slice(early, group)
    out_ref[first, 0] = gq0[...]
    out_ref[last, 0] = gq1[...]
    put(first, 1, gk0[WINDOW:] + gk1[:WINDOW])
    put(first, 2, gv0[WINDOW:] + gv1[:WINDOW])
    k = ev_ref[early:, 1].reshape(WINDOW, hd)
    v = ev_ref[early:, 2].reshape(WINDOW, hd)
    gk = jnp.zeros((WINDOW, hd), jnp.float32)
    gv = jnp.zeros((WINDOW, hd), jnp.float32)
    kpos = base + span - WINDOW + lax.broadcasted_iota(jnp.int32, (WINDOW, TILE), 0)
    for tile in range(WINDOW // TILE):
        blocks = slice(early + tile * TILE // rows, early + (tile + 1) * TILE // rows)
        q = edge_ref[blocks, 0].reshape(TILE, hd)
        g = edge_ref[blocks, 1].reshape(TILE, hd)
        qpos = base + span + tile * TILE + lax.broadcasted_iota(jnp.int32, (WINDOW, TILE), 1)
        allowed = (qpos - kpos < WINDOW) & (kpos < length) & follows
        s = jnp.where(allowed, dot_nt(k, q) * slope - stats_ref[tile, 0:1], NEG)
        p = jnp.exp2(s)
        d = dot_nt(v, g)
        ds = p * (d - stats_ref[tile, 1:2])
        gk += dot_nn(ds.astype(jnp.bfloat16), q)
        gv += dot_nn(p.astype(jnp.bfloat16), g)
    put(last, 1, gk1[WINDOW:] + gk * scale)
    put(last, 2, gv1[WINDOW:] + gv)


def finish(scale, seq_lengths, events, edge, stats, halves):
    group, _, rows, hd = events.shape
    vmem = pl.BlockSpec(memory_space=pltpu.VMEM)
    return call(
        functools.partial(finish_body, scale),
        in_specs=[pl.BlockSpec(memory_space=pltpu.SMEM)] + [vmem] * 9,
        out_specs=vmem,
        out_shape=jax.ShapeDtypeStruct((group, 3, rows, hd), jnp.bfloat16),
    )(seq_lengths, events, edge, stats, *halves)


def join_body(in_ref, *outs):
    hd = in_ref.shape[-1]
    for part, out_ref in enumerate(outs):
        for head in range(H):
            out_ref[0, :, head * hd : (head + 1) * hd] = in_ref[head, part]


def join_heads(pieces):
    heads, parts, rows, hd = pieces.shape
    vmem = pl.BlockSpec(memory_space=pltpu.VMEM)
    return call(
        join_body,
        in_specs=[vmem],
        out_specs=[vmem] * parts,
        out_shape=[jax.ShapeDtypeStruct((1, rows, heads * hd), pieces.dtype)] * parts,
    )(pieces)


def on_device(
    queries,
    keys,
    values,
    grad_out,
    mem_keys,
    mem_values,
    seq_lengths,
    mem_counts,
    block_lists,
    block_slots,
):
    rows, width = queries.shape[1:]
    scale = 1.0 / math.sqrt(width // H)
    reach = WINDOW // rows
    seq, users = lax.axis_size("seq"), lax.axis_size("dp")
    groups = [[first + i for i in range(H)] for first in range(0, seq, H)]
    swap = functools.partial(
        lax.all_to_all, axis_name="seq", split_axis=0, concat_axis=0, tiled=True
    )

    arrays = (queries, keys, values, grad_out)
    *packed, edge = pack(users, block_slots, block_lists, arrays, mem_keys, mem_values)
    sources = [packed[0]]
    sources.append(lax.ppermute(packed[users], "seq", [(i, i ^ 1) for i in range(seq)]))
    places = [(u, i) for u in range(users) for i in range(seq)]
    for step in range(1, users):
        for side in range(2):
            pairs = [
                (u * seq + i, (u + step) % users * seq + (i ^ side)) for u, i in places
            ]
            sources.append(lax.ppermute(packed[side * users + step], ("dp", "seq"), pairs))
    pairs = [(i, i - reach if i % H < reach else i + reach) for i in range(seq)]
    edge = lax.ppermute(edge, "seq", [(i, j) for i, j in pairs if 0 <= j < seq])

    by_head = split_heads(seq_lengths, arrays, sources[1])
    events = swap(by_head, axis_index_groups=groups)

    held, depth = mem_keys.shape[:2]
    pieces = memory_pieces(held, depth, block_slots, block_lists, sources, by_head)
    memory = []
    for around in range(seq // H - 1, -1, -1):
        for step, piece in enumerate(pieces):
            if around == 0 and step == 0:
                memory.append(piece)
                continue
            pairs = [
                (i, ((i // H + around) * H) % seq + ((i % H) ^ (2 * step))) for i in range(seq)
            ]
            memory.append(lax.ppermute(piece, "seq", pairs))

    edge = swap(split_edge(seq_lengths, edge, events, pieces[0]), axis_index_groups=groups)
    part = functools.partial(attend, scale, depth)
    *first, stats = part(0, seq_lengths, mem_counts, events, edge, memory)
    stats = lax.ppermute(stats, "seq", [(i + H, i) for i in range(seq - H)])
    second = part(1, seq_lengths, mem_counts, events, edge, memory)
    out = finish(scale, seq_lengths, events, edge, stats, [*first, *second])
    return tuple(join_heads(swap(out, axis_index_groups=groups)))


def solution(mesh):
    spread = P("dp", "seq", None)
    return jax.shard_map(
        on_device,
        mesh=mesh,
        in_specs=(spread,) * 6 + (P(),) * 4,
        out_specs=(spread,) * 3,
        check_vma=False,
    )
```

profile of v0, /device:TPU:0, one launch (start us, length us, event | category | flops | bytes accessed | tf_op | source)
XLA Modules:
  0.0 97.3 jit_solution(456764436966072544)
XLA Ops:
  0.6 3.5 %shard_map.121 = (bf16[4,2,128,128]{3,2,1,0:T(8,128)(2,1)}, bf16[4,2,128,128]{3,2,1,0:T(8,128)(2,1)}, bf16[4,2,128,128]{3,2,1,0:T(8,128)(2,1)}, bf16[4,2,128,128]{3,2,1,0:T(8,128)(2,1)}, bf16[2,128,1024]{2,1,0:T(8,128)(2,1)}) custom-call(s32[16]{0:T(128)} %slots_ref.3, s32[2,4]{1,0:T(2,128)} %lists_ref.3, bf16[1,128,1024]{2,1,0:T(8,128)(2,1)} %refs_0_.3, ...), custom_call_target="tpu_custom_call" | custom-call | tf_op jit(solution)/shard_map/pallas_call | solution.py:115
  4.2 0.5 collective-permute-start
  4.7 1.5 %collective-permute-done.refs_4_.refs_1_ = bf16[4,2,128,128]{3,2,1,0:T(8,128)(2,1)} collective-permute-done((bf16[4,2,128,128]{3,2,1,0:T(8,128)(2,1)}, bf16[4,2,128,128]{3,2,1,0:T(8,128)(2,1)}, u32[]{:S(2)}, u32[]{:S(2)}) %collective-permute-start) | collective-permute-done | bytes 262176 | tf_op jit(solution)/shard_map/ppermute | solution.py:444
  6.2 2.9 %shard_map.122._ = bf16[8,4,128,128]{3,2,1,0:T(8,128)(2,1)} custom-call(s32[2]{0:T(128)} %length_ref.9, bf16[1,128,1024]{2,1,0:T(8,128)(2,1)} %refs_0_.3, bf16[1,128,1024]{2,1,0:T(8,128)(2,1)} %refs_1_.3, bf16[1,128,1024]{2,1,0:T(8,128)(2,1)} %refs_2_.3, bf16[1,128,1024]{2,1,0:T(8,128)(2,1)} %refs_3_.3, ...), custom_call_target="tpu_custom_call" | custom-call | tf_op jit(solution)/shard_map/pallas_call | solution.py:153
  9.2 5.3 %all-to-all-start = ((bf16[8,4,128,128]{3,2,1,0:T(8,128)(2,1)}), bf16[8,4,128,128]{3,2,1,0:T(8,128)(2,1)S(1)}, u32[]{:S(2)}, u32[]{:S(2)}) async-start(bf16[8,4,128,128]{3,2,1,0:T(8,128)(2,1)} %shard_map.122._), calls=%async_computation | async-start | bytes 2097152 | tf_op jit(solution)/shard_map/all_to_all | solution.py:456
  14.5 0.7 collective-permute-start.1
  15.2 1.6 %collective-permute-start.2 = (bf16[4,2,128,128]{3,2,1,0:T(8,128)(2,1)S(1)}, bf16[4,2,128,128]{3,2,1,0:T(8,128)(2,1)S(1)}, u32[]{:S(2)}, u32[]{:S(2)}) collective-permute-start(bf16[4,2,128,128]{3,2,1,0:T(8,128)(2,1)S(1)} %copy-done.7), channel_id=1, source_target_pairs={{0,16},{1,17},{2,18},{3,19},{4,20},{5,21},{6,22},{7,23},{8,24},{9,... | collective-permute-start | bytes 786440 | tf_op jit(solution)/shard_map/ppermute | solution.py:451
  16.8 0.4 collective-permute-start.3
  17.1 7.2 %collective-permute-done.2.refs_2_ = bf16[4,2,128,128]{3,2,1,0:T(8,128)(2,1)S(1)} collective-permute-done((bf16[4,2,128,128]{3,2,1,0:T(8,128)(2,1)S(1)}, bf16[4,2,128,128]{3,2,1,0:T(8,128)(2,1)S(1)}, u32[]{:S(2)}, u32[]{:S(2)}) %collective-permute-start.2) | collective-permute-done | bytes 262176 | tf_op jit(solution)/shard_map/ppermute | solution.py:451
  24.4 4.8 %collective-permute-done.3.refs_3_ = bf16[4,2,128,128]{3,2,1,0:T(8,128)(2,1)S(1)} collective-permute-done((bf16[4,2,128,128]{3,2,1,0:T(8,128)(2,1)S(1)}, bf16[4,2,128,128]{3,2,1,0:T(8,128)(2,1)S(1)}, u32[]{:S(2)}, u32[]{:S(2)}) %collective-permute-start.3) | collective-permute-done | bytes 262176 | tf_op jit(solution)/shard_map/ppermute | solution.py:451
  29.2 1.1 %shard_map.123 = (bf16[2,2,128,128]{3,2,1,0:T(8,128)(2,1)S(1)}, bf16[2,2,128,128]{3,2,1,0:T(8,128)(2,1)S(1)}, bf16[2,2,128,128]{3,2,1,0:T(8,128)(2,1)S(1)}, bf16[2,2,128,128]{3,2,1,0:T(8,128)(2,1)S(1)}) custom-call(s32[16]{0:T(128)S(1)} %copy-done.4, s32[2,4]{1,0:T(2,128)S(1)} %copy-done.3, bf16[8,4,128,128]{3,2,1,0:T(8,128)(2,1)S(1)} %copy-done, ...), custom_call_target="tpu_custom_call" | custom-call | tf_op jit(solution)/shard_map/pallas_call | solution.py:221
  30.4 0.6 copy-done.2
  31.0 1.4 %shard_map.124 = bf16[8,2,128,128]{3,2,1,0:T(8,128)(2,1)} custom-call(s32[2]{0:T(128)S(1)} %copy-done.2, bf16[2,128,1024]{2,1,0:T(8,128)(2,1)S(1)} %collective-permute-done.1.in_ref, bf16[8,4,128,128]{3,2,1,0:T(8,128)(2,1)S(1)} %all-to-all-done.refs_0_.ev_ref, bf16[2,2,128,128]{3,2,1,0:T(8,128)(2,1)S(1)} %get-tuple-element.24.refs_1_.refs_4_), custom_call_target="tpu_custom_call" | custom-call | tf_op jit(solution)/shard_map/pallas_call | solution.py:187
  32.5 6.3 %all-to-all-start.1 = ((bf16[8,2,128,128]{3,2,1,0:T(8,128)(2,1)}), bf16[8,2,128,128]{3,2,1,0:T(8,128)(2,1)S(1)}, u32[]{:S(2)}, u32[]{:S(2)}) async-start(bf16[8,2,128,128]{3,2,1,0:T(8,128)(2,1)} %shard_map.124), calls=%async_computation.1 | async-start | bytes 1048576 | tf_op jit(solution)/shard_map/all_to_all | solution.py:471
  38.7 2.0 %collective-permute-start.8 = (bf16[2,2,128,128]{3,2,1,0:T(8,128)(2,1)S(1)}, bf16[2,2,128,128]{3,2,1,0:T(8,128)(2,1)S(1)}, u32[]{:S(2)}, u32[]{:S(2)}) collective-permute-start(bf16[2,2,128,128]{3,2,1,0:T(8,128)(2,1)S(1)} %get-tuple-element.25), channel_id=1, source_target_pairs={{0,2},{1,3},{2,0},{3,1},{4,6},{5,7},{6,4},{7,5},{8,10},{9,11},{10,... | collective-permute-start | bytes 393224 | tf_op jit(solution)/shard_map/ppermute | solution.py:469
  41.0 1.9 %collective-permute-start.9 = (bf16[2,2,128,128]{3,2,1,0:T(8,128)(2,1)S(1)}, bf16[2,2,128,128]{3,2,1,0:T(8,128)(2,1)S(1)}, u32[]{:S(2)}, u32[]{:S(2)}) collective-permute-start(bf16[2,2,128,128]{3,2,1,0:T(8,128)(2,1)S(1)} %get-tuple-element.26), channel_id=1, source_target_pairs={{0,4},{1,5},{2,6},{3,7},{4,0},{5,1},{6,2},{7,3},{8,12},{9,13},{10,... | collective-permute-start | bytes 393224 | tf_op jit(solution)/shard_map/ppermute | solution.py:469
  42.9 1.8 %collective-permute-start.6 = (bf16[2,2,128,128]{3,2,1,0:T(8,128)(2,1)S(1)}, bf16[2,2,128,128]{3,2,1,0:T(8,128)(2,1)S(1)}, u32[]{:S(2)}, u32[]{:S(2)}) collective-permute-start(bf16[2,2,128,128]{3,2,1,0:T(8,128)(2,1)S(1)} %get-tuple-element.26), channel_id=1, source_target_pairs={{0,12},{1,13},{2,14},{3,15},{4,8},{5,9},{6,10},{7,11},{8,4},{9,5},... | collective-permute-start | bytes 393224 | tf_op jit(solution)/shard_map/ppermute | solution.py:469
  44.6 2.0 %collective-permute-start.10 = (bf16[2,2,128,128]{3,2,1,0:T(8,128)(2,1)S(1)}, bf16[2,2,128,128]{3,2,1,0:T(8,128)(2,1)S(1)}, u32[]{:S(2)}, u32[]{:S(2)}) collective-permute-start(bf16[2,2,128,128]{3,2,1,0:T(8,128)(2,1)S(1)} %get-tuple-element.27), channel_id=1, source_target_pairs={{0,6},{1,7},{2,4},{3,5},{4,2},{5,3},{6,0},{7,1},{8,14},{9,15},{10,... | collective-permute-start | bytes 393224 | tf_op jit(solution)/shard_map/ppermute | solution.py:469
  46.6 6.6 %collective-permute-done.8.refs_5_ = bf16[2,2,128,128]{3,2,1,0:T(8,128)(2,1)S(1)} collective-permute-done((bf16[2,2,128,128]{3,2,1,0:T(8,128)(2,1)S(1)}, bf16[2,2,128,128]{3,2,1,0:T(8,128)(2,1)S(1)}, u32[]{:S(2)}, u32[]{:S(2)}) %collective-permute-start.8) | collective-permute-done | bytes 131104 | tf_op jit(solution)/shard_map/ppermute | solution.py:469
  53.2 1.7 %collective-permute-start.7 = (bf16[2,2,128,128]{3,2,1,0:T(8,128)(2,1)S(1)}, bf16[2,2,128,128]{3,2,1,0:T(8,128)(2,1)S(1)}, u32[]{:S(2)}, u32[]{:S(2)}) collective-permute-start(bf16[2,2,128,128]{3,2,1,0:T(8,128)(2,1)S(1)} %get-tuple-element.27), channel_id=1, source_target_pairs={{0,14},{1,15},{2,12},{3,13},{4,10},{5,11},{6,8},{7,9},{8,6},{9,7},... | collective-permute-start | bytes 393224 | tf_op jit(solution)/shard_map/ppermute | solution.py:469
  54.9 1.2 %collective-permute-start.4 = (bf16[2,2,128,128]{3,2,1,0:T(8,128)(2,1)S(1)}, bf16[2,2,128,128]{3,2,1,0:T(8,128)(2,1)S(1)}, u32[]{:S(2)}, u32[]{:S(2)}) collective-permute-start(bf16[2,2,128,128]{3,2,1,0:T(8,128)(2,1)S(1)} %get-tuple-element.24.refs_1_.refs_4_), channel_id=1, source_target_pairs={{0,8},{1,9},{2,10},{3,11},{4,12},{5,13},{6,14},{7,15},{8,0},{9,1},... | collective-permute-start | bytes 393224 | tf_op jit(solution)/shard_map/ppermute | solution.py:469
  56.1 0.2 collective-permute-done.9.refs_6_
  56.4 0.2 collective-permute-done.6.refs_2_
  56.6 3.3 %collective-permute-done.10.refs_7_ = bf16[2,2,128,128]{3,2,1,0:T(8,128)(2,1)S(1)} collective-permute-done((bf16[2,2,128,128]{3,2,1,0:T(8,128)(2,1)S(1)}, bf16[2,2,128,128]{3,2,1,0:T(8,128)(2,1)S(1)}, u32[]{:S(2)}, u32[]{:S(2)}) %collective-permute-start.10) | collective-permute-done | bytes 131104 | tf_op jit(solution)/shard_map/ppermute | solution.py:469
  59.9 3.9 %collective-permute-done.7.refs_3_ = bf16[2,2,128,128]{3,2,1,0:T(8,128)(2,1)S(1)} collective-permute-done((bf16[2,2,128,128]{3,2,1,0:T(8,128)(2,1)S(1)}, bf16[2,2,128,128]{3,2,1,0:T(8,128)(2,1)S(1)}, u32[]{:S(2)}, u32[]{:S(2)}) %collective-permute-start.7) | collective-permute-done | bytes 131104 | tf_op jit(solution)/shard_map/ppermute | solution.py:469
  63.8 4.8 %collective-permute-done.4.refs_0_ = bf16[2,2,128,128]{3,2,1,0:T(8,128)(2,1)S(1)} collective-permute-done((bf16[2,2,128,128]{3,2,1,0:T(8,128)(2,1)S(1)}, bf16[2,2,128,128]{3,2,1,0:T(8,128)(2,1)S(1)}, u32[]{:S(2)}, u32[]{:S(2)}) %collective-permute-start.4) | collective-permute-done | bytes 131104 | tf_op jit(solution)/shard_map/ppermute | solution.py:469
  68.5 5.4 %shard_map.125 = (bf16[4,128,128]{2,1,0:T(8,128)(2,1)S(1)}, f32[1024,128]{1,0:T(8,128)S(1)}, f32[1024,128]{1,0:T(8,128)S(1)}, f32[2,8,256]{2,1,0:T(8,128)S(1)}) custom-call(s32[2]{0:T(128)S(1)} %copy-done.2, s32[2]{0:T(128)S(1)} %copy-done.5, bf16[8,4,128,128]{3,2,1,0:T(8,128)(2,1)S(1)} %all-to-all-done.refs_0_.ev_ref, ...), custom_call_target="tpu_custom_call" | custom-call | flops 1677721600 | bytes 1310720 | tf_op jit(solution)/shard_map/pallas_call | solution.py:333
  73.9 1.3 %collective-permute-start.11 = (f32[2,8,256]{2,1,0:T(8,128)S(1)}, f32[2,8,256]{2,1,0:T(8,128)S(1)}, u32[]{:S(2)}, u32[]{:S(2)}) collective-permute-start(f32[2,8,256]{2,1,0:T(8,128)S(1)} %get-tuple-element.28), channel_id=1, source_target_pairs={{8,0},{9,1},{10,2},{11,3},{12,4},{13,5},{14,6},{15,7},{24,16},{25,... | collective-permute-start | bytes 49160 | tf_op jit(solution)/shard_map/ppermute | solution.py:474
  75.2 5.4 %shard_map.126 = (bf16[4,128,128]{2,1,0:T(8,128)(2,1)S(1)}, f32[1024,128]{1,0:T(8,128)S(1)}, f32[1024,128]{1,0:T(8,128)S(1)}) custom-call(s32[2]{0:T(128)S(1)} %copy-done.2, s32[2]{0:T(128)S(1)} %copy-done.5, bf16[8,4,128,128]{3,2,1,0:T(8,128)(2,1)S(1)} %all-to-all-done.refs_0_.ev_ref, bf16[8,2,128,128]{3,2,1,0:T(8,128)(2,1)S(1)} %all-to-all-done.1.edge_ref, ...), custom_call_target="tpu_custom_call" | custom-call | flops 1677721600 | bytes 1310720 | tf_op jit(solution)/shard_map/pallas_call | solution.py:333
  80.7 1.4 %shard_map.127 = bf16[8,3,128,128]{3,2,1,0:T(8,128)(2,1)S(1)} custom-call(s32[2]{0:T(128)S(1)} %copy-done.2, bf16[8,4,128,128]{3,2,1,0:T(8,128)(2,1)S(1)} %all-to-all-done.refs_0_.ev_ref, bf16[8,2,128,128]{3,2,1,0:T(8,128)(2,1)S(1)} %all-to-all-done.1.edge_ref, f32[2,8,256]{2,1,0:T(8,128)S(1)} %collective-permute-done.11.stats_ref, ...), custom_call_target="tpu_custom_call" | custom-call | tf_op jit(solution)/shard_map/pallas_call | solution.py:394
  82.1 14.2 %all_to_all.15.in_ref = bf16[8,3,128,128]{3,2,1,0:T(8,128)(2,1)S(1)} all-to-all(bf16[8,3,128,128]{3,2,1,0:T(8,128)(2,1)S(1)} %shard_map.127), channel_id=1, replica_groups={{0,1,2,3,4,5,6,7},{8,9,10,11,12,13,14,15},{16,17,18,19,20,21,22,23},{24..., dimensions={0} | all-to-all | bytes 1572864 | tf_op jit(solution)/shard_map/all_to_all | solution.py:477
  96.3 1.1 %shard_map.128 = (bf16[1,128,1024]{2,1,0:T(8,128)(2,1)}, bf16[1,128,1024]{2,1,0:T(8,128)(2,1)}, bf16[1,128,1024]{2,1,0:T(8,128)(2,1)}) custom-call(bf16[8,3,128,128]{3,2,1,0:T(8,128)(2,1)S(1)} %all_to_all.15.in_ref), custom_call_target="tpu_custom_call" | custom-call | tf_op jit(solution)/shard_map/pallas_call | solution.py:412
  (21 shorter events, 0.2 us)
Async XLA Ops:
  4.2 2.0 %collective-permute-start = (bf16[4,2,128,128]{3,2,1,0:T(8,128)(2,1)}, bf16[4,2,128,128]{3,2,1,0:T(8,128)(2,1)}, u32[]{:S(2)}, u32[]{:S(2)}) collective-permute-start(bf16[4,2,128,128]{3,2,1,0:T(8,128)(2,1)} %get-tuple-element.19), channel_id=1, source_target_pairs={{0,1},{1,0},{2,3},{3,2},{4,5},{5,4},{6,7},{7,6},{8,9},{9,8},{10,11... | collective-permute-start | bytes 786440 | tf_op jit(solution)/shard_map/ppermute | solution.py:444
  9.1 6.1 %copy-start.7 = (bf16[4,2,128,128]{3,2,1,0:T(8,128)(2,1)S(1)}, bf16[4,2,128,128]{3,2,1,0:T(8,128)(2,1)}, u32[]{:S(2)}) copy-start(bf16[4,2,128,128]{3,2,1,0:T(8,128)(2,1)} %get-tuple-element.22) | copy-start | bytes 786436
  9.1 7.6 %copy-start.6 = (bf16[4,2,128,128]{3,2,1,0:T(8,128)(2,1)S(1)}, bf16[4,2,128,128]{3,2,1,0:T(8,128)(2,1)}, u32[]{:S(2)}) copy-start(bf16[4,2,128,128]{3,2,1,0:T(8,128)(2,1)} %get-tuple-element.23) | copy-start | bytes 786436
  9.2 20.1 %copy-start = (bf16[8,4,128,128]{3,2,1,0:T(8,128)(2,1)S(1)}, bf16[8,4,128,128]{3,2,1,0:T(8,128)(2,1)}, u32[]{:S(2)}) copy-start(bf16[8,4,128,128]{3,2,1,0:T(8,128)(2,1)} %shard_map.122._) | copy-start | bytes 3145732
  9.2 20.0 %copy-start.1 = (bf16[4,2,128,128]{3,2,1,0:T(8,128)(2,1)S(1)}, bf16[4,2,128,128]{3,2,1,0:T(8,128)(2,1)}, u32[]{:S(2)}) copy-start(bf16[4,2,128,128]{3,2,1,0:T(8,128)(2,1)} %get-tuple-element.21.refs_0_) | copy-start | bytes 786436
  9.2 21.2 %all-to-all-start = ((bf16[8,4,128,128]{3,2,1,0:T(8,128)(2,1)}), bf16[8,4,128,128]{3,2,1,0:T(8,128)(2,1)S(1)}, u32[]{:S(2)}, u32[]{:S(2)}) async-start(bf16[8,4,128,128]{3,2,1,0:T(8,128)(2,1)} %shard_map.122._), calls=%async_computation | async-start | bytes 2097152 | tf_op jit(solution)/shard_map/all_to_all | solution.py:456
  14.5 15.9 %collective-permute-start.1 = (bf16[2,128,1024]{2,1,0:T(8,128)(2,1)}, bf16[2,128,1024]{2,1,0:T(8,128)(2,1)S(1)}, u32[]{:S(2)}, u32[]{:S(2)}) collective-permute-start(bf16[2,128,1024]{2,1,0:T(8,128)(2,1)} %get-tuple-element.20), channel_id=1, source_target_pairs={{4,8},{5,9},{6,10},{7,11},{8,4},{9,5},{10,6},{11,7},{20,24},{21,25... | collective-permute-start | bytes 1572872 | tf_op jit(solution)/shard_map/ppermute | solution.py:453
  15.2 9.2 %collective-permute-start.2 = (bf16[4,2,128,128]{3,2,1,0:T(8,128)(2,1)S(1)}, bf16[4,2,128,128]{3,2,1,0:T(8,128)(2,1)S(1)}, u32[]{:S(2)}, u32[]{:S(2)}) collective-permute-start(bf16[4,2,128,128]{3,2,1,0:T(8,128)(2,1)S(1)} %copy-done.7), channel_id=1, source_target_pairs={{0,16},{1,17},{2,18},{3,19},{4,20},{5,21},{6,22},{7,23},{8,24},{9,... | collective-permute-start | bytes 786440 | tf_op jit(solution)/shard_map/ppermute | solution.py:451
  16.8 12.5 %copy-start.3 = (s32[2,4]{1,0:T(2,128)S(1)}, s32[2,4]{1,0:T(2,128)}, u32[]{:S(2)}) copy-start(s32[2,4]{1,0:T(2,128)} %lists_ref.3) | copy-start | bytes 100
  16.8 12.5 %copy-start.4 = (s32[16]{0:T(128)S(1)}, s32[16]{0:T(128)}, u32[]{:S(2)}) copy-start(s32[16]{0:T(128)} %slots_ref.3) | copy-start | bytes 196
  16.8 12.4 %collective-permute-start.3 = (bf16[4,2,128,128]{3,2,1,0:T(8,128)(2,1)S(1)}, bf16[4,2,128,128]{3,2,1,0:T(8,128)(2,1)S(1)}, u32[]{:S(2)}, u32[]{:S(2)}) collective-permute-start(bf16[4,2,128,128]{3,2,1,0:T(8,128)(2,1)S(1)} %copy-done.6), channel_id=1, source_target_pairs={{0,17},{1,16},{2,19},{3,18},{4,21},{5,20},{6,23},{7,22},{8,25},{9,... | collective-permute-start | bytes 786440 | tf_op jit(solution)/shard_map/ppermute | solution.py:451
  30.4 0.7 copy-start.2
  32.5 36.1 %all-to-all-start.1 = ((bf16[8,2,128,128]{3,2,1,0:T(8,128)(2,1)}), bf16[8,2,128,128]{3,2,1,0:T(8,128)(2,1)S(1)}, u32[]{:S(2)}, u32[]{:S(2)}) async-start(bf16[8,2,128,128]{3,2,1,0:T(8,128)(2,1)} %shard_map.124), calls=%async_computation.1 | async-start | bytes 1048576 | tf_op jit(solution)/shard_map/all_to_all | solution.py:471
  38.7 14.5 %collective-permute-start.8 = (bf16[2,2,128,128]{3,2,1,0:T(8,128)(2,1)S(1)}, bf16[2,2,128,128]{3,2,1,0:T(8,128)(2,1)S(1)}, u32[]{:S(2)}, u32[]{:S(2)}) collective-permute-start(bf16[2,2,128,128]{3,2,1,0:T(8,128)(2,1)S(1)} %get-tuple-element.25), channel_id=1, source_target_pairs={{0,2},{1,3},{2,0},{3,1},{4,6},{5,7},{6,4},{7,5},{8,10},{9,11},{10,... | collective-permute-start | bytes 393224 | tf_op jit(solution)/shard_map/ppermute | solution.py:469
  40.8 14.2 %collective-permute-start.5 = (bf16[2,2,128,128]{3,2,1,0:T(8,128)(2,1)S(1)}, bf16[2,2,128,128]{3,2,1,0:T(8,128)(2,1)S(1)}, u32[]{:S(2)}, u32[]{:S(2)}) collective-permute-start(bf16[2,2,128,128]{3,2,1,0:T(8,128)(2,1)S(1)} %get-tuple-element.25), channel_id=1, source_target_pairs={{0,10},{1,11},{2,8},{3,9},{4,14},{5,15},{6,12},{7,13},{8,2},{9,3},... | collective-permute-start | bytes 393224 | tf_op jit(solution)/shard_map/ppermute | solution.py:469
  40.9 27.6 %copy-start.5 = (s32[2]{0:T(128)S(1)}, s32[2]{0:T(128)}, u32[]{:S(2)}) copy-start(s32[2]{0:T(128)} %count_ref.3) | copy-start | bytes 28
  41.0 15.4 %collective-permute-start.9 = (bf16[2,2,128,128]{3,2,1,0:T(8,128)(2,1)S(1)}, bf16[2,2,128,128]{3,2,1,0:T(8,128)(2,1)S(1)}, u32[]{:S(2)}, u32[]{:S(2)}) collective-permute-start(bf16[2,2,128,128]{3,2,1,0:T(8,128)(2,1)S(1)} %get-tuple-element.26), channel_id=1, source_target_pairs={{0,4},{1,5},{2,6},{3,7},{4,0},{5,1},{6,2},{7,3},{8,12},{9,13},{10,... | collective-permute-start | bytes 393224 | tf_op jit(solution)/shard_map/ppermute | solution.py:469
  42.9 13.7 %collective-permute-start.6 = (bf16[2,2,128,128]{3,2,1,0:T(8,128)(2,1)S(1)}, bf16[2,2,128,128]{3,2,1,0:T(8,128)(2,1)S(1)}, u32[]{:S(2)}, u32[]{:S(2)}) collective-permute-start(bf16[2,2,128,128]{3,2,1,0:T(8,128)(2,1)S(1)} %get-tuple-element.26), channel_id=1, source_target_pairs={{0,12},{1,13},{2,14},{3,15},{4,8},{5,9},{6,10},{7,11},{8,4},{9,5},... | collective-permute-start | bytes 393224 | tf_op jit(solution)/shard_map/ppermute | solution.py:469
  44.6 15.2 %collective-permute-start.10 = (bf16[2,2,128,128]{3,2,1,0:T(8,128)(2,1)S(1)}, bf16[2,2,128,128]{3,2,1,0:T(8,128)(2,1)S(1)}, u32[]{:S(2)}, u32[]{:S(2)}) collective-permute-start(bf16[2,2,128,128]{3,2,1,0:T(8,128)(2,1)S(1)} %get-tuple-element.27), channel_id=1, source_target_pairs={{0,6},{1,7},{2,4},{3,5},{4,2},{5,3},{6,0},{7,1},{8,14},{9,15},{10,... | collective-permute-start | bytes 393224 | tf_op jit(solution)/shard_map/ppermute | solution.py:469
  53.2 10.6 %collective-permute-start.7 = (bf16[2,2,128,128]{3,2,1,0:T(8,128)(2,1)S(1)}, bf16[2,2,128,128]{3,2,1,0:T(8,128)(2,1)S(1)}, u32[]{:S(2)}, u32[]{:S(2)}) collective-permute-start(bf16[2,2,128,128]{3,2,1,0:T(8,128)(2,1)S(1)} %get-tuple-element.27), channel_id=1, source_target_pairs={{0,14},{1,15},{2,12},{3,13},{4,10},{5,11},{6,8},{7,9},{8,6},{9,7},... | collective-permute-start | bytes 393224 | tf_op jit(solution)/shard_map/ppermute | solution.py:469
  54.9 13.6 %collective-permute-start.4 = (bf16[2,2,128,128]{3,2,1,0:T(8,128)(2,1)S(1)}, bf16[2,2,128,128]{3,2,1,0:T(8,128)(2,1)S(1)}, u32[]{:S(2)}, u32[]{:S(2)}) collective-permute-start(bf16[2,2,128,128]{3,2,1,0:T(8,128)(2,1)S(1)} %get-tuple-element.24.refs_1_.refs_4_), channel_id=1, source_target_pairs={{0,8},{1,9},{2,10},{3,11},{4,12},{5,13},{6,14},{7,15},{8,0},{9,1},... | collective-permute-start | bytes 393224 | tf_op jit(solution)/shard_map/ppermute | solution.py:469
  73.9 6.7 %collective-permute-start.11 = (f32[2,8,256]{2,1,0:T(8,128)S(1)}, f32[2,8,256]{2,1,0:T(8,128)S(1)}, u32[]{:S(2)}, u32[]{:S(2)}) collective-permute-start(f32[2,8,256]{2,1,0:T(8,128)S(1)} %get-tuple-element.28), channel_id=1, source_target_pairs={{8,0},{9,1},{10,2},{11,3},{12,4},{13,5},{14,6},{15,7},{24,16},{25,... | collective-permute-start | bytes 49160 | tf_op jit(solution)/shard_map/ppermute | solution.py:474
where the time goes:
time: 97.8 us; the launch traced here: 97.3 us
  waiting for transfers between devices  32.6 us (33%)
  starting transfers between devices  26.8 us (27%)
  Pallas kernels  22.4 us (23%)
  blocking collectives  14.2 us (15%)
    ppermute x7, waiting for transfers between devices, on_device(): memory.append(lax.ppermute(piece, 'seq', pairs))  19 us
    all_to_all x1, blocking collectives, on_device(): return tuple(join_heads(swap(out, axis_index_groups=groups)))  14.2 us
    ppermute x2, waiting for transfers between devices, on_device(): lax.ppermute(packed[side * users + step], ('dp', 'seq'), pairs)  12.1 us
    pallas_call x2, Pallas kernels, attend(): call(functools.partial(attend_body, scale, depth, half, len(memory)), gri...  10.8 us
    ppermute x7, starting transfers between devices, on_device(): memory.append(lax.ppermute(piece, 'seq', pairs))  10.8 us
    all_to_all x1, starting transfers between devices, on_device(): swap(split_edge(seq_lengths, edge, events, pieces[0]), axis_index_groups=...  6.28 us
    all_to_all x1, starting transfers between devices, on_device(): events = swap(by_head, axis_index_groups=groups)  5.32 us
    pallas_call x1, Pallas kernels, pack(): call(functools.partial(pack_body, users), limit=VMEM_WHOLE, in_specs=[sme...  3.52 us
  transfers between devices with their start and end apart: 14, of which 9 were waited for; matrix products, arithmetic and copies ran while one was open for 0% of the time, Pallas kernels for 7%

commit v1 on v0

v1 whole, which is shorter than its diff:
```python
import functools
import math

import jax
import jax.numpy as jnp
from jax import lax
from jax.experimental import pallas as pl
from jax.experimental.pallas import tpu as pltpu
from jax.sharding import PartitionSpec as P

H = 8
WINDOW = 512
TILE = 256
NEG = -1e30
LOG2E = 1.4426950408889634
VMEM_LIMIT = 48 * 1024 * 1024
VMEM_WHOLE = 64 * 1024 * 1024 - 256 * 1024

NT = (((1,), (1,)), ((), ()))
TN = (((0,), (0,)), ((), ()))


def dot_nt(a, b):
    return lax.dot_general(a, b, NT, preferred_element_type=jnp.float32)


def dot_tn(a, b):
    return lax.dot_general(a, b, TN, preferred_element_type=jnp.float32)


def dot_nn(a, b):
    return jnp.dot(a, b, preferred_element_type=jnp.float32)


def call(body, limit=VMEM_LIMIT, **kw):
    return pl.pallas_call(
        body, compiler_params=pltpu.CompilerParams(vmem_limit_bytes=limit), **kw
    )


def load_listed(user, slots_ref, lists_ref, mk_ref, mv_ref, buffer, sems):
    copies = []
    for block in range(buffer.shape[0]):
        index = lax.rem(slots_ref[lists_ref[user, block]], mk_ref.shape[0])
        for part, pool in enumerate((mk_ref, mv_ref)):
            copies.append(
                pltpu.make_async_copy(
                    pool.at[index], buffer.at[block, part], sems.at[block, part]
                )
            )
    for copy in copies:
        copy.start()
    return copies


def split_parity(value, where, same_ref, other_ref):
    hd = value.shape[1] // H
    odd = lax.rem(lax.axis_index("seq"), 2) == 1
    for pair in range(H // 2):
        first = value[:, 2 * pair * hd : (2 * pair + 1) * hd]
        second = value[:, (2 * pair + 1) * hd : (2 * pair + 2) * hd]
        same_ref[(pair,) + where] = jnp.where(odd, second, first)
        other_ref[(pair,) + where] = jnp.where(odd, first, second)


def pack_body(users, length_ref, slots_ref, lists_ref, *refs):
    (q_ref, k_ref, v_ref, g_ref, mk_ref, mv_ref), refs = refs[:6], refs[6:]
    same, other = refs[: users + 1], refs[users + 1 : 2 * users + 2]
    buffer, sems, edge, edge_sems = refs[2 * users + 2 :]
    user, shard = lax.axis_index("dp"), lax.axis_index("seq")
    _, blocks, parts, depth, _ = buffer.shape
    rows, width = edge.shape[1:]
    early = lax.rem(shard, H) < WINDOW // rows
    order = [step % users for step in range(1, users + 1)]
    loads = {
        step: load_listed(
            lax.rem(user + step, users),
            slots_ref,
            lists_ref,
            mk_ref,
            mv_ref,
            buffer.at[step],
            sems.at[step],
        )
        for step in order
    }

    @pl.when(early)
    def _():
        for part, ref in enumerate((q_ref, g_ref)):
            pltpu.make_async_copy(ref.at[0], edge.at[part], edge_sems.at[part]).start()

    @pl.when(jnp.logical_not(early))
    def _():
        for part, ref in enumerate((k_ref, v_ref)):
            pltpu.make_async_copy(ref.at[0], edge.at[part], edge_sems.at[part]).start()

    for step in order:
        for copy in loads[step]:
            copy.wait()
        for block in range(blocks):
            for part in range(parts):
                where = (part, slice(block * depth, (block + 1) * depth))
                split_parity(buffer[step, block, part], where, same[step], other[step])
    live = jnp.where(early, length_ref[user] - shard * rows, rows)
    for part in range(2):
        pltpu.make_async_copy(q_ref.at[0], edge.at[part], edge_sems.at[part]).wait()
        value = edge[part]
        if part == 1:
            position = lax.broadcasted_iota(jnp.int32, (rows, width), 0)
            value = jnp.where(position < live, value.astype(jnp.float32), 0.0)
            value = value.astype(edge.dtype)
        split_parity(value, (part,), same[users], other[users])


def pack(users, seq_lengths, block_slots, block_lists, events, mem_keys, mem_values):
    _, depth, width = mem_keys.shape
    blocks = block_lists.shape[1]
    rows = events[0].shape[1]
    dtype = mem_keys.dtype
    smem = pl.BlockSpec(memory_space=pltpu.SMEM)
    hbm = pl.BlockSpec(memory_space=pltpu.HBM)
    pieces = jax.ShapeDtypeStruct((H // 2, 2, blocks * depth, width // H), dtype)
    edges = jax.ShapeDtypeStruct((H // 2, 2, rows, width // H), dtype)
    outs = ([pieces] * users + [edges]) * 2
    return call(
        functools.partial(pack_body, users),
        limit=VMEM_WHOLE,
        in_specs=[smem] * 3 + [hbm] * 6,
        out_specs=[pl.BlockSpec(memory_space=pltpu.VMEM)] * len(outs),
        out_shape=outs,
        scratch_shapes=[
            pltpu.VMEM((users, blocks, 2, depth, width), dtype),
            pltpu.SemaphoreType.DMA((users, blocks, 2)),
            pltpu.VMEM((2, rows, width), dtype),
            pltpu.SemaphoreType.DMA((2,)),
        ],
    )(seq_lengths, block_slots, block_lists, *events, mem_keys, mem_values)


def split_body(hd, length_ref, *refs):
    sources, (out_ref, buffer, sems) = refs[:4], refs[4:]
    rows = buffer.shape[1]
    copies = [
        pltpu.make_async_copy(source.at[0], buffer.at[part], sems.at[part])
        for part, source in enumerate(sources)
    ]
    for copy in copies:
        copy.start()
    live = length_ref[lax.axis_index("dp")] - lax.axis_index("seq") * rows
    position = lax.broadcasted_iota(jnp.int32, (rows, hd), 0)
    for part, copy in enumerate(copies):
        copy.wait()
        for head in range(H):
            block = buffer[part, :, head * hd : (head + 1) * hd]
            if part == 3:
                block = jnp.where(position < live, block.astype(jnp.float32), 0.0)
            out_ref[head, part] = block.astype(out_ref.dtype)


def split_heads(seq_lengths, arrays):
    _, rows, width = arrays[0].shape
    parts = len(arrays)
    hbm = pl.BlockSpec(memory_space=pltpu.HBM)
    return call(
        functools.partial(split_body, width // H),
        limit=VMEM_WHOLE,
        in_specs=[pl.BlockSpec(memory_space=pltpu.SMEM)] + [hbm] * parts,
        out_specs=pl.BlockSpec(memory_space=pltpu.VMEM),
        out_shape=jax.ShapeDtypeStruct((H, parts, rows, width // H), arrays[0].dtype),
        scratch_shapes=[
            pltpu.VMEM((parts, rows, width), arrays[0].dtype),
            pltpu.SemaphoreType.DMA((parts,)),
        ],
    )(seq_lengths, *arrays)


def memory_rows(held, slots_ref, lists_ref, block, depth, sources, side, pair, part):
    users = len(sources) // 2
    user = lax.axis_index("dp")
    slot = slots_ref[lists_ref[user, block]]
    source = lax.rem(user - slot // held + users, users)
    rows = slice(block * depth, (block + 1) * depth)
    value = sources[side][pair, part, rows]
    for other in range(1, users):
        value = jnp.where(source == other, sources[2 * other + side][pair, part, rows], value)
    return rows, value


def far_body(held, depth, slots_ref, lists_ref, *refs):
    outs = refs[-(H // 2) :]
    sources = refs[: -(H // 2)]
    pair = lax.rem(lax.axis_index("seq") // 2, H // 2)
    for block in range(lists_ref.shape[1]):
        for step, out_ref in enumerate(outs):
            for side in range(2):
                for part in range(2):
                    rows, value = memory_rows(
                        held, slots_ref, lists_ref, block, depth, sources, side, pair ^ step, part
                    )
                    out_ref[part, side, rows] = value


def far_pieces(held, depth, block_slots, block_lists, sources):
    _, parts, rows, hd = sources[0].shape
    smem = pl.BlockSpec(memory_space=pltpu.SMEM)
    vmem = pl.BlockSpec(memory_space=pltpu.VMEM)
    return call(
        functools.partial(far_body, held, depth),
        in_specs=[smem] * 2 + [vmem] * len(sources),
        out_specs=[vmem] * (H // 2),
        out_shape=[jax.ShapeDtypeStruct((parts, 2, rows, hd), sources[0].dtype)] * (H // 2),
    )(block_slots, block_lists, *sources)


def near_body(held, depth, slots_ref, lists_ref, _, *refs):
    (edge_same, edge_other), sources, out_ref = refs[:2], refs[2:-1], refs[-1]
    odd = lax.rem(lax.axis_index("seq"), 2) == 1
    memory, edges = sources[0].shape[2], edge_same.shape[2]
    for pair in range(H // 2):
        for part in range(2):
            for side in range(2):
                for block in range(lists_ref.shape[1]):
                    rows, value = memory_rows(
                        held, slots_ref, lists_ref, block, depth, sources, side, pair, part
                    )
                    first = side * memory + rows.start
                    out_ref[pair, part, first : first + depth] = value
            same, other = edge_same[pair, part], edge_other[pair, part]
            first = 2 * memory
            out_ref[pair, part, first : first + edges] = jnp.where(odd, other, same)
            out_ref[pair, part, first + edges :] = jnp.where(odd, same, other)


def near_pieces(held, depth, block_slots, block_lists, edges, sources, later_than):
    pairs, parts, rows, hd = sources[0].shape
    smem = pl.BlockSpec(memory_space=pltpu.SMEM)
    vmem = pl.BlockSpec(memory_space=pltpu.VMEM)
    size = 2 * (rows + edges[0].shape[2])
    return call(
        functools.partial(near_body, held, depth),
        in_specs=[smem] * 2
        + [pl.BlockSpec(memory_space=pl.ANY)]
        + [vmem] * (2 + len(sources)),
        out_specs=vmem,
        out_shape=jax.ShapeDtypeStruct((pairs, parts, size, hd), sources[0].dtype),
    )(block_slots, block_lists, later_than, *edges, *sources)


def attend_body(
    scale,
    depth,
    half,
    memories,
    length_ref,
    count_ref,
    ev_ref,
    near_ref,
    *refs,
):
    far_refs, (gq_ref, gk_ref, gv_ref) = refs[:memories], refs[memories : memories + 3]
    k_all, v_all, mk_all, mv_all = refs[-4:]
    step = pl.program_id(0)
    hd = ev_ref.shape[-1]
    rows = ev_ref.shape[2]
    reach = WINDOW // rows
    user = lax.axis_index("dp")
    length, count = length_ref[user], count_ref[user]
    base = (lax.axis_index("seq") // H) * (H * rows) + half * WINDOW
    slope = scale * LOG2E
    blocks_per_tile = TILE // rows
    near = near_ref.shape[2] - 2 * rows

    @pl.when(step == 0)
    def _():
        if half == 0:
            k_all[:WINDOW] = near_ref[: reach // 2, 0, near:].reshape(WINDOW, hd)
            v_all[:WINDOW] = near_ref[: reach // 2, 1, near:].reshape(WINDOW, hd)
        else:
            k_all[:WINDOW] = ev_ref[:reach, 1].reshape(WINDOW, hd)
            v_all[:WINDOW] = ev_ref[:reach, 2].reshape(WINDOW, hd)
        own = slice(half * reach, (half + 1) * reach)
        k_all[WINDOW:] = ev_ref[own, 1].reshape(WINDOW, hd)
        v_all[WINDOW:] = ev_ref[own, 2].reshape(WINDOW, hd)
        gk_ref[...] = jnp.zeros_like(gk_ref)
        gv_ref[...] = jnp.zeros_like(gv_ref)
        for part, all_ref in enumerate((mk_all, mv_all)):
            first = near_ref.shape[0] * near
            all_ref[:first] = near_ref[:, part, :near].reshape(first, hd)
            for far_ref in far_refs:
                all_ref[first : first + near] = far_ref[part].reshape(near, hd)
                first += near

    span = WINDOW + TILE
    here = pl.ds(half * reach + step * blocks_per_tile, blocks_per_tile)
    q = ev_ref[here, 0].reshape(TILE, hd)
    g = ev_ref[here, 3].reshape(TILE, hd)
    start = pl.multiple_of(step * TILE, TILE)
    kw = k_all[pl.ds(start, span)]
    vw = v_all[pl.ds(start, span)]
    mk = mk_all[...]
    mv = mv_all[...]

    qpos = base + start + lax.broadcasted_iota(jnp.int32, (TILE, span), 0)
    kpos = base + start - WINDOW + lax.broadcasted_iota(jnp.int32, (TILE, span), 1)
    allowed = (
        (kpos <= qpos)
        & (qpos - kpos < WINDOW)
        & (kpos >= 0)
        & ((kpos < length) | (kpos == qpos))
    )
    per_source = near // 2
    memory = mk.shape[0]
    which = lax.rem(lax.broadcasted_iota(jnp.int32, (1, memory), 1), per_source) // depth
    live = which < count

    sw = jnp.where(allowed, dot_nt(q, kw), NEG)
    sm = jnp.where(live, dot_nt(q, mk), NEG)
    top = jnp.maximum(
        jnp.max(sw, axis=1, keepdims=True), jnp.max(sm, axis=1, keepdims=True)
    )
    ew = jnp.exp2((sw - top) * slope)
    em = jnp.exp2((sm - top) * slope)
    dw = dot_nt(g, vw)
    dm = dot_nt(g, mv)
    total = jnp.sum(ew, axis=1, keepdims=True) + jnp.sum(em, axis=1, keepdims=True)
    inv = 1.0 / total
    delta = (
        jnp.sum(ew * dw, axis=1, keepdims=True) + jnp.sum(em * dm, axis=1, keepdims=True)
    ) * inv
    pw = ew * inv
    dsw = (pw * (dw - delta)).astype(jnp.bfloat16)
    dsm = (em * (dm - delta)).astype(jnp.bfloat16)
    gq = (dot_nn(dsw, kw) + dot_nn(dsm, mk) * inv) * scale
    gq_ref[pl.ds(step * blocks_per_tile, blocks_per_tile)] = gq.astype(gq_ref.dtype).reshape(
        blocks_per_tile, rows, hd
    )
    gk_ref[pl.ds(start, span)] += dot_tn(dsw, q) * scale
    gv_ref[pl.ds(start, span)] += dot_tn(pw.astype(jnp.bfloat16), g)
    if half == 0:
        stats_ref = refs[memories + 3]
        lane = lax.broadcasted_iota(jnp.int32, (TILE, hd), 1)
        both = jnp.where(lane == 0, top * slope + jnp.log2(total), delta)
        stats_ref[step] = both.T[:8]


def attend(scale, depth, half, seq_lengths, mem_counts, events, near, far):
    _, _, rows, hd = events.shape
    reach = WINDOW // rows
    memories = (near.shape[2] - 2 * rows) * (near.shape[0] + len(far))
    keys = WINDOW + memories
    whole = lambda shape: pl.BlockSpec(shape, lambda t: (0,) * len(shape))
    smem = pl.BlockSpec(memory_space=pltpu.SMEM)
    outs = [((reach, rows, hd), jnp.bfloat16)] + [((2 * WINDOW, hd), jnp.float32)] * 2
    if half == 0:
        outs.append(((WINDOW // TILE, 8, TILE), jnp.float32))
    return call(
        functools.partial(attend_body, scale, depth, half, len(far)),
        grid=(WINDOW // TILE,),
        in_specs=[smem, smem, whole(events.shape), whole(near.shape)]
        + [whole(piece.shape) for piece in far],
        out_specs=[whole(shape) for shape, _ in outs],
        out_shape=[jax.ShapeDtypeStruct(shape, dtype) for shape, dtype in outs],
        scratch_shapes=[pltpu.VMEM((2 * WINDOW, hd), jnp.bfloat16)] * 2
        + [pltpu.VMEM((memories, hd), jnp.bfloat16)] * 2,
        cost_estimate=pl.CostEstimate(
            flops=10 * WINDOW * keys * hd,
            bytes_accessed=4 * keys * hd,
            transcendentals=WINDOW * keys,
        ),
    )(seq_lengths, mem_counts, events, near, *far)


def finish_body(scale, length_ref, ev_ref, near_ref, stats_ref, *refs):
    (gq0, gk0, gv0, gq1, gk1, gv1), out_ref = refs[:-1], refs[-1]
    group, _, rows, hd = ev_ref.shape
    reach = WINDOW // rows
    early = group - reach
    near = near_ref.shape[2] - 2 * rows
    number = lax.axis_index("seq") // H
    length = length_ref[lax.axis_index("dp")]
    follows = number + 1 < lax.axis_size("seq") // H
    base = number * (H * rows)
    slope = scale * LOG2E
    span = group * rows

    def put(where, part, value):
        out_ref[where, part] = value.astype(out_ref.dtype).reshape(reach, rows, hd)

    first, last = slice(0, early), slice(early, group)
    out_ref[first, 0] = gq0[...]
    out_ref[last, 0] = gq1[...]
    put(first, 1, gk0[WINDOW:] + gk1[:WINDOW])
    put(first, 2, gv0[WINDOW:] + gv1[:WINDOW])
    k = ev_ref[early:, 1].reshape(WINDOW, hd)
    v = ev_ref[early:, 2].reshape(WINDOW, hd)
    gk = jnp.zeros((WINDOW, hd), jnp.float32)
    gv = jnp.zeros((WINDOW, hd), jnp.float32)
    kpos = base + span - WINDOW + lax.broadcasted_iota(jnp.int32, (WINDOW, TILE), 0)
    for tile in range(WINDOW // TILE):
        pairs = early // 2 + tile * TILE // (2 * rows)
        pairs = slice(pairs, pairs + TILE // (2 * rows))
        q = near_ref[pairs, 0, near:].reshape(TILE, hd)
        g = near_ref[pairs, 1, near:].reshape(TILE, hd)
        qpos = base + span + tile * TILE + lax.broadcasted_iota(jnp.int32, (WINDOW, TILE), 1)
        allowed = (qpos - kpos < WINDOW) & (kpos < length) & follows
        s = jnp.where(allowed, dot_nt(k, q) * slope - stats_ref[tile, 0:1], NEG)
        p = jnp.exp2(s)
        d = dot_nt(v, g)
        ds = p * (d - stats_ref[tile, 1:2])
        gk += dot_nn(ds.astype(jnp.bfloat16), q)
        gv += dot_nn(p.astype(jnp.bfloat16), g)
    put(last, 1, gk1[WINDOW:] + gk * scale)
    put(last, 2, gv1[WINDOW:] + gv)


def finish(scale, seq_lengths, events, near, stats, halves):
    group, _, rows, hd = events.shape
    vmem = pl.BlockSpec(memory_space=pltpu.VMEM)
    return call(
        functools.partial(finish_body, scale),
        in_specs=[pl.BlockSpec(memory_space=pltpu.SMEM)] + [vmem] * 9,
        out_specs=vmem,
        out_shape=jax.ShapeDtypeStruct((group, 3, rows, hd), jnp.bfloat16),
    )(seq_lengths, events, near, stats, *halves)


def join_body(in_ref, *outs):
    hd = in_ref.shape[-1]
    for part, out_ref in enumerate(outs):
        for head in range(H):
            out_ref[0, :, head * hd : (head + 1) * hd] = in_ref[head, part]


def join_heads(pieces):
    heads, parts, rows, hd = pieces.shape
    vmem = pl.BlockSpec(memory_space=pltpu.VMEM)
    return call(
        join_body,
        in_specs=[vmem],
        out_specs=[vmem] * parts,
        out_shape=[jax.ShapeDtypeStruct((1, rows, heads * hd), pieces.dtype)] * parts,
    )(pieces)


def on_device(
    queries,
    keys,
    values,
    grad_out,
    mem_keys,
    mem_values,
    seq_lengths,
    mem_counts,
    block_lists,
    block_slots,
):
    rows, width = queries.shape[1:]
    scale = 1.0 / math.sqrt(width // H)
    reach = WINDOW // rows
    seq, users = lax.axis_size("seq"), lax.axis_size("dp")
    groups = [[first + i for i in range(H)] for first in range(0, seq, H)]
    swap = functools.partial(
        lax.all_to_all, axis_name="seq", split_axis=0, concat_axis=0, tiled=True
    )

    arrays = (queries, keys, values, grad_out)
    packed = pack(users, seq_lengths, block_slots, block_lists, arrays, mem_keys, mem_values)
    packed = packed[: users + 1], packed[users + 1 :]
    sources = [packed[0][0]]
    sources.append(lax.ppermute(packed[1][0], "seq", [(i, i ^ 1) for i in range(seq)]))
    places = [(u, i) for u in range(users) for i in range(seq)]
    for step in range(1, users):
        for side in range(2):
            pairs = [
                (u * seq + i, (u + step) % users * seq + (i ^ side)) for u, i in places
            ]
            sources.append(lax.ppermute(packed[side][step], ("dp", "seq"), pairs))
    pairs = [(i, i - reach if i % H < reach else i + reach) for i in range(seq)]
    pairs = [(i, j) for i, j in pairs if 0 <= j < seq]
    edges = [
        lax.ppermute(packed[side][users], "seq", [(i, j ^ side) for i, j in pairs])
        for side in range(2)
    ]

    events = swap(split_heads(seq_lengths, arrays), axis_index_groups=groups)

    held, depth = mem_keys.shape[:2]
    pieces = far_pieces(held, depth, block_slots, block_lists, sources)
    far = []
    for around in range(1, seq // H):
        for step, piece in enumerate(pieces):
            pairs = [
                (i, ((i // H + around) * H) % seq + ((i % H) ^ (2 * step))) for i in range(seq)
            ]
            far.append(lax.ppermute(piece, "seq", pairs))
    near = near_pieces(held, depth, block_slots, block_lists, edges, sources, events)
    parities = [group[parity::2] for group in groups for parity in range(2)]
    near = swap(near, axis_index_groups=parities)

    part = functools.partial(attend, scale, depth)
    *first, stats = part(0, seq_lengths, mem_counts, events, near, far)
    stats = lax.ppermute(stats, "seq", [(i + H, i) for i in range(seq - H)])
    second = part(1, seq_lengths, mem_counts, events, near, far)
    out = finish(scale, seq_lengths, events, near, stats, [*first, *second])
    return tuple(join_heads(swap(out, axis_index_groups=groups)))


def solution(mesh):
    spread = P("dp", "seq", None)
    return jax.shard_map(
        on_device,
        mesh=mesh,
        in_specs=(spread,) * 6 + (P(),) * 4,
        out_specs=(spread,) * 3,
        check_vma=False,
    )
```

time: 97.8 us -> 99.2 us (1.014)
  Pallas kernels: 22.4 us -> 25 us
  waiting for transfers between devices: 32.6 us -> 31.1 us
    ppermute x11 -> x9, starting transfers between devices: 13.9 us -> 11.4 us  [the longest x4 7.71 us: on_device(): far.append(lax.ppermute(piece, 'seq', pairs))]
    all_to_all x2, starting transfers between devices: 11.6 us -> 14 us  [the longest x1 8.7 us: on_device(): near = swap(near, axis_index_groups=parities)]
    pallas_call x4, Pallas kernels: 13.4 us -> 15.3 us  [the longest x2 12.2 us: attend(): call(functools.partial(attend_body, scale, depth, half, len(far)), grid=(...]
    ppermute x11 -> x9, waiting for transfers between devices: 32.6 us -> 31.1 us  [the longest x4 19.3 us: on_device(): far.append(lax.ppermute(piece, 'seq', pairs))]
  transfers between devices with their start and end apart: 14 -> 12, of which waited for: 9 -> 6; matrix products, arithmetic and copies ran while one was open for 0% -> 0% of each run, Pallas kernels for 7% -> 11%
where the time goes in v1:
time: 99.2 us; the launch traced here: 98.7 us
  waiting for transfers between devices  31.1 us (31%)
  starting transfers between devices  26.7 us (27%)
  Pallas kernels  25 us (25%)
  blocking collectives  14.2 us (14%)
    ppermute x4, waiting for transfers between devices, on_device(): far.append(lax.ppermute(piece, 'seq', pairs))  19.3 us
    all_to_all x1, blocking collectives, on_device(): return tuple(join_heads(swap(out, axis_index_groups=groups)))  14.2 us
    pallas_call x2, Pallas kernels, attend(): call(functools.partial(attend_body, scale, depth, half, len(far)), grid=(...  12.2 us
    ppermute x2, waiting for transfers between devices, on_device(): sources.append(lax.ppermute(packed[side][step], ('dp', 'seq'), pairs))  11.8 us
    all_to_all x1, starting transfers between devices, on_device(): near = swap(near, axis_index_groups=parities)  8.7 us
    ppermute x4, starting transfers between devices, on_device(): far.append(lax.ppermute(piece, 'seq', pairs))  7.71 us
    all_to_all x1, starting transfers between devices, on_device(): events = swap(split_heads(seq_lengths, arrays), axis_index_groups=groups)  5.27 us
    pallas_call x1, Pallas kernels, pack(): call(functools.partial(pack_body, users), limit=VMEM_WHOLE, in_specs=[sme...  3.54 us
  transfers between devices with their start and end apart: 12, of which 6 were waited for; matrix products, arithmetic and copies ran while one was open for 0% of the time, Pallas kernels for 11%

profile of v1, /device:TPU:0, one launch (start us, length us, event | category | flops | bytes accessed | tf_op | source)
XLA Modules:
  0.0 98.7 jit_solution(8702510303305820607)
XLA Ops:
  0.6 2.9 %shard_map.121 = bf16[8,4,128,128]{3,2,1,0:T(8,128)(2,1)} custom-call(s32[2]{0:T(128)} %length_ref.9, bf16[1,128,1024]{2,1,0:T(8,128)(2,1)} %refs_0_.3, bf16[1,128,1024]{2,1,0:T(8,128)(2,1)} %refs_1_.3, bf16[1,128,1024]{2,1,0:T(8,128)(2,1)} %refs_2_.3, bf16[1,128,1024]{2,1,0:T(8,128)(2,1)} %refs_3_.3), custom_call_target="tpu_custom_call" | custom-call | tf_op jit(solution)/shard_map/pallas_call | solution.py:165
  3.5 5.3 %all-to-all-start = ((bf16[8,4,128,128]{3,2,1,0:T(8,128)(2,1)}), bf16[8,4,128,128]{3,2,1,0:T(8,128)(2,1)}, u32[]{:S(2)}, u32[]{:S(2)}) async-start(bf16[8,4,128,128]{3,2,1,0:T(8,128)(2,1)} %shard_map.121), calls=%async_computation | async-start | bytes 2097152 | tf_op jit(solution)/shard_map/all_to_all | solution.py:486
  8.8 3.5 %shard_map.122 = (bf16[4,2,128,128]{3,2,1,0:T(8,128)(2,1)}, bf16[4,2,128,128]{3,2,1,0:T(8,128)(2,1)}, bf16[4,2,128,128]{3,2,1,0:T(8,128)(2,1)}, bf16[4,2,128,128...) custom-call(s32[2]{0:T(128)} %length_ref.9, s32[16]{0:T(128)} %slots_ref.5, ...), custom_call_target="tpu_custom_call" | custom-call | tf_op jit(solution)/shard_map/pallas_call | solution.py:126
  12.4 0.7 collective-permute-start
  13.0 0.7 collective-permute-start.1
  13.7 0.6 collective-permute-start.2
  14.3 1.8 %collective-permute-start.3 = (bf16[4,2,128,128]{3,2,1,0:T(8,128)(2,1)}, bf16[4,2,128,128]{3,2,1,0:T(8,128)(2,1)S(1)}, u32[]{:S(2)}, u32[]{:S(2)}) collective-permute-start(bf16[4,2,128,128]{3,2,1,0:T(8,128)(2,1)} %get-tuple-element.24), channel_id=1, source_target_pairs={{0,16},{1,17},{2,18},{3,19},{4,20},{5,21},{6,22},{7,23},{8,24},{9,... | collective-permute-start | bytes 786440 | tf_op jit(solution)/shard_map/ppermute | solution.py:478
  16.1 0.0 collective-permute-start.4
  16.1 0.0 collective-permute-done.refs_0_
  16.1 0.0 collective-permute-done.1.refs_1_
  16.1 0.0 collective-permute-done.2.refs_3_.refs_1_
  16.1 7.5 %collective-permute-done.3.refs_4_.refs_2_ = bf16[4,2,128,128]{3,2,1,0:T(8,128)(2,1)S(1)} collective-permute-done((bf16[4,2,128,128]{3,2,1,0:T(8,128)(2,1)}, bf16[4,2,128,128]{3,2,1,0:T(8,128)(2,1)S(1)}, u32[]{:S(2)}, u32[]{:S(2)}) %collective-permute-start.3) | collective-permute-done | bytes 262176 | tf_op jit(solution)/shard_map/ppermute | solution.py:478
  23.6 4.3 %collective-permute-done.4.refs_5_.refs_3_ = bf16[4,2,128,128]{3,2,1,0:T(8,128)(2,1)S(1)} collective-permute-done((bf16[4,2,128,128]{3,2,1,0:T(8,128)(2,1)}, bf16[4,2,128,128]{3,2,1,0:T(8,128)(2,1)S(1)}, u32[]{:S(2)}, u32[]{:S(2)}) %collective-permute-start.4) | collective-permute-done | bytes 262176 | tf_op jit(solution)/shard_map/ppermute | solution.py:478
  27.9 0.9 copy-done
  28.9 2.0 %shard_map.123 = bf16[4,2,512,128]{3,2,1,0:T(8,128)(2,1)} custom-call(s32[16]{0:T(128)S(1)} %copy-done.3, s32[2,4]{1,0:T(2,128)S(1)} %copy-done.2, bf16[8,4,128,128]{3,2,1,0:T(8,128)(2,1)} %all-to-all-done._.ev_ref, bf16[4,2,128,128]{3,2,1,0:T(8,128)(2,1)S(1)} %collective-permute-done.refs_0_, bf16[4,2,128,128]{3,2,1,0:T(8,128)(2,1)S(1)} %collective-permute-done.1.refs_1_, ...), custom_call_target="tpu_custom_call" | custom-call | tf_op jit(solution)/shard_map/pallas_call | solution.py:240
  30.9 8.7 %all-to-all-start.1 = ((bf16[4,2,512,128]{3,2,1,0:T(8,128)(2,1)}), bf16[4,2,512,128]{3,2,1,0:T(8,128)(2,1)S(1)}, u32[]{:S(2)}, u32[]{:S(2)}) async-start(bf16[4,2,512,128]{3,2,1,0:T(8,128)(2,1)} %shard_map.123), calls=%async_computation.1 | async-start | bytes 2097152 | tf_op jit(solution)/shard_map/all_to_all | solution.py:499
  39.6 1.1 %shard_map.124 = (bf16[2,2,128,128]{3,2,1,0:T(8,128)(2,1)S(1)}, bf16[2,2,128,128]{3,2,1,0:T(8,128)(2,1)S(1)}, bf16[2,2,128,128]{3,2,1,0:T(8,128)(2,1)S(1)}, bf16[2,2,128,128]{3,2,1,0:T(8,128)(2,1)S(1)}) custom-call(s32[16]{0:T(128)S(1)} %copy-done.3, s32[2,4]{1,0:T(2,128)S(1)} %copy-done.2, bf16[4,2,128,128]{3,2,1,0:T(8,128)(2,1)S(1)} %copy-done.1, ...), custom_call_target="tpu_custom_call" | custom-call | tf_op jit(solution)/shard_map/pallas_call | solution.py:208
  40.7 1.8 %collective-permute-start.5 = (bf16[2,2,128,128]{3,2,1,0:T(8,128)(2,1)S(1)}, bf16[2,2,128,128]{3,2,1,0:T(8,128)(2,1)S(1)}, u32[]{:S(2)}, u32[]{:S(2)}) collective-permute-start(bf16[2,2,128,128]{3,2,1,0:T(8,128)(2,1)S(1)} %get-tuple-element.26), channel_id=1, source_target_pairs={{0,8},{1,9},{2,10},{3,11},{4,12},{5,13},{6,14},{7,15},{8,0},{9,1},... | collective-permute-start | bytes 393224 | tf_op jit(solution)/shard_map/ppermute | solution.py:496
  42.5 2.6 %collective-permute-start.6 = (bf16[2,2,128,128]{3,2,1,0:T(8,128)(2,1)S(1)}, bf16[2,2,128,128]{3,2,1,0:T(8,128)(2,1)S(1)}, u32[]{:S(2)}, u32[]{:S(2)}) collective-permute-start(bf16[2,2,128,128]{3,2,1,0:T(8,128)(2,1)S(1)} %get-tuple-element.27), channel_id=1, source_target_pairs={{0,10},{1,11},{2,8},{3,9},{4,14},{5,15},{6,12},{7,13},{8,2},{9,3},... | collective-permute-start | bytes 393224 | tf_op jit(solution)/shard_map/ppermute | solution.py:496
  45.2 2.6 %collective-permute-start.7 = (bf16[2,2,128,128]{3,2,1,0:T(8,128)(2,1)S(1)}, bf16[2,2,128,128]{3,2,1,0:T(8,128)(2,1)S(1)}, u32[]{:S(2)}, u32[]{:S(2)}) collective-permute-start(bf16[2,2,128,128]{3,2,1,0:T(8,128)(2,1)S(1)} %get-tuple-element.28), channel_id=1, source_target_pairs={{0,12},{1,13},{2,14},{3,15},{4,8},{5,9},{6,10},{7,11},{8,4},{9,5},... | collective-permute-start | bytes 393224 | tf_op jit(solution)/shard_map/ppermute | solution.py:496
  47.8 0.7 collective-permute-start.8
  48.4 6.5 %collective-permute-done.5.refs_0_ = bf16[2,2,128,128]{3,2,1,0:T(8,128)(2,1)S(1)} collective-permute-done((bf16[2,2,128,128]{3,2,1,0:T(8,128)(2,1)S(1)}, bf16[2,2,128,128]{3,2,1,0:T(8,128)(2,1)S(1)}, u32[]{:S(2)}, u32[]{:S(2)}) %collective-permute-start.5) | collective-permute-done | bytes 131104 | tf_op jit(solution)/shard_map/ppermute | solution.py:496
  55.0 2.8 %collective-permute-done.6.refs_1_ = bf16[2,2,128,128]{3,2,1,0:T(8,128)(2,1)S(1)} collective-permute-done((bf16[2,2,128,128]{3,2,1,0:T(8,128)(2,1)S(1)}, bf16[2,2,128,128]{3,2,1,0:T(8,128)(2,1)S(1)}, u32[]{:S(2)}, u32[]{:S(2)}) %collective-permute-start.6) | collective-permute-done | bytes 131104 | tf_op jit(solution)/shard_map/ppermute | solution.py:496
  57.8 6.5 %collective-permute-done.7.refs_2_ = bf16[2,2,128,128]{3,2,1,0:T(8,128)(2,1)S(1)} collective-permute-done((bf16[2,2,128,128]{3,2,1,0:T(8,128)(2,1)S(1)}, bf16[2,2,128,128]{3,2,1,0:T(8,128)(2,1)S(1)}, u32[]{:S(2)}, u32[]{:S(2)}) %collective-permute-start.7) | collective-permute-done | bytes 131104 | tf_op jit(solution)/shard_map/ppermute | solution.py:496
  64.3 3.4 %collective-permute-done.8.refs_3_ = bf16[2,2,128,128]{3,2,1,0:T(8,128)(2,1)S(1)} collective-permute-done((bf16[2,2,128,128]{3,2,1,0:T(8,128)(2,1)S(1)}, bf16[2,2,128,128]{3,2,1,0:T(8,128)(2,1)S(1)}, u32[]{:S(2)}, u32[]{:S(2)}) %collective-permute-start.8) | collective-permute-done | bytes 131104 | tf_op jit(solution)/shard_map/ppermute | solution.py:496
  67.8 6.1 %shard_map.125 = (bf16[4,128,128]{2,1,0:T(8,128)(2,1)S(1)}, f32[1024,128]{1,0:T(8,128)S(1)}, f32[1024,128]{1,0:T(8,128)S(1)}, f32[2,8,256]{2,1,0:T(8,128)S(1)}) custom-call(s32[2]{0:T(128)S(1)} %copy-done.4, s32[2]{0:T(128)S(1)} %copy-done.5, bf16[8,4,128,128]{3,2,1,0:T(8,128)(2,1)} %all-to-all-done._.ev_ref, ...), custom_call_target="tpu_custom_call" | custom-call | flops 1677721600 | bytes 1310720 | tf_op jit(solution)/shard_map/pallas_call | solution.py:357
  73.9 1.3 %collective-permute-start.9 = (f32[2,8,256]{2,1,0:T(8,128)S(1)}, f32[2,8,256]{2,1,0:T(8,128)S(1)}, u32[]{:S(2)}, u32[]{:S(2)}) collective-permute-start(f32[2,8,256]{2,1,0:T(8,128)S(1)} %get-tuple-element.30), channel_id=1, source_target_pairs={{8,0},{9,1},{10,2},{11,3},{12,4},{13,5},{14,6},{15,7},{24,16},{25,... | collective-permute-start | bytes 49160 | tf_op jit(solution)/shard_map/ppermute | solution.py:503
  75.2 6.1 %shard_map.126 = (bf16[4,128,128]{2,1,0:T(8,128)(2,1)S(1)}, f32[1024,128]{1,0:T(8,128)S(1)}, f32[1024,128]{1,0:T(8,128)S(1)}) custom-call(s32[2]{0:T(128)S(1)} %copy-done.4, s32[2]{0:T(128)S(1)} %copy-done.5, bf16[8,4,128,128]{3,2,1,0:T(8,128)(2,1)} %all-to-all-done._.ev_ref, bf16[4,2,512,128]{3,2,1,0:T(8,128)(2,1)S(1)} %all-to-all-done.1.near_ref, ...), custom_call_target="tpu_custom_call" | custom-call | flops 1677721600 | bytes 1310720 | tf_op jit(solution)/shard_map/pallas_call | solution.py:357
  81.3 0.0 collective-permute-done.9.stats_ref
  81.3 2.1 %shard_map.127 = bf16[8,3,128,128]{3,2,1,0:T(8,128)(2,1)S(1)} custom-call(s32[2]{0:T(128)S(1)} %copy-done.4, bf16[8,4,128,128]{3,2,1,0:T(8,128)(2,1)} %all-to-all-done._.ev_ref, bf16[4,2,512,128]{3,2,1,0:T(8,128)(2,1)S(1)} %all-to-all-done.1.near_ref, f32[2,8,256]{2,1,0:T(8,128)S(1)} %collective-permute-done.9.stats_ref, ...), custom_call_target="tpu_custom_call" | custom-call | tf_op jit(solution)/shard_map/pallas_call | solution.py:420
  83.4 14.2 %all_to_all.15.in_ref = bf16[8,3,128,128]{3,2,1,0:T(8,128)(2,1)S(1)} all-to-all(bf16[8,3,128,128]{3,2,1,0:T(8,128)(2,1)S(1)} %shard_map.127), channel_id=1, replica_groups={{0,1,2,3,4,5,6,7},{8,9,10,11,12,13,14,15},{16,17,18,19,20,21,22,23},{24..., dimensions={0} | all-to-all | bytes 1572864 | tf_op jit(solution)/shard_map/all_to_all | solution.py:506
  97.6 1.1 %shard_map.128 = (bf16[1,128,1024]{2,1,0:T(8,128)(2,1)}, bf16[1,128,1024]{2,1,0:T(8,128)(2,1)}, bf16[1,128,1024]{2,1,0:T(8,128)(2,1)}) custom-call(bf16[8,3,128,128]{3,2,1,0:T(8,128)(2,1)S(1)} %all_to_all.15.in_ref), custom_call_target="tpu_custom_call" | custom-call | tf_op jit(solution)/shard_map/pallas_call | solution.py:438
  (13 shorter events, 0.0 us)
Async XLA Ops:
  3.5 24.4 %all-to-all-start = ((bf16[8,4,128,128]{3,2,1,0:T(8,128)(2,1)}), bf16[8,4,128,128]{3,2,1,0:T(8,128)(2,1)}, u32[]{:S(2)}, u32[]{:S(2)}) async-start(bf16[8,4,128,128]{3,2,1,0:T(8,128)(2,1)} %shard_map.121), calls=%async_computation | async-start | bytes 2097152 | tf_op jit(solution)/shard_map/all_to_all | solution.py:486
  12.4 3.8 %collective-permute-start = (bf16[4,2,128,128]{3,2,1,0:T(8,128)(2,1)}, bf16[4,2,128,128]{3,2,1,0:T(8,128)(2,1)S(1)}, u32[]{:S(2)}, u32[]{:S(2)}) collective-permute-start(bf16[4,2,128,128]{3,2,1,0:T(8,128)(2,1)} %get-tuple-element.20), channel_id=1, source_target_pairs={{4,8},{5,9},{6,10},{7,11},{8,4},{9,5},{10,6},{11,7},{20,24},{21,25... | collective-permute-start | bytes 786440 | tf_op jit(solution)/shard_map/ppermute | solution.py:482
  13.0 3.1 %collective-permute-start.1 = (bf16[4,2,128,128]{3,2,1,0:T(8,128)(2,1)}, bf16[4,2,128,128]{3,2,1,0:T(8,128)(2,1)S(1)}, u32[]{:S(2)}, u32[]{:S(2)}) collective-permute-start(bf16[4,2,128,128]{3,2,1,0:T(8,128)(2,1)} %get-tuple-element.21), channel_id=1, source_target_pairs={{4,9},{5,8},{6,11},{7,10},{8,5},{9,4},{10,7},{11,6},{20,25},{21,24... | collective-permute-start | bytes 786440 | tf_op jit(solution)/shard_map/ppermute | solution.py:482
  13.7 2.4 %collective-permute-start.2 = (bf16[4,2,128,128]{3,2,1,0:T(8,128)(2,1)}, bf16[4,2,128,128]{3,2,1,0:T(8,128)(2,1)S(1)}, u32[]{:S(2)}, u32[]{:S(2)}) collective-permute-start(bf16[4,2,128,128]{3,2,1,0:T(8,128)(2,1)} %get-tuple-element.23), channel_id=1, source_target_pairs={{0,1},{1,0},{2,3},{3,2},{4,5},{5,4},{6,7},{7,6},{8,9},{9,8},{10,11... | collective-permute-start | bytes 786440 | tf_op jit(solution)/shard_map/ppermute | solution.py:471
  14.3 9.4 %collective-permute-start.3 = (bf16[4,2,128,128]{3,2,1,0:T(8,128)(2,1)}, bf16[4,2,128,128]{3,2,1,0:T(8,128)(2,1)S(1)}, u32[]{:S(2)}, u32[]{:S(2)}) collective-permute-start(bf16[4,2,128,128]{3,2,1,0:T(8,128)(2,1)} %get-tuple-element.24), channel_id=1, source_target_pairs={{0,16},{1,17},{2,18},{3,19},{4,20},{5,21},{6,22},{7,23},{8,24},{9,... | collective-permute-start | bytes 786440 | tf_op jit(solution)/shard_map/ppermute | solution.py:478
  16.1 11.8 %copy-start.2 = (s32[2,4]{1,0:T(2,128)S(1)}, s32[2,4]{1,0:T(2,128)}, u32[]{:S(2)}) copy-start(s32[2,4]{1,0:T(2,128)} %lists_ref.5) | copy-start | bytes 100
  16.1 11.8 %copy-start.3 = (s32[16]{0:T(128)S(1)}, s32[16]{0:T(128)}, u32[]{:S(2)}) copy-start(s32[16]{0:T(128)} %slots_ref.5) | copy-start | bytes 196
  16.1 11.8 %collective-permute-start.4 = (bf16[4,2,128,128]{3,2,1,0:T(8,128)(2,1)}, bf16[4,2,128,128]{3,2,1,0:T(8,128)(2,1)S(1)}, u32[]{:S(2)}, u32[]{:S(2)}) collective-permute-start(bf16[4,2,128,128]{3,2,1,0:T(8,128)(2,1)} %get-tuple-element.25), channel_id=1, source_target_pairs={{0,17},{1,16},{2,19},{3,18},{4,21},{5,20},{6,23},{7,22},{8,25},{9,... | collective-permute-start | bytes 786440 | tf_op jit(solution)/shard_map/ppermute | solution.py:478
  27.9 1.0 copy-start
  30.9 8.7 %copy-start.1 = (bf16[4,2,128,128]{3,2,1,0:T(8,128)(2,1)S(1)}, bf16[4,2,128,128]{3,2,1,0:T(8,128)(2,1)}, u32[]{:S(2)}) copy-start(bf16[4,2,128,128]{3,2,1,0:T(8,128)(2,1)} %get-tuple-element.22.refs_2_.refs_0_) | copy-start | bytes 786436
  30.9 36.9 %all-to-all-start.1 = ((bf16[4,2,512,128]{3,2,1,0:T(8,128)(2,1)}), bf16[4,2,512,128]{3,2,1,0:T(8,128)(2,1)S(1)}, u32[]{:S(2)}, u32[]{:S(2)}) async-start(bf16[4,2,512,128]{3,2,1,0:T(8,128)(2,1)} %shard_map.123), calls=%async_computation.1 | async-start | bytes 2097152 | tf_op jit(solution)/shard_map/all_to_all | solution.py:499
  40.7 14.3 %collective-permute-start.5 = (bf16[2,2,128,128]{3,2,1,0:T(8,128)(2,1)S(1)}, bf16[2,2,128,128]{3,2,1,0:T(8,128)(2,1)S(1)}, u32[]{:S(2)}, u32[]{:S(2)}) collective-permute-start(bf16[2,2,128,128]{3,2,1,0:T(8,128)(2,1)S(1)} %get-tuple-element.26), channel_id=1, source_target_pairs={{0,8},{1,9},{2,10},{3,11},{4,12},{5,13},{6,14},{7,15},{8,0},{9,1},... | collective-permute-start | bytes 393224 | tf_op jit(solution)/shard_map/ppermute | solution.py:496
  42.5 15.3 %collective-permute-start.6 = (bf16[2,2,128,128]{3,2,1,0:T(8,128)(2,1)S(1)}, bf16[2,2,128,128]{3,2,1,0:T(8,128)(2,1)S(1)}, u32[]{:S(2)}, u32[]{:S(2)}) collective-permute-start(bf16[2,2,128,128]{3,2,1,0:T(8,128)(2,1)S(1)} %get-tuple-element.27), channel_id=1, source_target_pairs={{0,10},{1,11},{2,8},{3,9},{4,14},{5,15},{6,12},{7,13},{8,2},{9,3},... | collective-permute-start | bytes 393224 | tf_op jit(solution)/shard_map/ppermute | solution.py:496
  45.2 22.6 %copy-start.4 = (s32[2]{0:T(128)S(1)}, s32[2]{0:T(128)}, u32[]{:S(2)}) copy-start(s32[2]{0:T(128)} %length_ref.9) | copy-start | bytes 28
  45.2 22.6 %copy-start.5 = (s32[2]{0:T(128)S(1)}, s32[2]{0:T(128)}, u32[]{:S(2)}) copy-start(s32[2]{0:T(128)} %count_ref.3) | copy-start | bytes 28
  45.2 19.2 %collective-permute-start.7 = (bf16[2,2,128,128]{3,2,1,0:T(8,128)(2,1)S(1)}, bf16[2,2,128,128]{3,2,1,0:T(8,128)(2,1)S(1)}, u32[]{:S(2)}, u32[]{:S(2)}) collective-permute-start(bf16[2,2,128,128]{3,2,1,0:T(8,128)(2,1)S(1)} %get-tuple-element.28), channel_id=1, source_target_pairs={{0,12},{1,13},{2,14},{3,15},{4,8},{5,9},{6,10},{7,11},{8,4},{9,5},... | collective-permute-start | bytes 393224 | tf_op jit(solution)/shard_map/ppermute | solution.py:496
  47.8 20.0 %collective-permute-start.8 = (bf16[2,2,128,128]{3,2,1,0:T(8,128)(2,1)S(1)}, bf16[2,2,128,128]{3,2,1,0:T(8,128)(2,1)S(1)}, u32[]{:S(2)}, u32[]{:S(2)}) collective-permute-start(bf16[2,2,128,128]{3,2,1,0:T(8,128)(2,1)S(1)} %get-tuple-element.29), channel_id=1, source_target_pairs={{0,14},{1,15},{2,12},{3,13},{4,10},{5,11},{6,8},{7,9},{8,6},{9,7},... | collective-permute-start | bytes 393224 | tf_op jit(solution)/shard_map/ppermute | solution.py:496
  73.9 7.4 %collective-permute-start.9 = (f32[2,8,256]{2,1,0:T(8,128)S(1)}, f32[2,8,256]{2,1,0:T(8,128)S(1)}, u32[]{:S(2)}, u32[]{:S(2)}) collective-permute-start(f32[2,8,256]{2,1,0:T(8,128)S(1)} %get-tuple-element.30), channel_id=1, source_target_pairs={{8,0},{9,1},{10,2},{11,3},{12,4},{13,5},{14,6},{15,7},{24,16},{25,... | collective-permute-start | bytes 49160 | tf_op jit(solution)/shard_map/ppermute | solution.py:503

commit v2 on v1

--- a/solution.py
+++ b/solution.py
@@ -13,7 +13,10 @@
 TILE = 256
 NEG = -1e30
 LOG2E = 1.4426950408889634
-VMEM_LIMIT = 48 * 1024 * 1024
+FAR_COST = 10**11
+GATHER_COST = 10**11
+NEAR_COST = 0
+VMEM_LIMIT = 32 * 1024 * 1024
 VMEM_WHOLE = 64 * 1024 * 1024 - 256 * 1024
 
 NT = (((1,), (1,)), ((), ()))
@@ -32,7 +35,9 @@
     return jnp.dot(a, b, preferred_element_type=jnp.float32)
 
 
-def call(body, limit=VMEM_LIMIT, **kw):
+def call(body, limit=VMEM_LIMIT, cost=None, **kw):
+    if cost:
+        kw["cost_estimate"] = pl.CostEstimate(flops=cost, bytes_accessed=0, transcendentals=0)
     return pl.pallas_call(
         body, compiler_params=pltpu.CompilerParams(vmem_limit_bytes=limit), **kw
     )
@@ -187,9 +192,9 @@
     return rows, value
 
 
-def far_body(held, depth, slots_ref, lists_ref, *refs):
+def far_body(held, depth, number, slots_ref, lists_ref, *refs):
     outs = refs[-(H // 2) :]
-    sources = refs[: -(H // 2)]
+    sources = refs[number - 2 : number] + refs[: number - 2]
     pair = lax.rem(lax.axis_index("seq") // 2, H // 2)
     for block in range(lists_ref.shape[1]):
         for step, out_ref in enumerate(outs):
@@ -201,19 +206,22 @@
                     out_ref[part, side, rows] = value
 
 
-def far_pieces(held, depth, block_slots, block_lists, sources):
+def far_pieces(held, depth, block_slots, block_lists, sources, *later_than):
     _, parts, rows, hd = sources[0].shape
     smem = pl.BlockSpec(memory_space=pltpu.SMEM)
     vmem = pl.BlockSpec(memory_space=pltpu.VMEM)
     return call(
-        functools.partial(far_body, held, depth),
-        in_specs=[smem] * 2 + [vmem] * len(sources),
+        functools.partial(far_body, held, depth, len(sources)),
+        cost=FAR_COST,
+        in_specs=[smem] * 2
+        + [vmem] * len(sources)
+        + [pl.BlockSpec(memory_space=pl.ANY)] * len(later_than),
         out_specs=[vmem] * (H // 2),
         out_shape=[jax.ShapeDtypeStruct((parts, 2, rows, hd), sources[0].dtype)] * (H // 2),
-    )(block_slots, block_lists, *sources)
-
-
-def near_body(held, depth, slots_ref, lists_ref, _, *refs):
+    )(block_slots, block_lists, *sources[2:], *sources[:2], *later_than)
+
+
+def near_body(held, depth, slots_ref, lists_ref, _, __, *refs):
     (edge_same, edge_other), sources, out_ref = refs[:2], refs[2:-1], refs[-1]
     odd = lax.rem(lax.axis_index("seq"), 2) == 1
     memory, edges = sources[0].shape[2], edge_same.shape[2]
@@ -232,33 +240,56 @@
             out_ref[pair, part, first + edges :] = jnp.where(odd, same, other)
 
 
-def near_pieces(held, depth, block_slots, block_lists, edges, sources, later_than):
+def near_pieces(held, depth, block_slots, block_lists, edges, sources, *later_than):
     pairs, parts, rows, hd = sources[0].shape
     smem = pl.BlockSpec(memory_space=pltpu.SMEM)
     vmem = pl.BlockSpec(memory_space=pltpu.VMEM)
     size = 2 * (rows + edges[0].shape[2])
     return call(
         functools.partial(near_body, held, depth),
+        cost=NEAR_COST,
         in_specs=[smem] * 2
-        + [pl.BlockSpec(memory_space=pl.ANY)]
+        + [pl.BlockSpec(memory_space=pl.ANY)] * len(later_than)
         + [vmem] * (2 + len(sources)),
         out_specs=vmem,
         out_shape=jax.ShapeDtypeStruct((pairs, parts, size, hd), sources[0].dtype),
-    )(block_slots, block_lists, later_than, *edges, *sources)
+    )(block_slots, block_lists, *later_than, *edges, *sources)
+
+
+def gather_body(*refs):
+    out_ref = refs[-1]
+    size = refs[0].shape[1] * refs[0].shape[2]
+    for i, ref in enumerate(refs[:-1]):
+        for part in range(2):
+            out_ref[part, i * size : (i + 1) * size] = ref[part].reshape(size, ref.shape[3])
+
+
+def gather_far(far):
+    _, sides, rows, hd = far[0].shape
+    vmem = pl.BlockSpec(memory_space=pltpu.VMEM)
+    return call(
+        gather_body,
+        cost=GATHER_COST,
+        in_specs=[vmem] * len(far),
+        out_specs=vmem,
+        out_shape=jax.ShapeDtypeStruct((2, len(far) * sides * rows, hd), far[0].dtype),
+    )(*far)
 
 
 def attend_body(
     scale,
     depth,
     half,
-    memories,
     length_ref,
     count_ref,
     ev_ref,
     near_ref,
+    far_ref,
+    gq_ref,
+    gk_ref,
+    gv_ref,
     *refs,
 ):
-    far_refs, (gq_ref, gk_ref, gv_ref) = refs[:memories], refs[memories : memories + 3]
     k_all, v_all, mk_all, mv_all = refs[-4:]
     step = pl.program_id(0)
     hd = ev_ref.shape[-1]
@@ -287,9 +318,7 @@
         for part, all_ref in enumerate((mk_all, mv_all)):
             first = near_ref.shape[0] * near
             all_ref[:first] = near_ref[:, part, :near].reshape(first, hd)
-            for far_ref in far_refs:
-                all_ref[first : first + near] = far_ref[part].reshape(near, hd)
-                first += near
+            all_ref[first:] = far_ref[part]
 
     span = WINDOW + TILE
     here = pl.ds(half * reach + step * blocks_per_tile, blocks_per_tile)
@@ -338,7 +367,7 @@
     gk_ref[pl.ds(start, span)] += dot_tn(dsw, q) * scale
     gv_ref[pl.ds(start, span)] += dot_tn(pw.astype(jnp.bfloat16), g)
     if half == 0:
-        stats_ref = refs[memories + 3]
+        stats_ref = refs[0]
         lane = lax.broadcasted_iota(jnp.int32, (TILE, hd), 1)
         both = jnp.where(lane == 0, top * slope + jnp.log2(total), delta)
         stats_ref[step] = both.T[:8]
@@ -347,7 +376,7 @@
 def attend(scale, depth, half, seq_lengths, mem_counts, events, near, far):
     _, _, rows, hd = events.shape
     reach = WINDOW // rows
-    memories = (near.shape[2] - 2 * rows) * (near.shape[0] + len(far))
+    memories = (near.shape[2] - 2 * rows) * near.shape[0] + far.shape[1]
     keys = WINDOW + memories
     whole = lambda shape: pl.BlockSpec(shape, lambda t: (0,) * len(shape))
     smem = pl.BlockSpec(memory_space=pltpu.SMEM)
@@ -355,10 +384,9 @@
     if half == 0:
         outs.append(((WINDOW // TILE, 8, TILE), jnp.float32))
     return call(
-        functools.partial(attend_body, scale, depth, half, len(far)),
+        functools.partial(attend_body, scale, depth, half),
         grid=(WINDOW // TILE,),
-        in_specs=[smem, smem, whole(events.shape), whole(near.shape)]
-        + [whole(piece.shape) for piece in far],
+        in_specs=[smem] * 2 + [whole(array.shape) for array in (events, near, far)],
         out_specs=[whole(shape) for shape, _ in outs],
         out_shape=[jax.ShapeDtypeStruct(shape, dtype) for shape, dtype in outs],
         scratch_shapes=[pltpu.VMEM((2 * WINDOW, hd), jnp.bfloat16)] * 2
@@ -368,7 +396,7 @@
             bytes_accessed=4 * keys * hd,
             transcendentals=WINDOW * keys,
         ),
-    )(seq_lengths, mem_counts, events, near, *far)
+    )(seq_lengths, mem_counts, events, near, far)
 
 
 def finish_body(scale, length_ref, ev_ref, near_ref, stats_ref, *refs):
@@ -486,7 +514,7 @@
     events = swap(split_heads(seq_lengths, arrays), axis_index_groups=groups)
 
     held, depth = mem_keys.shape[:2]
-    pieces = far_pieces(held, depth, block_slots, block_lists, sources)
+    pieces = far_pieces(held, depth, block_slots, block_lists, sources, *edges)
     far = []
     for around in range(1, seq // H):
         for step, piece in enumerate(pieces):
@@ -494,7 +522,8 @@
                 (i, ((i // H + around) * H) % seq + ((i % H) ^ (2 * step))) for i in range(seq)
             ]
             far.append(lax.ppermute(piece, "seq", pairs))
-    near = near_pieces(held, depth, block_slots, block_lists, edges, sources, events)
+    far = gather_far(far)
+    near = near_pieces(held, depth, block_slots, block_lists, edges, sources, events, pieces[0])
     parities = [group[parity::2] for group in groups for parity in range(2)]
     near = swap(near, axis_index_groups=parities)
 

time: 99.2 us -> 90.9 us (0.916)
  waiting for transfers between devices: 31.1 us -> 20.7 us
  local copies, waits for them, and re-layouts: 0.96 us -> 2.45 us
  starting transfers between devices: 26.7 us -> 27.9 us
    ppermute x4, waiting for transfers between devices: 19.3 us -> 6.69 us  [on_device(): far.append(lax.ppermute(piece, 'seq', pairs))]
    ppermute x2, waiting for transfers between devices: 11.8 us -> 0.01 us  [on_device(): sources.append(lax.ppermute(packed[side][step], ('dp', 'seq'), pairs))]
    all_to_all x1, waiting for transfers between devices: 0.01 us -> 8.42 us  [on_device(): near = swap(near, axis_index_groups=parities)]
    all_to_all x1, waiting for transfers between devices: 0.01 us -> 5.61 us  [on_device(): events = swap(split_heads(seq_lengths, arrays), axis_index_groups=groups)]
    all_to_all x1, starting transfers between devices: 8.7 us -> 4.1 us  [on_device(): near = swap(near, axis_index_groups=parities)]
    all_to_all x1, starting transfers between devices: 5.27 us -> 7.26 us  [on_device(): events = swap(split_heads(seq_lengths, arrays), axis_index_groups=groups)]
    ppermute x4, starting transfers between devices: 7.71 us -> 9.32 us  [on_device(): far.append(lax.ppermute(piece, 'seq', pairs))]
    unnamed x12 -> x14, local copies, waits for them, and re-layouts: 0.96 us -> 2.45 us
  transfers between devices with their start and end apart: 12 -> 12, of which waited for: 6 -> 4; matrix products, arithmetic and copies ran while one was open for 0% -> 0% of each run, Pallas kernels for 11% -> 14%
where the time goes in v2:
time: 90.9 us; the launch traced here: 90.4 us
  starting transfers between devices  27.9 us (31%)
  Pallas kernels  24.3 us (27%)
  waiting for transfers between devices  20.7 us (23%)
  blocking collectives  14.3 us (16%)
  local copies, waits for them, and re-layouts  2.45 us (3%)
    all_to_all x1, blocking collectives, on_device(): return tuple(join_heads(swap(out, axis_index_groups=groups)))  14.3 us
    pallas_call x2, Pallas kernels, attend(): call(functools.partial(attend_body, scale, depth, half), grid=(WINDOW //...  10.8 us
    ppermute x4, starting transfers between devices, on_device(): far.append(lax.ppermute(piece, 'seq', pairs))  9.32 us
    all_to_all x1, waiting for transfers between devices, on_device(): near = swap(near, axis_index_groups=parities)  8.42 us
    all_to_all x1, starting transfers between devices, on_device(): events = swap(split_heads(seq_lengths, arrays), axis_index_groups=groups)  7.26 us
    ppermute x4, waiting for transfers between devices, on_device(): far.append(lax.ppermute(piece, 'seq', pairs))  6.69 us
    all_to_all x1, waiting for transfers between devices, on_device(): events = swap(split_heads(seq_lengths, arrays), axis_index_groups=groups)  5.61 us
    all_to_all x1, starting transfers between devices, on_device(): near = swap(near, axis_index_groups=parities)  4.1 us
  transfers between devices with their start and end apart: 12, of which 4 were waited for; matrix products, arithmetic and copies ran while one was open for 0% of the time, Pallas kernels for 14%

profile of v2, /device:TPU:0, one launch (start us, length us, event | category | flops | bytes accessed | tf_op | source)
XLA Modules:
  0.0 90.4 jit_solution(11426293653362138993)
XLA Ops:
  0.6 3.5 %shard_map.122 = (bf16[4,2,128,128]{3,2,1,0:T(8,128)(2,1)}, bf16[4,2,128,128]{3,2,1,0:T(8,128)(2,1)}, bf16[4,2,128,128]{3,2,1,0:T(8,128)(2,1)}, bf16[4,2,128,128...) custom-call(s32[2]{0:T(128)} %length_ref.9, s32[16]{0:T(128)} %slots_ref.5, ...), custom_call_target="tpu_custom_call" | custom-call | tf_op jit(solution)/shard_map/pallas_call | solution.py:131
  4.2 3.0 %collective-permute-start = (bf16[4,2,128,128]{3,2,1,0:T(8,128)(2,1)}, bf16[4,2,128,128]{3,2,1,0:T(8,128)(2,1)}, u32[]{:S(2)}, u32[]{:S(2)}) collective-permute-start(bf16[4,2,128,128]{3,2,1,0:T(8,128)(2,1)} %get-tuple-element.20), channel_id=1, source_target_pairs={{0,16},{1,17},{2,18},{3,19},{4,20},{5,21},{6,22},{7,23},{8,24},{9,... | collective-permute-start | bytes 786440 | tf_op jit(solution)/shard_map/ppermute | solution.py:506
  7.2 0.0 collective-permute-start.1
  7.2 0.2 collective-permute-start.2
  7.4 1.4 %collective-permute-start.3 = (bf16[4,2,128,128]{3,2,1,0:T(8,128)(2,1)}, bf16[4,2,128,128]{3,2,1,0:T(8,128)(2,1)}, u32[]{:S(2)}, u32[]{:S(2)}) collective-permute-start(bf16[4,2,128,128]{3,2,1,0:T(8,128)(2,1)} %get-tuple-element.24), channel_id=1, source_target_pairs={{4,8},{5,9},{6,10},{7,11},{8,4},{9,5},{10,6},{11,7},{20,24},{21,25... | collective-permute-start | bytes 786440 | tf_op jit(solution)/shard_map/ppermute | solution.py:510
  8.7 1.4 %collective-permute-start.4 = (bf16[4,2,128,128]{3,2,1,0:T(8,128)(2,1)}, bf16[4,2,128,128]{3,2,1,0:T(8,128)(2,1)}, u32[]{:S(2)}, u32[]{:S(2)}) collective-permute-start(bf16[4,2,128,128]{3,2,1,0:T(8,128)(2,1)} %get-tuple-element.25), channel_id=1, source_target_pairs={{4,9},{5,8},{6,11},{7,10},{8,5},{9,4},{10,7},{11,6},{20,25},{21,24... | collective-permute-start | bytes 786440 | tf_op jit(solution)/shard_map/ppermute | solution.py:510
  10.1 2.9 %shard_map.121 = bf16[8,4,128,128]{3,2,1,0:T(8,128)(2,1)} custom-call(s32[2]{0:T(128)} %length_ref.9, bf16[1,128,1024]{2,1,0:T(8,128)(2,1)} %refs_0_.3, bf16[1,128,1024]{2,1,0:T(8,128)(2,1)} %refs_1_.3, bf16[1,128,1024]{2,1,0:T(8,128)(2,1)} %refs_2_.3, bf16[1,128,1024]{2,1,0:T(8,128)(2,1)} %refs_3_.3), custom_call_target="tpu_custom_call" | custom-call | tf_op jit(solution)/shard_map/pallas_call | solution.py:170
  13.0 0.0 copy-start
  13.0 7.3 %all-to-all-start = ((bf16[8,4,128,128]{3,2,1,0:T(8,128)(2,1)}), bf16[8,4,128,128]{3,2,1,0:T(8,128)(2,1)S(1)}, u32[]{:S(2)}, u32[]{:S(2)}) async-start(bf16[8,4,128,128]{3,2,1,0:T(8,128)(2,1)} %shard_map.121), calls=%async_computation | async-start | bytes 2097152 | tf_op jit(solution)/shard_map/all_to_all | solution.py:514
  20.3 0.0 copy-start.3
  20.3 0.0 collective-permute-done.2.refs_3_
  20.4 0.0 collective-permute-done.3.refs_4_.refs_0_
  20.4 0.6 copy-done.2
  21.0 1.7 %shard_map.123 = (bf16[2,2,128,128]{3,2,1,0:T(8,128)(2,1)S(1)}, bf16[2,2,128,128]{3,2,1,0:T(8,128)(2,1)S(1)}, bf16[2,2,128,128]{3,2,1,0:T(8,128)(2,1)S(1)}, bf16[2,2,128,128]{3,2,1,0:T(8,128)(2,1)S(1)}) custom-call(s32[16]{0:T(128)S(1)} %copy-done.3, s32[2,4]{1,0:T(2,128)S(1)} %copy-done.2, bf16[4,2,128,128]{3,2,1,0:T(8,128)(2,1)} %collective-permute-done.refs_0_.refs_4_, ...), custom_call_target="tpu_custom_call" | custom-call | flops 99999997952 | tf_op jit(solution)/shard_map/pallas_call | solution.py:213
  22.6 5.5 %collective-permute-start.6 = (bf16[2,2,128,128]{3,2,1,0:T(8,128)(2,1)S(1)}, bf16[2,2,128,128]{3,2,1,0:T(8,128)(2,1)S(1)}, u32[]{:S(2)}, u32[]{:S(2)}) collective-permute-start(bf16[2,2,128,128]{3,2,1,0:T(8,128)(2,1)S(1)} %get-tuple-element.27), channel_id=1, source_target_pairs={{0,10},{1,11},{2,8},{3,9},{4,14},{5,15},{6,12},{7,13},{8,2},{9,3},... | collective-permute-start | bytes 393224 | tf_op jit(solution)/shard_map/ppermute | solution.py:524
  28.2 1.4 %collective-permute-start.7 = (bf16[2,2,128,128]{3,2,1,0:T(8,128)(2,1)S(1)}, bf16[2,2,128,128]{3,2,1,0:T(8,128)(2,1)S(1)}, u32[]{:S(2)}, u32[]{:S(2)}) collective-permute-start(bf16[2,2,128,128]{3,2,1,0:T(8,128)(2,1)S(1)} %get-tuple-element.28), channel_id=1, source_target_pairs={{0,12},{1,13},{2,14},{3,15},{4,8},{5,9},{6,10},{7,11},{8,4},{9,5},... | collective-permute-start | bytes 393224 | tf_op jit(solution)/shard_map/ppermute | solution.py:524
  29.6 2.4 %collective-permute-start.8 = (bf16[2,2,128,128]{3,2,1,0:T(8,128)(2,1)S(1)}, bf16[2,2,128,128]{3,2,1,0:T(8,128)(2,1)S(1)}, u32[]{:S(2)}, u32[]{:S(2)}) collective-permute-start(bf16[2,2,128,128]{3,2,1,0:T(8,128)(2,1)S(1)} %get-tuple-element.29), channel_id=1, source_target_pairs={{0,14},{1,15},{2,12},{3,13},{4,10},{5,11},{6,8},{7,9},{8,6},{9,7},... | collective-permute-start | bytes 393224 | tf_op jit(solution)/shard_map/ppermute | solution.py:524
  32.0 5.6 %all-to-all-done._.ev_ref = bf16[8,4,128,128]{3,2,1,0:T(8,128)(2,1)S(1)} async-done(((bf16[8,4,128,128]{3,2,1,0:T(8,128)(2,1)}), bf16[8,4,128,128]{3,2,1,0:T(8,128)(2,1)S(1)}, u32[]{:S(2)}, u32[]{:S(2)}) %all-to-all-start) | async-done | bytes 1048608 | tf_op jit(solution)/shard_map/all_to_all | solution.py:514
  37.6 2.8 %shard_map.124 = bf16[4,2,512,128]{3,2,1,0:T(8,128)(2,1)} custom-call(s32[16]{0:T(128)S(1)} %copy-done.3, s32[2,4]{1,0:T(2,128)S(1)} %copy-done.2, bf16[8,4,128,128]{3,2,1,0:T(8,128)(2,1)S(1)} %all-to-all-done._.ev_ref, bf16[2,2,128,128]{3,2,1,0:T(8,128)(2,1)S(1)} %get-tuple-element.26.__, bf16[4,2,128,128]{3,2,1,0:T(8,128)(2,1)} %collective-permute-done.3.refs_4_.refs_0_, ...), custom_call_target="tpu_custom_call" | custom-call | tf_op jit(solution)/shard_map/pallas_call | solution.py:248
  40.4 4.1 %all-to-all-start.1 = ((bf16[4,2,512,128]{3,2,1,0:T(8,128)(2,1)}), bf16[4,2,512,128]{3,2,1,0:T(8,128)(2,1)S(1)}, u32[]{:S(2)}, u32[]{:S(2)}) async-start(bf16[4,2,512,128]{3,2,1,0:T(8,128)(2,1)} %shard_map.124), calls=%async_computation.1 | async-start | bytes 2097152 | tf_op jit(solution)/shard_map/all_to_all | solution.py:528
  44.5 0.0 collective-permute-done.6.refs_1_
  44.5 1.4 %collective-permute-done.8.refs_3_ = bf16[2,2,128,128]{3,2,1,0:T(8,128)(2,1)S(1)} collective-permute-done((bf16[2,2,128,128]{3,2,1,0:T(8,128)(2,1)S(1)}, bf16[2,2,128,128]{3,2,1,0:T(8,128)(2,1)S(1)}, u32[]{:S(2)}, u32[]{:S(2)}) %collective-permute-start.8) | collective-permute-done | bytes 131104 | tf_op jit(solution)/shard_map/ppermute | solution.py:524
  45.9 5.3 %collective-permute-done.5.refs_0_ = bf16[2,2,128,128]{3,2,1,0:T(8,128)(2,1)S(1)} collective-permute-done((bf16[2,2,128,128]{3,2,1,0:T(8,128)(2,1)S(1)}, bf16[2,2,128,128]{3,2,1,0:T(8,128)(2,1)S(1)}, u32[]{:S(2)}, u32[]{:S(2)}) %collective-permute-start.5) | collective-permute-done | bytes 131104 | tf_op jit(solution)/shard_map/ppermute | solution.py:524
  51.2 0.8 copy-done.5
  52.0 8.4 %all-to-all-done.1.near_ref = bf16[4,2,512,128]{3,2,1,0:T(8,128)(2,1)S(1)} async-done(((bf16[4,2,512,128]{3,2,1,0:T(8,128)(2,1)}), bf16[4,2,512,128]{3,2,1,0:T(8,128)(2,1)S(1)}, u32[]{:S(2)}, u32[]{:S(2)}) %all-to-all-start.1) | async-done | bytes 1048608 | tf_op jit(solution)/shard_map/all_to_all | solution.py:528
  60.4 1.0 %copy-done.6 = bf16[2,1024,128]{2,1,0:T(8,128)(2,1)S(1)} copy-done((bf16[2,1024,128]{2,1,0:T(8,128)(2,1)S(1)}, bf16[2,1024,128]{2,1,0:T(8,128)(2,1)}, u32[]{:S(2)}) %copy-start.6) | copy-done | bytes 524312
  61.5 5.4 %shard_map.126 = (bf16[4,128,128]{2,1,0:T(8,128)(2,1)S(1)}, f32[1024,128]{1,0:T(8,128)S(1)}, f32[1024,128]{1,0:T(8,128)S(1)}, f32[2,8,256]{2,1,0:T(8,128)S(1)}) custom-call(s32[2]{0:T(128)S(1)} %copy-done.1, s32[2]{0:T(128)S(1)} %copy-done.4, bf16[8,4,128,128]{3,2,1,0:T(8,128)(2,1)S(1)} %all-to-all-done._.ev_ref, ...), custom_call_target="tpu_custom_call" | custom-call | flops 1677721600 | bytes 1310720 | tf_op jit(solution)/shard_map/pallas_call | solution.py:386
  66.9 1.3 %collective-permute-start.9 = (f32[2,8,256]{2,1,0:T(8,128)S(1)}, f32[2,8,256]{2,1,0:T(8,128)S(1)}, u32[]{:S(2)}, u32[]{:S(2)}) collective-permute-start(f32[2,8,256]{2,1,0:T(8,128)S(1)} %get-tuple-element.30), channel_id=1, source_target_pairs={{8,0},{9,1},{10,2},{11,3},{12,4},{13,5},{14,6},{15,7},{24,16},{25,... | collective-permute-start | bytes 49160 | tf_op jit(solution)/shard_map/ppermute | solution.py:532
  68.2 5.4 %shard_map.127 = (bf16[4,128,128]{2,1,0:T(8,128)(2,1)S(1)}, f32[1024,128]{1,0:T(8,128)S(1)}, f32[1024,128]{1,0:T(8,128)S(1)}) custom-call(s32[2]{0:T(128)S(1)} %copy-done.1, s32[2]{0:T(128)S(1)} %copy-done.4, bf16[8,4,128,128]{3,2,1,0:T(8,128)(2,1)S(1)} %all-to-all-done._.ev_ref, bf16[4,2,512,128]{3,2,1,0:T(8,128)(2,1)S(1)} %all-to-all-done.1.near_ref, ...), custom_call_target="tpu_custom_call" | custom-call | flops 1677721600 | bytes 1310720 | tf_op jit(solution)/shard_map/pallas_call | solution.py:386
  73.6 1.5 %shard_map.128 = bf16[8,3,128,128]{3,2,1,0:T(8,128)(2,1)S(1)} custom-call(s32[2]{0:T(128)S(1)} %copy-done.1, bf16[8,4,128,128]{3,2,1,0:T(8,128)(2,1)S(1)} %all-to-all-done._.ev_ref, bf16[4,2,512,128]{3,2,1,0:T(8,128)(2,1)S(1)} %all-to-all-done.1.near_ref, f32[2,8,256]{2,1,0:T(8,128)S(1)} %collective-permute-done.9.stats_ref, ...), custom_call_target="tpu_custom_call" | custom-call | tf_op jit(solution)/shard_map/pallas_call | solution.py:448
  75.0 14.3 %all_to_all.15.in_ref = bf16[8,3,128,128]{3,2,1,0:T(8,128)(2,1)S(1)} all-to-all(bf16[8,3,128,128]{3,2,1,0:T(8,128)(2,1)S(1)} %shard_map.128), channel_id=1, replica_groups={{0,1,2,3,4,5,6,7},{8,9,10,11,12,13,14,15},{16,17,18,19,20,21,22,23},{24..., dimensions={0} | all-to-all | bytes 1572864 | tf_op jit(solution)/shard_map/all_to_all | solution.py:535
  89.3 1.1 %shard_map.129 = (bf16[1,128,1024]{2,1,0:T(8,128)(2,1)}, bf16[1,128,1024]{2,1,0:T(8,128)(2,1)}, bf16[1,128,1024]{2,1,0:T(8,128)(2,1)}) custom-call(bf16[8,3,128,128]{3,2,1,0:T(8,128)(2,1)S(1)} %all_to_all.15.in_ref), custom_call_target="tpu_custom_call" | custom-call | tf_op jit(solution)/shard_map/pallas_call | solution.py:466
  (16 shorter events, 0.1 us)
Async XLA Ops:
  4.2 16.1 %collective-permute-start = (bf16[4,2,128,128]{3,2,1,0:T(8,128)(2,1)}, bf16[4,2,128,128]{3,2,1,0:T(8,128)(2,1)}, u32[]{:S(2)}, u32[]{:S(2)}) collective-permute-start(bf16[4,2,128,128]{3,2,1,0:T(8,128)(2,1)} %get-tuple-element.20), channel_id=1, source_target_pairs={{0,16},{1,17},{2,18},{3,19},{4,20},{5,21},{6,22},{7,23},{8,24},{9,... | collective-permute-start | bytes 786440 | tf_op jit(solution)/shard_map/ppermute | solution.py:506
  7.2 13.1 %collective-permute-start.1 = (bf16[4,2,128,128]{3,2,1,0:T(8,128)(2,1)}, bf16[4,2,128,128]{3,2,1,0:T(8,128)(2,1)}, u32[]{:S(2)}, u32[]{:S(2)}) collective-permute-start(bf16[4,2,128,128]{3,2,1,0:T(8,128)(2,1)} %get-tuple-element.21), channel_id=1, source_target_pairs={{0,17},{1,16},{2,19},{3,18},{4,21},{5,20},{6,23},{7,22},{8,25},{9,... | collective-permute-start | bytes 786440 | tf_op jit(solution)/shard_map/ppermute | solution.py:506
  7.2 13.2 %collective-permute-start.2 = (bf16[4,2,128,128]{3,2,1,0:T(8,128)(2,1)}, bf16[4,2,128,128]{3,2,1,0:T(8,128)(2,1)}, u32[]{:S(2)}, u32[]{:S(2)}) collective-permute-start(bf16[4,2,128,128]{3,2,1,0:T(8,128)(2,1)} %get-tuple-element.23), channel_id=1, source_target_pairs={{0,1},{1,0},{2,3},{3,2},{4,5},{5,4},{6,7},{7,6},{8,9},{9,8},{10,11... | collective-permute-start | bytes 786440 | tf_op jit(solution)/shard_map/ppermute | solution.py:499
  7.4 13.0 %collective-permute-start.3 = (bf16[4,2,128,128]{3,2,1,0:T(8,128)(2,1)}, bf16[4,2,128,128]{3,2,1,0:T(8,128)(2,1)}, u32[]{:S(2)}, u32[]{:S(2)}) collective-permute-start(bf16[4,2,128,128]{3,2,1,0:T(8,128)(2,1)} %get-tuple-element.24), channel_id=1, source_target_pairs={{4,8},{5,9},{6,10},{7,11},{8,4},{9,5},{10,6},{11,7},{20,24},{21,25... | collective-permute-start | bytes 786440 | tf_op jit(solution)/shard_map/ppermute | solution.py:510
  8.7 11.6 %collective-permute-start.4 = (bf16[4,2,128,128]{3,2,1,0:T(8,128)(2,1)}, bf16[4,2,128,128]{3,2,1,0:T(8,128)(2,1)}, u32[]{:S(2)}, u32[]{:S(2)}) collective-permute-start(bf16[4,2,128,128]{3,2,1,0:T(8,128)(2,1)} %get-tuple-element.25), channel_id=1, source_target_pairs={{4,9},{5,8},{6,11},{7,10},{8,5},{9,4},{10,7},{11,6},{20,25},{21,24... | collective-permute-start | bytes 786440 | tf_op jit(solution)/shard_map/ppermute | solution.py:510
  13.0 7.3 %copy-start = (bf16[4,2,128,128]{3,2,1,0:T(8,128)(2,1)S(1)}, bf16[4,2,128,128]{3,2,1,0:T(8,128)(2,1)}, u32[]{:S(2)}) copy-start(bf16[4,2,128,128]{3,2,1,0:T(8,128)(2,1)} %get-tuple-element.22.refs_2_) | copy-start | bytes 786436
  13.0 24.5 %all-to-all-start = ((bf16[8,4,128,128]{3,2,1,0:T(8,128)(2,1)}), bf16[8,4,128,128]{3,2,1,0:T(8,128)(2,1)S(1)}, u32[]{:S(2)}, u32[]{:S(2)}) async-start(bf16[8,4,128,128]{3,2,1,0:T(8,128)(2,1)} %shard_map.121), calls=%async_computation | async-start | bytes 2097152 | tf_op jit(solution)/shard_map/all_to_all | solution.py:514
  20.3 0.7 copy-start.2
  20.3 0.7 copy-start.3
  22.6 21.8 %collective-permute-start.6 = (bf16[2,2,128,128]{3,2,1,0:T(8,128)(2,1)S(1)}, bf16[2,2,128,128]{3,2,1,0:T(8,128)(2,1)S(1)}, u32[]{:S(2)}, u32[]{:S(2)}) collective-permute-start(bf16[2,2,128,128]{3,2,1,0:T(8,128)(2,1)S(1)} %get-tuple-element.27), channel_id=1, source_target_pairs={{0,10},{1,11},{2,8},{3,9},{4,14},{5,15},{6,12},{7,13},{8,2},{9,3},... | collective-permute-start | bytes 393224 | tf_op jit(solution)/shard_map/ppermute | solution.py:524
  28.2 16.3 %collective-permute-start.7 = (bf16[2,2,128,128]{3,2,1,0:T(8,128)(2,1)S(1)}, bf16[2,2,128,128]{3,2,1,0:T(8,128)(2,1)S(1)}, u32[]{:S(2)}, u32[]{:S(2)}) collective-permute-start(bf16[2,2,128,128]{3,2,1,0:T(8,128)(2,1)S(1)} %get-tuple-element.28), channel_id=1, source_target_pairs={{0,12},{1,13},{2,14},{3,15},{4,8},{5,9},{6,10},{7,11},{8,4},{9,5},... | collective-permute-start | bytes 393224 | tf_op jit(solution)/shard_map/ppermute | solution.py:524
  29.6 16.3 %collective-permute-start.8 = (bf16[2,2,128,128]{3,2,1,0:T(8,128)(2,1)S(1)}, bf16[2,2,128,128]{3,2,1,0:T(8,128)(2,1)S(1)}, u32[]{:S(2)}, u32[]{:S(2)}) collective-permute-start(bf16[2,2,128,128]{3,2,1,0:T(8,128)(2,1)S(1)} %get-tuple-element.29), channel_id=1, source_target_pairs={{0,14},{1,15},{2,12},{3,13},{4,10},{5,11},{6,8},{7,9},{8,6},{9,7},... | collective-permute-start | bytes 393224 | tf_op jit(solution)/shard_map/ppermute | solution.py:524
  32.0 19.2 %collective-permute-start.5 = (bf16[2,2,128,128]{3,2,1,0:T(8,128)(2,1)S(1)}, bf16[2,2,128,128]{3,2,1,0:T(8,128)(2,1)S(1)}, u32[]{:S(2)}, u32[]{:S(2)}) collective-permute-start(bf16[2,2,128,128]{3,2,1,0:T(8,128)(2,1)S(1)} %get-tuple-element.26.__), channel_id=1, source_target_pairs={{0,8},{1,9},{2,10},{3,11},{4,12},{5,13},{6,14},{7,15},{8,0},{9,1},... | collective-permute-start | bytes 393224 | tf_op jit(solution)/shard_map/ppermute | solution.py:524
  40.4 20.1 %all-to-all-start.1 = ((bf16[4,2,512,128]{3,2,1,0:T(8,128)(2,1)}), bf16[4,2,512,128]{3,2,1,0:T(8,128)(2,1)S(1)}, u32[]{:S(2)}, u32[]{:S(2)}) async-start(bf16[4,2,512,128]{3,2,1,0:T(8,128)(2,1)} %shard_map.124), calls=%async_computation.1 | async-start | bytes 2097152 | tf_op jit(solution)/shard_map/all_to_all | solution.py:528
  44.5 16.0 %copy-start.1 = (s32[2]{0:T(128)S(1)}, s32[2]{0:T(128)}, u32[]{:S(2)}) copy-start(s32[2]{0:T(128)} %length_ref.9) | copy-start | bytes 28
  44.5 16.0 %copy-start.4 = (s32[2]{0:T(128)S(1)}, s32[2]{0:T(128)}, u32[]{:S(2)}) copy-start(s32[2]{0:T(128)} %count_ref.3) | copy-start | bytes 28
  51.2 0.8 copy-start.5
  60.4 1.0 %copy-start.6 = (bf16[2,1024,128]{2,1,0:T(8,128)(2,1)S(1)}, bf16[2,1024,128]{2,1,0:T(8,128)(2,1)}, u32[]{:S(2)}) copy-start(bf16[2,1024,128]{2,1,0:T(8,128)(2,1)} %copy-done.5) | copy-start | bytes 1572868
  66.9 6.7 %collective-permute-start.9 = (f32[2,8,256]{2,1,0:T(8,128)S(1)}, f32[2,8,256]{2,1,0:T(8,128)S(1)}, u32[]{:S(2)}, u32[]{:S(2)}) collective-permute-start(f32[2,8,256]{2,1,0:T(8,128)S(1)} %get-tuple-element.30), channel_id=1, source_target_pairs={{8,0},{9,1},{10,2},{11,3},{12,4},{13,5},{14,6},{15,7},{24,16},{25,... | collective-permute-start | bytes 49160 | tf_op jit(solution)/shard_map/ppermute | solution.py:532

commit v3 on v2

--- a/solution.py
+++ b/solution.py
@@ -14,7 +14,7 @@
 NEG = -1e30
 LOG2E = 1.4426950408889634
 FAR_COST = 10**11
-GATHER_COST = 10**11
+ARRIVED_COST = 10**11
 NEAR_COST = 0
 VMEM_LIMIT = 32 * 1024 * 1024
 VMEM_WHOLE = 64 * 1024 * 1024 - 256 * 1024
@@ -221,7 +221,7 @@
     )(block_slots, block_lists, *sources[2:], *sources[:2], *later_than)
 
 
-def near_body(held, depth, slots_ref, lists_ref, _, __, *refs):
+def near_body(held, depth, slots_ref, lists_ref, _, *refs):
     (edge_same, edge_other), sources, out_ref = refs[:2], refs[2:-1], refs[-1]
     odd = lax.rem(lax.axis_index("seq"), 2) == 1
     memory, edges = sources[0].shape[2], edge_same.shape[2]
@@ -256,147 +256,143 @@
     )(block_slots, block_lists, *later_than, *edges, *sources)
 
 
-def gather_body(*refs):
-    out_ref = refs[-1]
-    size = refs[0].shape[1] * refs[0].shape[2]
-    for i, ref in enumerate(refs[:-1]):
-        for part in range(2):
-            out_ref[part, i * size : (i + 1) * size] = ref[part].reshape(size, ref.shape[3])
-
-
-def gather_far(far):
-    _, sides, rows, hd = far[0].shape
-    vmem = pl.BlockSpec(memory_space=pltpu.VMEM)
-    return call(
-        gather_body,
-        cost=GATHER_COST,
-        in_specs=[vmem] * len(far),
-        out_specs=vmem,
-        out_shape=jax.ShapeDtypeStruct((2, len(far) * sides * rows, hd), far[0].dtype),
+def arrived_body(*refs):
+    refs[-1][...] = jnp.zeros_like(refs[-1])
+
+
+def arrived(far):
+    return call(
+        arrived_body,
+        cost=ARRIVED_COST,
+        in_specs=[pl.BlockSpec(memory_space=pl.ANY)] * len(far),
+        out_specs=pl.BlockSpec(memory_space=pltpu.VMEM),
+        out_shape=jax.ShapeDtypeStruct((8, 128), jnp.float32),
     )(*far)
 
 
-def attend_body(
-    scale,
-    depth,
-    half,
-    length_ref,
-    count_ref,
-    ev_ref,
-    near_ref,
-    far_ref,
-    gq_ref,
-    gk_ref,
-    gv_ref,
-    *refs,
-):
-    k_all, v_all, mk_all, mv_all = refs[-4:]
-    step = pl.program_id(0)
-    hd = ev_ref.shape[-1]
-    rows = ev_ref.shape[2]
-    reach = WINDOW // rows
+def attend_body(scale, depth, half, memories, length_ref, count_ref, _, ev_ref, near_ref, *refs):
+    far_refs, refs = refs[:memories], refs[memories:]
+    gq_ref, gk_ref, gv_ref = refs[:3]
+    rows, hd = ev_ref.shape[2:]
+    tile = 2 * rows
+    tiles = WINDOW // tile
+    near = near_ref.shape[2] - 2 * rows
     user = lax.axis_index("dp")
     length, count = length_ref[user], count_ref[user]
     base = (lax.axis_index("seq") // H) * (H * rows) + half * WINDOW
     slope = scale * LOG2E
-    blocks_per_tile = TILE // rows
-    near = near_ref.shape[2] - 2 * rows
-
-    @pl.when(step == 0)
-    def _():
+
+    def events(part, chunk):
+        return ev_ref[2 * chunk : 2 * chunk + 2, part].reshape(tile, hd)
+
+    def window(part, chunk):
+        chunk += half * tiles
+        if chunk < 0:
+            return near_ref[tiles + chunk, part - 1, near:].reshape(tile, hd)
+        return events(part, chunk)
+
+    per = max(1, tile // near)
+    memory = [
+        [
+            near_ref[first : first + per, part, :near].reshape(-1, hd)
+            for first in range(0, near_ref.shape[0], per)
+        ]
+        + [
+            jnp.concatenate(
+                [ref[part].reshape(near, hd) for ref in far_refs[first : first + per]], axis=0
+            )
+            for first in range(0, memories, per)
+        ]
+        for part in range(2)
+    ]
+    line = lax.broadcasted_iota(jnp.int32, (tile, tile), 0)
+    column = lax.broadcasted_iota(jnp.int32, (tile, tile), 1)
+    which = lax.broadcasted_iota(jnp.int32, (1, per * near), 1)
+    live = lax.rem(which, near // 2) // depth < count
+
+    sums = {}
+    for this in range(tiles):
+        q, g = events(0, half * tiles + this), events(3, half * tiles + this)
+        chunks = list(range(this - tiles, this + 1))
+        keys = [window(1, chunk) for chunk in chunks] + memory[0]
+        values = [window(2, chunk) for chunk in chunks] + memory[1]
+        score = []
+        for i, key in enumerate(keys):
+            s = dot_nt(q, key)
+            if i <= tiles:
+                position = base + chunks[i] * tile + column[:1]
+                allowed = (position >= 0) & (position < length)
+                if i == 0:
+                    allowed = allowed & (column > line)
+                elif i == tiles:
+                    allowed = (allowed & (column < line)) | (column == line)
+                s = jnp.where(allowed, s, NEG)
+            else:
+                s = jnp.where(live, s, NEG)
+            score.append(s)
+        top = functools.reduce(
+            jnp.maximum, [s for s in score if s.shape == score[0].shape]
+        )
+        top = jnp.max(top, axis=1, keepdims=True)
+        for s in score:
+            if s.shape != score[0].shape:
+                top = jnp.maximum(top, jnp.max(s, axis=1, keepdims=True))
+        expo = [jnp.exp2((s - top) * slope) for s in score]
+        dprob = [dot_nt(g, value) for value in values]
+
+        def row_sum(blocks):
+            first = [block for block in blocks if block.shape == score[0].shape]
+            total = jnp.sum(functools.reduce(jnp.add, first), axis=1, keepdims=True)
+            for block in blocks:
+                if block.shape != score[0].shape:
+                    total += jnp.sum(block, axis=1, keepdims=True)
+            return total
+
+        total = row_sum(expo)
+        inv = 1.0 / total
+        delta = row_sum([e * d for e, d in zip(expo, dprob)]) * inv
+        gq = jnp.zeros((tile, hd), jnp.float32)
+        for e, d, key in zip(expo[tiles + 1 :], dprob[tiles + 1 :], memory[0]):
+            gq += dot_nn((e * (d - delta)).astype(jnp.bfloat16), key)
+        gq = gq * inv
+        for i, chunk in enumerate(chunks):
+            prob = expo[i] * inv
+            dscore = (prob * (dprob[i] - delta)).astype(jnp.bfloat16)
+            gq += dot_nn(dscore, keys[i])
+            if chunk + half * tiles >= 0:
+                owed = dot_tn(dscore, q), dot_tn(prob.astype(jnp.bfloat16), g)
+                old = sums.get(chunk)
+                sums[chunk] = owed if old is None else (old[0] + owed[0], old[1] + owed[1])
+        gq_ref[2 * this : 2 * this + 2] = (gq * scale).astype(gq_ref.dtype).reshape(2, rows, hd)
         if half == 0:
-            k_all[:WINDOW] = near_ref[: reach // 2, 0, near:].reshape(WINDOW, hd)
-            v_all[:WINDOW] = near_ref[: reach // 2, 1, near:].reshape(WINDOW, hd)
-        else:
-            k_all[:WINDOW] = ev_ref[:reach, 1].reshape(WINDOW, hd)
-            v_all[:WINDOW] = ev_ref[:reach, 2].reshape(WINDOW, hd)
-        own = slice(half * reach, (half + 1) * reach)
-        k_all[WINDOW:] = ev_ref[own, 1].reshape(WINDOW, hd)
-        v_all[WINDOW:] = ev_ref[own, 2].reshape(WINDOW, hd)
-        gk_ref[...] = jnp.zeros_like(gk_ref)
-        gv_ref[...] = jnp.zeros_like(gv_ref)
-        for part, all_ref in enumerate((mk_all, mv_all)):
-            first = near_ref.shape[0] * near
-            all_ref[:first] = near_ref[:, part, :near].reshape(first, hd)
-            all_ref[first:] = far_ref[part]
-
-    span = WINDOW + TILE
-    here = pl.ds(half * reach + step * blocks_per_tile, blocks_per_tile)
-    q = ev_ref[here, 0].reshape(TILE, hd)
-    g = ev_ref[here, 3].reshape(TILE, hd)
-    start = pl.multiple_of(step * TILE, TILE)
-    kw = k_all[pl.ds(start, span)]
-    vw = v_all[pl.ds(start, span)]
-    mk = mk_all[...]
-    mv = mv_all[...]
-
-    qpos = base + start + lax.broadcasted_iota(jnp.int32, (TILE, span), 0)
-    kpos = base + start - WINDOW + lax.broadcasted_iota(jnp.int32, (TILE, span), 1)
-    allowed = (
-        (kpos <= qpos)
-        & (qpos - kpos < WINDOW)
-        & (kpos >= 0)
-        & ((kpos < length) | (kpos == qpos))
-    )
-    per_source = near // 2
-    memory = mk.shape[0]
-    which = lax.rem(lax.broadcasted_iota(jnp.int32, (1, memory), 1), per_source) // depth
-    live = which < count
-
-    sw = jnp.where(allowed, dot_nt(q, kw), NEG)
-    sm = jnp.where(live, dot_nt(q, mk), NEG)
-    top = jnp.maximum(
-        jnp.max(sw, axis=1, keepdims=True), jnp.max(sm, axis=1, keepdims=True)
-    )
-    ew = jnp.exp2((sw - top) * slope)
-    em = jnp.exp2((sm - top) * slope)
-    dw = dot_nt(g, vw)
-    dm = dot_nt(g, mv)
-    total = jnp.sum(ew, axis=1, keepdims=True) + jnp.sum(em, axis=1, keepdims=True)
-    inv = 1.0 / total
-    delta = (
-        jnp.sum(ew * dw, axis=1, keepdims=True) + jnp.sum(em * dm, axis=1, keepdims=True)
-    ) * inv
-    pw = ew * inv
-    dsw = (pw * (dw - delta)).astype(jnp.bfloat16)
-    dsm = (em * (dm - delta)).astype(jnp.bfloat16)
-    gq = (dot_nn(dsw, kw) + dot_nn(dsm, mk) * inv) * scale
-    gq_ref[pl.ds(step * blocks_per_tile, blocks_per_tile)] = gq.astype(gq_ref.dtype).reshape(
-        blocks_per_tile, rows, hd
-    )
-    gk_ref[pl.ds(start, span)] += dot_tn(dsw, q) * scale
-    gv_ref[pl.ds(start, span)] += dot_tn(pw.astype(jnp.bfloat16), g)
+            lane = lax.broadcasted_iota(jnp.int32, (tile, hd), 1)
+            both = jnp.where(lane == 0, top * slope + jnp.log2(total), delta)
+            refs[3][this] = both.T[:8]
+    for i, chunk in enumerate(sorted(sums)):
+        gk_ref[i * tile : (i + 1) * tile] = sums[chunk][0] * scale
+        gv_ref[i * tile : (i + 1) * tile] = sums[chunk][1]
+
+
+def attend(scale, depth, half, seq_lengths, mem_counts, after, events, near, far):
+    _, _, rows, hd = events.shape
+    keys = WINDOW + (near.shape[2] - 2 * rows) * (near.shape[0] + len(far))
+    smem = pl.BlockSpec(memory_space=pltpu.SMEM)
+    vmem = pl.BlockSpec(memory_space=pltpu.VMEM)
+    outs = [((WINDOW // rows, rows, hd), jnp.bfloat16)]
+    outs += [(((1 + half) * WINDOW, hd), jnp.float32)] * 2
     if half == 0:
-        stats_ref = refs[0]
-        lane = lax.broadcasted_iota(jnp.int32, (TILE, hd), 1)
-        both = jnp.where(lane == 0, top * slope + jnp.log2(total), delta)
-        stats_ref[step] = both.T[:8]
-
-
-def attend(scale, depth, half, seq_lengths, mem_counts, events, near, far):
-    _, _, rows, hd = events.shape
-    reach = WINDOW // rows
-    memories = (near.shape[2] - 2 * rows) * near.shape[0] + far.shape[1]
-    keys = WINDOW + memories
-    whole = lambda shape: pl.BlockSpec(shape, lambda t: (0,) * len(shape))
-    smem = pl.BlockSpec(memory_space=pltpu.SMEM)
-    outs = [((reach, rows, hd), jnp.bfloat16)] + [((2 * WINDOW, hd), jnp.float32)] * 2
-    if half == 0:
-        outs.append(((WINDOW // TILE, 8, TILE), jnp.float32))
-    return call(
-        functools.partial(attend_body, scale, depth, half),
-        grid=(WINDOW // TILE,),
-        in_specs=[smem] * 2 + [whole(array.shape) for array in (events, near, far)],
-        out_specs=[whole(shape) for shape, _ in outs],
+        outs.append(((WINDOW // (2 * rows), 8, 2 * rows), jnp.float32))
+    return call(
+        functools.partial(attend_body, scale, depth, half, len(far)),
+        in_specs=[smem] * 2 + [pl.BlockSpec(memory_space=pl.ANY)] + [vmem] * (2 + len(far)),
+        out_specs=[vmem] * len(outs),
         out_shape=[jax.ShapeDtypeStruct(shape, dtype) for shape, dtype in outs],
-        scratch_shapes=[pltpu.VMEM((2 * WINDOW, hd), jnp.bfloat16)] * 2
-        + [pltpu.VMEM((memories, hd), jnp.bfloat16)] * 2,
         cost_estimate=pl.CostEstimate(
             flops=10 * WINDOW * keys * hd,
             bytes_accessed=4 * keys * hd,
             transcendentals=WINDOW * keys,
         ),
-    )(seq_lengths, mem_counts, events, near, far)
+    )(seq_lengths, mem_counts, after, events, near, *far)
 
 
 def finish_body(scale, length_ref, ev_ref, near_ref, stats_ref, *refs):
@@ -418,8 +414,8 @@
     first, last = slice(0, early), slice(early, group)
     out_ref[first, 0] = gq0[...]
     out_ref[last, 0] = gq1[...]
-    put(first, 1, gk0[WINDOW:] + gk1[:WINDOW])
-    put(first, 2, gv0[WINDOW:] + gv1[:WINDOW])
+    put(first, 1, gk0[...] + gk1[:WINDOW])
+    put(first, 2, gv0[...] + gv1[:WINDOW])
     k = ev_ref[early:, 1].reshape(WINDOW, hd)
     v = ev_ref[early:, 2].reshape(WINDOW, hd)
     gk = jnp.zeros((WINDOW, hd), jnp.float32)
@@ -522,15 +518,15 @@
                 (i, ((i // H + around) * H) % seq + ((i % H) ^ (2 * step))) for i in range(seq)
             ]
             far.append(lax.ppermute(piece, "seq", pairs))
-    far = gather_far(far)
-    near = near_pieces(held, depth, block_slots, block_lists, edges, sources, events, pieces[0])
+    after = arrived(far)
+    near = near_pieces(held, depth, block_slots, block_lists, edges, sources, pieces[0])
     parities = [group[parity::2] for group in groups for parity in range(2)]
     near = swap(near, axis_index_groups=parities)
 
     part = functools.partial(attend, scale, depth)
-    *first, stats = part(0, seq_lengths, mem_counts, events, near, far)
+    *first, stats = part(0, seq_lengths, mem_counts, after, events, near, far)
     stats = lax.ppermute(stats, "seq", [(i + H, i) for i in range(seq - H)])
-    second = part(1, seq_lengths, mem_counts, events, near, far)
+    second = part(1, seq_lengths, mem_counts, after, events, near, far)
     out = finish(scale, seq_lengths, events, near, stats, [*first, *second])
     return tuple(join_heads(swap(out, axis_index_groups=groups)))
 

time: 90.9 us -> 87.2 us (0.959)
  local copies, waits for them, and re-layouts: 2.45 us -> 0.62 us
  Pallas kernels: 24.3 us -> 22.9 us
    ppermute x4, waiting for transfers between devices: 6.69 us -> 9.45 us  [on_device(): far.append(lax.ppermute(piece, 'seq', pairs))]
    all_to_all x1, waiting for transfers between devices: 5.61 us -> 2.86 us  [on_device(): events = swap(split_heads(seq_lengths, arrays), axis_index_groups=groups)]
    unnamed x14 -> x10, local copies, waits for them, and re-layouts: 2.45 us -> 0.62 us
    pallas_call x3, Pallas kernels: 10.8 us -> 9.48 us  [the longest x2 9.48 us: attend(): call(functools.partial(attend_body, scale, depth, half, len(far)), in_spe...]
    all_to_all x1, waiting for transfers between devices: 8.42 us -> 7.44 us  [on_device(): near = swap(near, axis_index_groups=parities)]
  transfers between devices with their start and end apart: 12 -> 12, of which waited for: 4 -> 6; matrix products, arithmetic and copies ran while one was open for 0% -> 0% of each run, Pallas kernels for 14% -> 14%
where the time goes in v3:
time: 87.2 us; the launch traced here: 86.7 us
  starting transfers between devices  28.1 us (32%)
  Pallas kernels  22.9 us (26%)
  waiting for transfers between devices  20 us (23%)
  blocking collectives  14.4 us (17%)
    all_to_all x1, blocking collectives, on_device(): return tuple(join_heads(swap(out, axis_index_groups=groups)))  14.4 us
    pallas_call x2, Pallas kernels, attend(): call(functools.partial(attend_body, scale, depth, half, len(far)), in_spe...  9.48 us
    ppermute x4, waiting for transfers between devices, on_device(): far.append(lax.ppermute(piece, 'seq', pairs))  9.45 us
    ppermute x4, starting transfers between devices, on_device(): far.append(lax.ppermute(piece, 'seq', pairs))  9.31 us
    all_to_all x1, waiting for transfers between devices, on_device(): near = swap(near, axis_index_groups=parities)  7.44 us
    all_to_all x1, starting transfers between devices, on_device(): events = swap(split_heads(seq_lengths, arrays), axis_index_groups=groups)  7.27 us
    all_to_all x1, starting transfers between devices, on_device(): near = swap(near, axis_index_groups=parities)  4.11 us
    pallas_call x1, Pallas kernels, pack(): call(functools.partial(pack_body, users), limit=VMEM_WHOLE, in_specs=[sme...  3.54 us
  transfers between devices with their start and end apart: 12, of which 6 were waited for; matrix products, arithmetic and copies ran while one was open for 0% of the time, Pallas kernels for 14%

profile of v3, /device:TPU:0, one launch (start us, length us, event | category | flops | bytes accessed | tf_op | source)
XLA Modules:
  0.0 86.7 jit_solution(11630206937724235246)
XLA Ops:
  0.6 3.5 %shard_map.122 = (bf16[4,2,128,128]{3,2,1,0:T(8,128)(2,1)}, bf16[4,2,128,128]{3,2,1,0:T(8,128)(2,1)}, bf16[4,2,128,128]{3,2,1,0:T(8,128)(2,1)}, bf16[4,2,128,128...) custom-call(s32[2]{0:T(128)} %length_ref.9, s32[16]{0:T(128)} %slots_ref.5, ...), custom_call_target="tpu_custom_call" | custom-call | tf_op jit(solution)/shard_map/pallas_call | solution.py:131
  4.2 3.0 %collective-permute-start = (bf16[4,2,128,128]{3,2,1,0:T(8,128)(2,1)}, bf16[4,2,128,128]{3,2,1,0:T(8,128)(2,1)}, u32[]{:S(2)}, u32[]{:S(2)}) collective-permute-start(bf16[4,2,128,128]{3,2,1,0:T(8,128)(2,1)} %get-tuple-element.20), channel_id=1, source_target_pairs={{0,16},{1,17},{2,18},{3,19},{4,20},{5,21},{6,22},{7,23},{8,24},{9,... | collective-permute-start | bytes 786440 | tf_op jit(solution)/shard_map/ppermute | solution.py:502
  7.2 0.0 collective-permute-start.1
  7.2 0.2 collective-permute-start.2
  7.4 1.4 %collective-permute-start.3 = (bf16[4,2,128,128]{3,2,1,0:T(8,128)(2,1)}, bf16[4,2,128,128]{3,2,1,0:T(8,128)(2,1)}, u32[]{:S(2)}, u32[]{:S(2)}) collective-permute-start(bf16[4,2,128,128]{3,2,1,0:T(8,128)(2,1)} %get-tuple-element.24), channel_id=1, source_target_pairs={{4,8},{5,9},{6,10},{7,11},{8,4},{9,5},{10,6},{11,7},{20,24},{21,25... | collective-permute-start | bytes 786440 | tf_op jit(solution)/shard_map/ppermute | solution.py:506
  8.7 1.3 %collective-permute-start.4 = (bf16[4,2,128,128]{3,2,1,0:T(8,128)(2,1)}, bf16[4,2,128,128]{3,2,1,0:T(8,128)(2,1)}, u32[]{:S(2)}, u32[]{:S(2)}) collective-permute-start(bf16[4,2,128,128]{3,2,1,0:T(8,128)(2,1)} %get-tuple-element.25), channel_id=1, source_target_pairs={{4,9},{5,8},{6,11},{7,10},{8,5},{9,4},{10,7},{11,6},{20,25},{21,24... | collective-permute-start | bytes 786440 | tf_op jit(solution)/shard_map/ppermute | solution.py:506
  10.1 2.9 %shard_map.121 = bf16[8,4,128,128]{3,2,1,0:T(8,128)(2,1)} custom-call(s32[2]{0:T(128)} %length_ref.9, bf16[1,128,1024]{2,1,0:T(8,128)(2,1)} %refs_0_.3, bf16[1,128,1024]{2,1,0:T(8,128)(2,1)} %refs_1_.3, bf16[1,128,1024]{2,1,0:T(8,128)(2,1)} %refs_2_.3, bf16[1,128,1024]{2,1,0:T(8,128)(2,1)} %refs_3_.3), custom_call_target="tpu_custom_call" | custom-call | tf_op jit(solution)/shard_map/pallas_call | solution.py:170
  13.0 0.0 copy-start
  13.0 7.3 %all-to-all-start = ((bf16[8,4,128,128]{3,2,1,0:T(8,128)(2,1)}), bf16[8,4,128,128]{3,2,1,0:T(8,128)(2,1)S(1)}, u32[]{:S(2)}, u32[]{:S(2)}) async-start(bf16[8,4,128,128]{3,2,1,0:T(8,128)(2,1)} %shard_map.121), calls=%async_computation | async-start | bytes 2097152 | tf_op jit(solution)/shard_map/all_to_all | solution.py:510
  20.3 0.0 copy-start.3
  20.3 0.0 collective-permute-done.refs_0_.refs_4_
  20.3 0.0 collective-permute-done.2.refs_3_
  20.4 0.0 collective-permute-done.3.refs_4_.refs_0_
  20.4 0.6 copy-done.2
  21.0 1.7 %shard_map.123 = (bf16[2,2,128,128]{3,2,1,0:T(8,128)(2,1)S(1)}, bf16[2,2,128,128]{3,2,1,0:T(8,128)(2,1)S(1)}, bf16[2,2,128,128]{3,2,1,0:T(8,128)(2,1)S(1)}, bf16[2,2,128,128]{3,2,1,0:T(8,128)(2,1)S(1)}) custom-call(s32[16]{0:T(128)S(1)} %copy-done.3, s32[2,4]{1,0:T(2,128)S(1)} %copy-done.2, bf16[4,2,128,128]{3,2,1,0:T(8,128)(2,1)} %collective-permute-done.refs_0_.refs_4_, ...), custom_call_target="tpu_custom_call" | custom-call | flops 99999997952 | tf_op jit(solution)/shard_map/pallas_call | solution.py:213
  22.7 5.5 %collective-permute-start.6 = (bf16[2,2,128,128]{3,2,1,0:T(8,128)(2,1)S(1)}, bf16[2,2,128,128]{3,2,1,0:T(8,128)(2,1)S(1)}, u32[]{:S(2)}, u32[]{:S(2)}) collective-permute-start(bf16[2,2,128,128]{3,2,1,0:T(8,128)(2,1)S(1)} %get-tuple-element.27), channel_id=1, source_target_pairs={{0,10},{1,11},{2,8},{3,9},{4,14},{5,15},{6,12},{7,13},{8,2},{9,3},... | collective-permute-start | bytes 393224 | tf_op jit(solution)/shard_map/ppermute | solution.py:520
  28.2 1.4 %collective-permute-start.7 = (bf16[2,2,128,128]{3,2,1,0:T(8,128)(2,1)S(1)}, bf16[2,2,128,128]{3,2,1,0:T(8,128)(2,1)S(1)}, u32[]{:S(2)}, u32[]{:S(2)}) collective-permute-start(bf16[2,2,128,128]{3,2,1,0:T(8,128)(2,1)S(1)} %get-tuple-element.28), channel_id=1, source_target_pairs={{0,12},{1,13},{2,14},{3,15},{4,8},{5,9},{6,10},{7,11},{8,4},{9,5},... | collective-permute-start | bytes 393224 | tf_op jit(solution)/shard_map/ppermute | solution.py:520
  29.6 2.4 %collective-permute-start.8 = (bf16[2,2,128,128]{3,2,1,0:T(8,128)(2,1)S(1)}, bf16[2,2,128,128]{3,2,1,0:T(8,128)(2,1)S(1)}, u32[]{:S(2)}, u32[]{:S(2)}) collective-permute-start(bf16[2,2,128,128]{3,2,1,0:T(8,128)(2,1)S(1)} %get-tuple-element.29), channel_id=1, source_target_pairs={{0,14},{1,15},{2,12},{3,13},{4,10},{5,11},{6,8},{7,9},{8,6},{9,7},... | collective-permute-start | bytes 393224 | tf_op jit(solution)/shard_map/ppermute | solution.py:520
  32.0 2.8 %shard_map.124 = bf16[4,2,512,128]{3,2,1,0:T(8,128)(2,1)} custom-call(s32[16]{0:T(128)S(1)} %copy-done.3, s32[2,4]{1,0:T(2,128)S(1)} %copy-done.2, bf16[2,2,128,128]{3,2,1,0:T(8,128)(2,1)S(1)} %get-tuple-element.26._, bf16[4,2,128,128]{3,2,1,0:T(8,128)(2,1)} %collective-permute-done.3.refs_4_.refs_0_, ...), custom_call_target="tpu_custom_call" | custom-call | tf_op jit(solution)/shard_map/pallas_call | solution.py:248
  34.7 2.9 %all-to-all-done.ev_ref = bf16[8,4,128,128]{3,2,1,0:T(8,128)(2,1)S(1)} async-done(((bf16[8,4,128,128]{3,2,1,0:T(8,128)(2,1)}), bf16[8,4,128,128]{3,2,1,0:T(8,128)(2,1)S(1)}, u32[]{:S(2)}, u32[]{:S(2)}) %all-to-all-start) | async-done | bytes 1048608 | tf_op jit(solution)/shard_map/all_to_all | solution.py:510
  37.6 4.1 %all-to-all-start.1 = ((bf16[4,2,512,128]{3,2,1,0:T(8,128)(2,1)}), bf16[4,2,512,128]{3,2,1,0:T(8,128)(2,1)S(1)}, u32[]{:S(2)}, u32[]{:S(2)}) async-start(bf16[4,2,512,128]{3,2,1,0:T(8,128)(2,1)} %shard_map.124), calls=%async_computation.1 | async-start | bytes 2097152 | tf_op jit(solution)/shard_map/all_to_all | solution.py:524
  41.7 0.5 collective-permute-done.7.refs_2_
  42.2 3.8 %collective-permute-done.8.refs_3_ = bf16[2,2,128,128]{3,2,1,0:T(8,128)(2,1)S(1)} collective-permute-done((bf16[2,2,128,128]{3,2,1,0:T(8,128)(2,1)S(1)}, bf16[2,2,128,128]{3,2,1,0:T(8,128)(2,1)S(1)}, u32[]{:S(2)}, u32[]{:S(2)}) %collective-permute-start.8) | collective-permute-done | bytes 131104 | tf_op jit(solution)/shard_map/ppermute | solution.py:520
  46.0 5.2 %collective-permute-done.5.refs_0_ = bf16[2,2,128,128]{3,2,1,0:T(8,128)(2,1)S(1)} collective-permute-done((bf16[2,2,128,128]{3,2,1,0:T(8,128)(2,1)S(1)}, bf16[2,2,128,128]{3,2,1,0:T(8,128)(2,1)S(1)}, u32[]{:S(2)}, u32[]{:S(2)}) %collective-permute-start.5) | collective-permute-done | bytes 131104 | tf_op jit(solution)/shard_map/ppermute | solution.py:520
  51.2 7.4 %all-to-all-done.1.near_ref = bf16[4,2,512,128]{3,2,1,0:T(8,128)(2,1)S(1)} async-done(((bf16[4,2,512,128]{3,2,1,0:T(8,128)(2,1)}), bf16[4,2,512,128]{3,2,1,0:T(8,128)(2,1)S(1)}, u32[]{:S(2)}, u32[]{:S(2)}) %all-to-all-start.1) | async-done | bytes 1048608 | tf_op jit(solution)/shard_map/all_to_all | solution.py:524
  58.6 4.6 %shard_map.126 = (bf16[4,128,128]{2,1,0:T(8,128)(2,1)S(1)}, f32[512,128]{1,0:T(8,128)S(1)}, f32[512,128]{1,0:T(8,128)S(1)}, f32[2,8,256]{2,1,0:T(8,128)S(1)}) custom-call(s32[2]{0:T(128)S(1)} %copy-done.1, s32[2]{0:T(128)S(1)} %copy-done.4, f32[8,128]{1,0:T(8,128)S(1)} %shard_map.125._, bf16[8,4,128,128]{3,2,1,0:T(8,128)(2,1)S(1)} %all-to-all-done.ev_ref, ...), custom_call_target="tpu_custom_call" | custom-call | flops 1677721600 | bytes 1310720 | tf_op jit(solution)/shard_map/pallas_call | solution.py:385
  63.3 1.5 %collective-permute-start.9 = (f32[2,8,256]{2,1,0:T(8,128)S(1)}, f32[2,8,256]{2,1,0:T(8,128)S(1)}, u32[]{:S(2)}, u32[]{:S(2)}) collective-permute-start(f32[2,8,256]{2,1,0:T(8,128)S(1)} %get-tuple-element.30), channel_id=1, source_target_pairs={{8,0},{9,1},{10,2},{11,3},{12,4},{13,5},{14,6},{15,7},{24,16},{25,... | collective-permute-start | bytes 49160 | tf_op jit(solution)/shard_map/ppermute | solution.py:528
  64.7 4.8 %shard_map.127 = (bf16[4,128,128]{2,1,0:T(8,128)(2,1)S(1)}, f32[1024,128]{1,0:T(8,128)S(1)}, f32[1024,128]{1,0:T(8,128)S(1)}) custom-call(s32[2]{0:T(128)S(1)} %copy-done.1, s32[2]{0:T(128)S(1)} %copy-done.4, f32[8,128]{1,0:T(8,128)S(1)} %shard_map.125._, bf16[8,4,128,128]{3,2,1,0:T(8,128)(2,1)S(1)} %all-to-all-done.ev_ref, ...), custom_call_target="tpu_custom_call" | custom-call | flops 1677721600 | bytes 1310720 | tf_op jit(solution)/shard_map/pallas_call | solution.py:385
  69.6 0.2 collective-permute-done.9.stats_ref
  69.8 1.4 %shard_map.128 = bf16[8,3,128,128]{3,2,1,0:T(8,128)(2,1)S(1)} custom-call(s32[2]{0:T(128)S(1)} %copy-done.1, bf16[8,4,128,128]{3,2,1,0:T(8,128)(2,1)S(1)} %all-to-all-done.ev_ref, bf16[4,2,512,128]{3,2,1,0:T(8,128)(2,1)S(1)} %all-to-all-done.1.near_ref, f32[2,8,256]{2,1,0:T(8,128)S(1)} %collective-permute-done.9.stats_ref, ...), custom_call_target="tpu_custom_call" | custom-call | tf_op jit(solution)/shard_map/pallas_call | solution.py:444
  71.2 14.4 %all_to_all.15.in_ref = bf16[8,3,128,128]{3,2,1,0:T(8,128)(2,1)S(1)} all-to-all(bf16[8,3,128,128]{3,2,1,0:T(8,128)(2,1)S(1)} %shard_map.128), channel_id=1, replica_groups={{0,1,2,3,4,5,6,7},{8,9,10,11,12,13,14,15},{16,17,18,19,20,21,22,23},{24..., dimensions={0} | all-to-all | bytes 1572864 | tf_op jit(solution)/shard_map/all_to_all | solution.py:531
  85.6 1.1 %shard_map.129 = (bf16[1,128,1024]{2,1,0:T(8,128)(2,1)}, bf16[1,128,1024]{2,1,0:T(8,128)(2,1)}, bf16[1,128,1024]{2,1,0:T(8,128)(2,1)}) custom-call(bf16[8,3,128,128]{3,2,1,0:T(8,128)(2,1)S(1)} %all_to_all.15.in_ref), custom_call_target="tpu_custom_call" | custom-call | tf_op jit(solution)/shard_map/pallas_call | solution.py:462
  (12 shorter events, 0.0 us)
Async XLA Ops:
  4.2 16.1 %collective-permute-start = (bf16[4,2,128,128]{3,2,1,0:T(8,128)(2,1)}, bf16[4,2,128,128]{3,2,1,0:T(8,128)(2,1)}, u32[]{:S(2)}, u32[]{:S(2)}) collective-permute-start(bf16[4,2,128,128]{3,2,1,0:T(8,128)(2,1)} %get-tuple-element.20), channel_id=1, source_target_pairs={{0,16},{1,17},{2,18},{3,19},{4,20},{5,21},{6,22},{7,23},{8,24},{9,... | collective-permute-start | bytes 786440 | tf_op jit(solution)/shard_map/ppermute | solution.py:502
  7.2 13.2 %collective-permute-start.1 = (bf16[4,2,128,128]{3,2,1,0:T(8,128)(2,1)}, bf16[4,2,128,128]{3,2,1,0:T(8,128)(2,1)}, u32[]{:S(2)}, u32[]{:S(2)}) collective-permute-start(bf16[4,2,128,128]{3,2,1,0:T(8,128)(2,1)} %get-tuple-element.21), channel_id=1, source_target_pairs={{0,17},{1,16},{2,19},{3,18},{4,21},{5,20},{6,23},{7,22},{8,25},{9,... | collective-permute-start | bytes 786440 | tf_op jit(solution)/shard_map/ppermute | solution.py:502
  7.2 13.2 %collective-permute-start.2 = (bf16[4,2,128,128]{3,2,1,0:T(8,128)(2,1)}, bf16[4,2,128,128]{3,2,1,0:T(8,128)(2,1)}, u32[]{:S(2)}, u32[]{:S(2)}) collective-permute-start(bf16[4,2,128,128]{3,2,1,0:T(8,128)(2,1)} %get-tuple-element.23), channel_id=1, source_target_pairs={{0,1},{1,0},{2,3},{3,2},{4,5},{5,4},{6,7},{7,6},{8,9},{9,8},{10,11... | collective-permute-start | bytes 786440 | tf_op jit(solution)/shard_map/ppermute | solution.py:495
  7.4 13.0 %collective-permute-start.3 = (bf16[4,2,128,128]{3,2,1,0:T(8,128)(2,1)}, bf16[4,2,128,128]{3,2,1,0:T(8,128)(2,1)}, u32[]{:S(2)}, u32[]{:S(2)}) collective-permute-start(bf16[4,2,128,128]{3,2,1,0:T(8,128)(2,1)} %get-tuple-element.24), channel_id=1, source_target_pairs={{4,8},{5,9},{6,10},{7,11},{8,4},{9,5},{10,6},{11,7},{20,24},{21,25... | collective-permute-start | bytes 786440 | tf_op jit(solution)/shard_map/ppermute | solution.py:506
  8.7 11.6 %collective-permute-start.4 = (bf16[4,2,128,128]{3,2,1,0:T(8,128)(2,1)}, bf16[4,2,128,128]{3,2,1,0:T(8,128)(2,1)}, u32[]{:S(2)}, u32[]{:S(2)}) collective-permute-start(bf16[4,2,128,128]{3,2,1,0:T(8,128)(2,1)} %get-tuple-element.25), channel_id=1, source_target_pairs={{4,9},{5,8},{6,11},{7,10},{8,5},{9,4},{10,7},{11,6},{20,25},{21,24... | collective-permute-start | bytes 786440 | tf_op jit(solution)/shard_map/ppermute | solution.py:506
  13.0 7.4 %copy-start = (bf16[4,2,128,128]{3,2,1,0:T(8,128)(2,1)S(1)}, bf16[4,2,128,128]{3,2,1,0:T(8,128)(2,1)}, u32[]{:S(2)}) copy-start(bf16[4,2,128,128]{3,2,1,0:T(8,128)(2,1)} %get-tuple-element.22.refs_2_) | copy-start | bytes 786436
  13.0 24.5 %all-to-all-start = ((bf16[8,4,128,128]{3,2,1,0:T(8,128)(2,1)}), bf16[8,4,128,128]{3,2,1,0:T(8,128)(2,1)S(1)}, u32[]{:S(2)}, u32[]{:S(2)}) async-start(bf16[8,4,128,128]{3,2,1,0:T(8,128)(2,1)} %shard_map.121), calls=%async_computation | async-start | bytes 2097152 | tf_op jit(solution)/shard_map/all_to_all | solution.py:510
  20.3 0.7 copy-start.2
  20.3 0.7 copy-start.3
  22.7 19.1 %collective-permute-start.6 = (bf16[2,2,128,128]{3,2,1,0:T(8,128)(2,1)S(1)}, bf16[2,2,128,128]{3,2,1,0:T(8,128)(2,1)S(1)}, u32[]{:S(2)}, u32[]{:S(2)}) collective-permute-start(bf16[2,2,128,128]{3,2,1,0:T(8,128)(2,1)S(1)} %get-tuple-element.27), channel_id=1, source_target_pairs={{0,10},{1,11},{2,8},{3,9},{4,14},{5,15},{6,12},{7,13},{8,2},{9,3},... | collective-permute-start | bytes 393224 | tf_op jit(solution)/shard_map/ppermute | solution.py:520
  28.2 14.0 %collective-permute-start.7 = (bf16[2,2,128,128]{3,2,1,0:T(8,128)(2,1)S(1)}, bf16[2,2,128,128]{3,2,1,0:T(8,128)(2,1)S(1)}, u32[]{:S(2)}, u32[]{:S(2)}) collective-permute-start(bf16[2,2,128,128]{3,2,1,0:T(8,128)(2,1)S(1)} %get-tuple-element.28), channel_id=1, source_target_pairs={{0,12},{1,13},{2,14},{3,15},{4,8},{5,9},{6,10},{7,11},{8,4},{9,5},... | collective-permute-start | bytes 393224 | tf_op jit(solution)/shard_map/ppermute | solution.py:520
  29.6 16.4 %collective-permute-start.8 = (bf16[2,2,128,128]{3,2,1,0:T(8,128)(2,1)S(1)}, bf16[2,2,128,128]{3,2,1,0:T(8,128)(2,1)S(1)}, u32[]{:S(2)}, u32[]{:S(2)}) collective-permute-start(bf16[2,2,128,128]{3,2,1,0:T(8,128)(2,1)S(1)} %get-tuple-element.29), channel_id=1, source_target_pairs={{0,14},{1,15},{2,12},{3,13},{4,10},{5,11},{6,8},{7,9},{8,6},{9,7},... | collective-permute-start | bytes 393224 | tf_op jit(solution)/shard_map/ppermute | solution.py:520
  32.0 19.2 %collective-permute-start.5 = (bf16[2,2,128,128]{3,2,1,0:T(8,128)(2,1)S(1)}, bf16[2,2,128,128]{3,2,1,0:T(8,128)(2,1)S(1)}, u32[]{:S(2)}, u32[]{:S(2)}) collective-permute-start(bf16[2,2,128,128]{3,2,1,0:T(8,128)(2,1)S(1)} %get-tuple-element.26._), channel_id=1, source_target_pairs={{0,8},{1,9},{2,10},{3,11},{4,12},{5,13},{6,14},{7,15},{8,0},{9,1},... | collective-permute-start | bytes 393224 | tf_op jit(solution)/shard_map/ppermute | solution.py:520
  37.6 21.0 %all-to-all-start.1 = ((bf16[4,2,512,128]{3,2,1,0:T(8,128)(2,1)}), bf16[4,2,512,128]{3,2,1,0:T(8,128)(2,1)S(1)}, u32[]{:S(2)}, u32[]{:S(2)}) async-start(bf16[4,2,512,128]{3,2,1,0:T(8,128)(2,1)} %shard_map.124), calls=%async_computation.1 | async-start | bytes 2097152 | tf_op jit(solution)/shard_map/all_to_all | solution.py:524
  41.7 16.9 %copy-start.1 = (s32[2]{0:T(128)S(1)}, s32[2]{0:T(128)}, u32[]{:S(2)}) copy-start(s32[2]{0:T(128)} %length_ref.9) | copy-start | bytes 28
  41.7 16.9 %copy-start.4 = (s32[2]{0:T(128)S(1)}, s32[2]{0:T(128)}, u32[]{:S(2)}) copy-start(s32[2]{0:T(128)} %count_ref.3) | copy-start | bytes 28
  63.3 6.5 %collective-permute-start.9 = (f32[2,8,256]{2,1,0:T(8,128)S(1)}, f32[2,8,256]{2,1,0:T(8,128)S(1)}, u32[]{:S(2)}, u32[]{:S(2)}) collective-permute-start(f32[2,8,256]{2,1,0:T(8,128)S(1)} %get-tuple-element.30), channel_id=1, source_target_pairs={{8,0},{9,1},{10,2},{11,3},{12,4},{13,5},{14,6},{15,7},{24,16},{25,... | collective-permute-start | bytes 49160 | tf_op jit(solution)/shard_map/ppermute | solution.py:528

commit v4 on v3

--- a/solution.py
+++ b/solution.py
@@ -70,8 +70,14 @@
 
 def pack_body(users, length_ref, slots_ref, lists_ref, *refs):
     (q_ref, k_ref, v_ref, g_ref, mk_ref, mv_ref), refs = refs[:6], refs[6:]
-    same, other = refs[: users + 1], refs[users + 1 : 2 * users + 2]
-    buffer, sems, edge, edge_sems = refs[2 * users + 2 :]
+    outs, refs = refs[: 2 * users + 2], refs[2 * users + 2 :]
+    buffer, sems, edge, edge_sems, out_sems = refs[:5]
+    cuts = refs[5:]
+    same, other = cuts[: users + 1], cuts[users + 1 :]
+    writes = [
+        pltpu.make_async_copy(cut, out, out_sems.at[i])
+        for i, (cut, out) in enumerate(zip(cuts, outs))
+    ]
     user, shard = lax.axis_index("dp"), lax.axis_index("seq")
     _, blocks, parts, depth, _ = buffer.shape
     rows, width = edge.shape[1:]
@@ -107,6 +113,8 @@
             for part in range(parts):
                 where = (part, slice(block * depth, (block + 1) * depth))
                 split_parity(buffer[step, block, part], where, same[step], other[step])
+        writes[step].start()
+        writes[users + 1 + step].start()
     live = jnp.where(early, length_ref[user] - shard * rows, rows)
     for part in range(2):
         pltpu.make_async_copy(q_ref.at[0], edge.at[part], edge_sems.at[part]).wait()
@@ -116,6 +124,10 @@
             value = jnp.where(position < live, value.astype(jnp.float32), 0.0)
             value = value.astype(edge.dtype)
         split_parity(value, (part,), same[users], other[users])
+    writes[users].start()
+    writes[2 * users + 1].start()
+    for write in writes:
+        write.wait()
 
 
 def pack(users, seq_lengths, block_slots, block_lists, events, mem_keys, mem_values):
@@ -132,19 +144,21 @@
         functools.partial(pack_body, users),
         limit=VMEM_WHOLE,
         in_specs=[smem] * 3 + [hbm] * 6,
-        out_specs=[pl.BlockSpec(memory_space=pltpu.VMEM)] * len(outs),
+        out_specs=[hbm] * len(outs),
         out_shape=outs,
         scratch_shapes=[
             pltpu.VMEM((users, blocks, 2, depth, width), dtype),
             pltpu.SemaphoreType.DMA((users, blocks, 2)),
             pltpu.VMEM((2, rows, width), dtype),
             pltpu.SemaphoreType.DMA((2,)),
-        ],
+            pltpu.SemaphoreType.DMA((len(outs),)),
+        ]
+        + [pltpu.VMEM(out.shape, out.dtype) for out in outs],
     )(seq_lengths, block_slots, block_lists, *events, mem_keys, mem_values)
 
 
 def split_body(hd, length_ref, *refs):
-    sources, (out_ref, buffer, sems) = refs[:4], refs[4:]
+    sources, (out_ref, buffer, sems, cut, out_sems) = refs[:4], refs[4:]
     rows = buffer.shape[1]
     copies = [
         pltpu.make_async_copy(source.at[0], buffer.at[part], sems.at[part])
@@ -160,7 +174,10 @@
             block = buffer[part, :, head * hd : (head + 1) * hd]
             if part == 3:
                 block = jnp.where(position < live, block.astype(jnp.float32), 0.0)
-            out_ref[head, part] = block.astype(out_ref.dtype)
+            cut[part, head] = block.astype(cut.dtype)
+        pltpu.make_async_copy(cut.at[part], out_ref.at[:, part], out_sems.at[part]).start()
+    for part in range(len(copies)):
+        pltpu.make_async_copy(cut.at[part], out_ref.at[:, part], out_sems.at[part]).wait()
 
 
 def split_heads(seq_lengths, arrays):
@@ -171,10 +188,12 @@
         functools.partial(split_body, width // H),
         limit=VMEM_WHOLE,
         in_specs=[pl.BlockSpec(memory_space=pltpu.SMEM)] + [hbm] * parts,
-        out_specs=pl.BlockSpec(memory_space=pltpu.VMEM),
+        out_specs=hbm,
         out_shape=jax.ShapeDtypeStruct((H, parts, rows, width // H), arrays[0].dtype),
         scratch_shapes=[
             pltpu.VMEM((parts, rows, width), arrays[0].dtype),
+            pltpu.SemaphoreType.DMA((parts,)),
+            pltpu.VMEM((parts, H, rows, width // H), arrays[0].dtype),
             pltpu.SemaphoreType.DMA((parts,)),
         ],
     )(seq_lengths, *arrays)
@@ -449,21 +468,33 @@
     )(seq_lengths, events, near, stats, *halves)
 
 
-def join_body(in_ref, *outs):
+def join_body(in_ref, *refs):
+    parts = in_ref.shape[1]
+    outs, (whole, sems) = refs[:parts], refs[parts:]
     hd = in_ref.shape[-1]
-    for part, out_ref in enumerate(outs):
+    writes = [
+        pltpu.make_async_copy(whole.at[part], out_ref.at[0], sems.at[part])
+        for part, out_ref in enumerate(outs)
+    ]
+    for part, write in enumerate(writes):
         for head in range(H):
-            out_ref[0, :, head * hd : (head + 1) * hd] = in_ref[head, part]
+            whole[part, :, head * hd : (head + 1) * hd] = in_ref[head, part]
+        write.start()
+    for write in writes:
+        write.wait()
 
 
 def join_heads(pieces):
     heads, parts, rows, hd = pieces.shape
-    vmem = pl.BlockSpec(memory_space=pltpu.VMEM)
     return call(
         join_body,
-        in_specs=[vmem],
-        out_specs=[vmem] * parts,
+        in_specs=[pl.BlockSpec(memory_space=pltpu.VMEM)],
+        out_specs=[pl.BlockSpec(memory_space=pltpu.HBM)] * parts,
         out_shape=[jax.ShapeDtypeStruct((1, rows, heads * hd), pieces.dtype)] * parts,
+        scratch_shapes=[
+            pltpu.VMEM((parts, rows, heads * hd), pieces.dtype),
+            pltpu.SemaphoreType.DMA((parts,)),
+        ],
     )(pieces)
 
 

time: 87.2 us -> 87 us (level)
  no operation moved by 1% of the time
where the time goes in v4:
time: 87 us; the launch traced here: 86.5 us
  starting transfers between devices  27.9 us (32%)
  Pallas kernels  22.4 us (26%)
  waiting for transfers between devices  20.3 us (23%)
  blocking collectives  14.3 us (16%)
  between operations  0.92 us (1%)
    all_to_all x1, blocking collectives, on_device(): return tuple(join_heads(swap(out, axis_index_groups=groups)))  14.3 us
    ppermute x4, waiting for transfers between devices, on_device(): far.append(lax.ppermute(piece, 'seq', pairs))  10.2 us
    ppermute x4, starting transfers between devices, on_device(): far.append(lax.ppermute(piece, 'seq', pairs))  9.51 us
    pallas_call x2, Pallas kernels, attend(): call(functools.partial(attend_body, scale, depth, half, len(far)), in_spe...  9.49 us
    all_to_all x1, starting transfers between devices, on_device(): events = swap(split_heads(seq_lengths, arrays), axis_index_groups=groups)  7.27 us
    all_to_all x1, waiting for transfers between devices, on_device(): near = swap(near, axis_index_groups=parities)  7.1 us
    all_to_all x1, starting transfers between devices, on_device(): near = swap(near, axis_index_groups=parities)  3.72 us
    pallas_call x1, Pallas kernels, pack(): call(functools.partial(pack_body, users), limit=VMEM_WHOLE, in_specs=[sme...  3.37 us
  transfers between devices with their start and end apart: 12, of which 6 were waited for; matrix products, arithmetic and copies ran while one was open for 0% of the time, Pallas kernels for 14%

profile of v4, /device:TPU:0, one launch (start us, length us, event | category | flops | bytes accessed | tf_op | source)
XLA Modules:
  0.0 86.5 jit_solution(13375051673677625580)
XLA Ops:
  0.6 3.4 %shard_map.122 = (bf16[4,2,128,128]{3,2,1,0:T(8,128)(2,1)}, bf16[4,2,128,128]{3,2,1,0:T(8,128)(2,1)}, bf16[4,2,128,128]{3,2,1,0:T(8,128)(2,1)}, bf16[4,2,128,128...) custom-call(s32[2]{0:T(128)} %length_ref.9, s32[16]{0:T(128)} %slots_ref.5, ...), custom_call_target="tpu_custom_call" | custom-call | tf_op jit(solution)/shard_map/pallas_call | solution.py:143
  4.0 3.0 %collective-permute-start = (bf16[4,2,128,128]{3,2,1,0:T(8,128)(2,1)}, bf16[4,2,128,128]{3,2,1,0:T(8,128)(2,1)}, u32[]{:S(2)}, u32[]{:S(2)}) collective-permute-start(bf16[4,2,128,128]{3,2,1,0:T(8,128)(2,1)} %get-tuple-element.20), channel_id=1, source_target_pairs={{0,16},{1,17},{2,18},{3,19},{4,20},{5,21},{6,22},{7,23},{8,24},{9,... | collective-permute-start | bytes 786440 | tf_op jit(solution)/shard_map/ppermute | solution.py:533
  7.0 0.0 collective-permute-start.1
  7.0 0.2 collective-permute-start.2
  7.2 1.4 %collective-permute-start.3 = (bf16[4,2,128,128]{3,2,1,0:T(8,128)(2,1)}, bf16[4,2,128,128]{3,2,1,0:T(8,128)(2,1)}, u32[]{:S(2)}, u32[]{:S(2)}) collective-permute-start(bf16[4,2,128,128]{3,2,1,0:T(8,128)(2,1)} %get-tuple-element.24), channel_id=1, source_target_pairs={{4,8},{5,9},{6,10},{7,11},{8,4},{9,5},{10,6},{11,7},{20,24},{21,25... | collective-permute-start | bytes 786440 | tf_op jit(solution)/shard_map/ppermute | solution.py:537
  8.6 1.3 %collective-permute-start.4 = (bf16[4,2,128,128]{3,2,1,0:T(8,128)(2,1)}, bf16[4,2,128,128]{3,2,1,0:T(8,128)(2,1)}, u32[]{:S(2)}, u32[]{:S(2)}) collective-permute-start(bf16[4,2,128,128]{3,2,1,0:T(8,128)(2,1)} %get-tuple-element.25), channel_id=1, source_target_pairs={{4,9},{5,8},{6,11},{7,10},{8,5},{9,4},{10,7},{11,6},{20,25},{21,24... | collective-permute-start | bytes 786440 | tf_op jit(solution)/shard_map/ppermute | solution.py:537
  9.9 2.7 %shard_map.121 = bf16[8,4,128,128]{3,2,1,0:T(8,128)(2,1)} custom-call(s32[2]{0:T(128)} %length_ref.9, bf16[1,128,1024]{2,1,0:T(8,128)(2,1)} %refs_0_.3, bf16[1,128,1024]{2,1,0:T(8,128)(2,1)} %refs_1_.3, bf16[1,128,1024]{2,1,0:T(8,128)(2,1)} %refs_2_.3, bf16[1,128,1024]{2,1,0:T(8,128)(2,1)} %refs_3_.3), custom_call_target="tpu_custom_call" | custom-call | tf_op jit(solution)/shard_map/pallas_call | solution.py:187
  12.6 0.0 copy-start
  12.7 7.3 %all-to-all-start = ((bf16[8,4,128,128]{3,2,1,0:T(8,128)(2,1)}), bf16[8,4,128,128]{3,2,1,0:T(8,128)(2,1)S(1)}, u32[]{:S(2)}, u32[]{:S(2)}) async-start(bf16[8,4,128,128]{3,2,1,0:T(8,128)(2,1)} %shard_map.121), calls=%async_computation | async-start | bytes 2097152 | tf_op jit(solution)/shard_map/all_to_all | solution.py:541
  19.9 0.0 copy-start.3
  20.0 0.0 collective-permute-done.refs_0_.refs_4_
  20.0 0.0 collective-permute-done.2.refs_3_
  20.0 0.0 collective-permute-done.3.refs_4_.refs_0_
  20.0 0.6 copy-done.2
  20.6 1.7 %shard_map.123 = (bf16[2,2,128,128]{3,2,1,0:T(8,128)(2,1)S(1)}, bf16[2,2,128,128]{3,2,1,0:T(8,128)(2,1)S(1)}, bf16[2,2,128,128]{3,2,1,0:T(8,128)(2,1)S(1)}, bf16[2,2,128,128]{3,2,1,0:T(8,128)(2,1)S(1)}) custom-call(s32[16]{0:T(128)S(1)} %copy-done.3, s32[2,4]{1,0:T(2,128)S(1)} %copy-done.2, bf16[4,2,128,128]{3,2,1,0:T(8,128)(2,1)} %collective-permute-done.refs_0_.refs_4_, ...), custom_call_target="tpu_custom_call" | custom-call | flops 99999997952 | tf_op jit(solution)/shard_map/pallas_call | solution.py:232
  22.3 5.7 %collective-permute-start.6 = (bf16[2,2,128,128]{3,2,1,0:T(8,128)(2,1)S(1)}, bf16[2,2,128,128]{3,2,1,0:T(8,128)(2,1)S(1)}, u32[]{:S(2)}, u32[]{:S(2)}) collective-permute-start(bf16[2,2,128,128]{3,2,1,0:T(8,128)(2,1)S(1)} %get-tuple-element.27), channel_id=1, source_target_pairs={{0,10},{1,11},{2,8},{3,9},{4,14},{5,15},{6,12},{7,13},{8,2},{9,3},... | collective-permute-start | bytes 393224 | tf_op jit(solution)/shard_map/ppermute | solution.py:551
  28.0 1.4 %collective-permute-start.7 = (bf16[2,2,128,128]{3,2,1,0:T(8,128)(2,1)S(1)}, bf16[2,2,128,128]{3,2,1,0:T(8,128)(2,1)S(1)}, u32[]{:S(2)}, u32[]{:S(2)}) collective-permute-start(bf16[2,2,128,128]{3,2,1,0:T(8,128)(2,1)S(1)} %get-tuple-element.28), channel_id=1, source_target_pairs={{0,12},{1,13},{2,14},{3,15},{4,8},{5,9},{6,10},{7,11},{8,4},{9,5},... | collective-permute-start | bytes 393224 | tf_op jit(solution)/shard_map/ppermute | solution.py:551
  29.4 2.4 %collective-permute-start.8 = (bf16[2,2,128,128]{3,2,1,0:T(8,128)(2,1)S(1)}, bf16[2,2,128,128]{3,2,1,0:T(8,128)(2,1)S(1)}, u32[]{:S(2)}, u32[]{:S(2)}) collective-permute-start(bf16[2,2,128,128]{3,2,1,0:T(8,128)(2,1)S(1)} %get-tuple-element.29), channel_id=1, source_target_pairs={{0,14},{1,15},{2,12},{3,13},{4,10},{5,11},{6,8},{7,9},{8,6},{9,7},... | collective-permute-start | bytes 393224 | tf_op jit(solution)/shard_map/ppermute | solution.py:551
  31.8 2.8 %shard_map.124 = bf16[4,2,512,128]{3,2,1,0:T(8,128)(2,1)} custom-call(s32[16]{0:T(128)S(1)} %copy-done.3, s32[2,4]{1,0:T(2,128)S(1)} %copy-done.2, bf16[2,2,128,128]{3,2,1,0:T(8,128)(2,1)S(1)} %get-tuple-element.26._, bf16[4,2,128,128]{3,2,1,0:T(8,128)(2,1)} %collective-permute-done.3.refs_4_.refs_0_, ...), custom_call_target="tpu_custom_call" | custom-call | tf_op jit(solution)/shard_map/pallas_call | solution.py:267
  34.5 2.7 %all-to-all-done.ev_ref = bf16[8,4,128,128]{3,2,1,0:T(8,128)(2,1)S(1)} async-done(((bf16[8,4,128,128]{3,2,1,0:T(8,128)(2,1)}), bf16[8,4,128,128]{3,2,1,0:T(8,128)(2,1)S(1)}, u32[]{:S(2)}, u32[]{:S(2)}) %all-to-all-start) | async-done | bytes 1048608 | tf_op jit(solution)/shard_map/all_to_all | solution.py:541
  37.2 3.7 %all-to-all-start.1 = ((bf16[4,2,512,128]{3,2,1,0:T(8,128)(2,1)}), bf16[4,2,512,128]{3,2,1,0:T(8,128)(2,1)S(1)}, u32[]{:S(2)}, u32[]{:S(2)}) async-start(bf16[4,2,512,128]{3,2,1,0:T(8,128)(2,1)} %shard_map.124), calls=%async_computation.1 | async-start | bytes 2097152 | tf_op jit(solution)/shard_map/all_to_all | solution.py:555
  40.9 0.9 collective-permute-done.7.refs_2_
  41.8 3.8 %collective-permute-done.8.refs_3_ = bf16[2,2,128,128]{3,2,1,0:T(8,128)(2,1)S(1)} collective-permute-done((bf16[2,2,128,128]{3,2,1,0:T(8,128)(2,1)S(1)}, bf16[2,2,128,128]{3,2,1,0:T(8,128)(2,1)S(1)}, u32[]{:S(2)}, u32[]{:S(2)}) %collective-permute-start.8) | collective-permute-done | bytes 131104 | tf_op jit(solution)/shard_map/ppermute | solution.py:551
  45.6 5.5 %collective-permute-done.5.refs_0_ = bf16[2,2,128,128]{3,2,1,0:T(8,128)(2,1)S(1)} collective-permute-done((bf16[2,2,128,128]{3,2,1,0:T(8,128)(2,1)S(1)}, bf16[2,2,128,128]{3,2,1,0:T(8,128)(2,1)S(1)}, u32[]{:S(2)}, u32[]{:S(2)}) %collective-permute-start.5) | collective-permute-done | bytes 131104 | tf_op jit(solution)/shard_map/ppermute | solution.py:551
  51.1 7.1 %all-to-all-done.1.near_ref = bf16[4,2,512,128]{3,2,1,0:T(8,128)(2,1)S(1)} async-done(((bf16[4,2,512,128]{3,2,1,0:T(8,128)(2,1)}), bf16[4,2,512,128]{3,2,1,0:T(8,128)(2,1)S(1)}, u32[]{:S(2)}, u32[]{:S(2)}) %all-to-all-start.1) | async-done | bytes 1048608 | tf_op jit(solution)/shard_map/all_to_all | solution.py:555
  58.2 4.6 %shard_map.126 = (bf16[4,128,128]{2,1,0:T(8,128)(2,1)S(1)}, f32[512,128]{1,0:T(8,128)S(1)}, f32[512,128]{1,0:T(8,128)S(1)}, f32[2,8,256]{2,1,0:T(8,128)S(1)}) custom-call(s32[2]{0:T(128)S(1)} %copy-done.1, s32[2]{0:T(128)S(1)} %copy-done.4, f32[8,128]{1,0:T(8,128)S(1)} %shard_map.125._, bf16[8,4,128,128]{3,2,1,0:T(8,128)(2,1)S(1)} %all-to-all-done.ev_ref, ...), custom_call_target="tpu_custom_call" | custom-call | flops 1677721600 | bytes 1310720 | tf_op jit(solution)/shard_map/pallas_call | solution.py:404
  62.9 1.5 %collective-permute-start.9 = (f32[2,8,256]{2,1,0:T(8,128)S(1)}, f32[2,8,256]{2,1,0:T(8,128)S(1)}, u32[]{:S(2)}, u32[]{:S(2)}) collective-permute-start(f32[2,8,256]{2,1,0:T(8,128)S(1)} %get-tuple-element.30), channel_id=1, source_target_pairs={{8,0},{9,1},{10,2},{11,3},{12,4},{13,5},{14,6},{15,7},{24,16},{25,... | collective-permute-start | bytes 49160 | tf_op jit(solution)/shard_map/ppermute | solution.py:559
  64.4 4.8 %shard_map.127 = (bf16[4,128,128]{2,1,0:T(8,128)(2,1)S(1)}, f32[1024,128]{1,0:T(8,128)S(1)}, f32[1024,128]{1,0:T(8,128)S(1)}) custom-call(s32[2]{0:T(128)S(1)} %copy-done.1, s32[2]{0:T(128)S(1)} %copy-done.4, f32[8,128]{1,0:T(8,128)S(1)} %shard_map.125._, bf16[8,4,128,128]{3,2,1,0:T(8,128)(2,1)S(1)} %all-to-all-done.ev_ref, ...), custom_call_target="tpu_custom_call" | custom-call | flops 1677721600 | bytes 1310720 | tf_op jit(solution)/shard_map/pallas_call | solution.py:404
  69.2 0.4 collective-permute-done.9.stats_ref
  69.6 1.4 %shard_map.128 = bf16[8,3,128,128]{3,2,1,0:T(8,128)(2,1)S(1)} custom-call(s32[2]{0:T(128)S(1)} %copy-done.1, bf16[8,4,128,128]{3,2,1,0:T(8,128)(2,1)S(1)} %all-to-all-done.ev_ref, bf16[4,2,512,128]{3,2,1,0:T(8,128)(2,1)S(1)} %all-to-all-done.1.near_ref, f32[2,8,256]{2,1,0:T(8,128)S(1)} %collective-permute-done.9.stats_ref, ...), custom_call_target="tpu_custom_call" | custom-call | tf_op jit(solution)/shard_map/pallas_call | solution.py:463
  71.0 14.3 %all_to_all.15.in_ref = bf16[8,3,128,128]{3,2,1,0:T(8,128)(2,1)S(1)} all-to-all(bf16[8,3,128,128]{3,2,1,0:T(8,128)(2,1)S(1)} %shard_map.128), channel_id=1, replica_groups={{0,1,2,3,4,5,6,7},{8,9,10,11,12,13,14,15},{16,17,18,19,20,21,22,23},{24..., dimensions={0} | all-to-all | bytes 1572864 | tf_op jit(solution)/shard_map/all_to_all | solution.py:562
  85.3 1.0 %shard_map.129 = (bf16[1,128,1024]{2,1,0:T(8,128)(2,1)}, bf16[1,128,1024]{2,1,0:T(8,128)(2,1)}, bf16[1,128,1024]{2,1,0:T(8,128)(2,1)}) custom-call(bf16[8,3,128,128]{3,2,1,0:T(8,128)(2,1)S(1)} %all_to_all.15.in_ref), custom_call_target="tpu_custom_call" | custom-call | tf_op jit(solution)/shard_map/pallas_call | solution.py:489
  (12 shorter events, 0.0 us)
Async XLA Ops:
  4.0 15.9 %collective-permute-start = (bf16[4,2,128,128]{3,2,1,0:T(8,128)(2,1)}, bf16[4,2,128,128]{3,2,1,0:T(8,128)(2,1)}, u32[]{:S(2)}, u32[]{:S(2)}) collective-permute-start(bf16[4,2,128,128]{3,2,1,0:T(8,128)(2,1)} %get-tuple-element.20), channel_id=1, source_target_pairs={{0,16},{1,17},{2,18},{3,19},{4,20},{5,21},{6,22},{7,23},{8,24},{9,... | collective-permute-start | bytes 786440 | tf_op jit(solution)/shard_map/ppermute | solution.py:533
  7.0 13.0 %collective-permute-start.1 = (bf16[4,2,128,128]{3,2,1,0:T(8,128)(2,1)}, bf16[4,2,128,128]{3,2,1,0:T(8,128)(2,1)}, u32[]{:S(2)}, u32[]{:S(2)}) collective-permute-start(bf16[4,2,128,128]{3,2,1,0:T(8,128)(2,1)} %get-tuple-element.21), channel_id=1, source_target_pairs={{0,17},{1,16},{2,19},{3,18},{4,21},{5,20},{6,23},{7,22},{8,25},{9,... | collective-permute-start | bytes 786440 | tf_op jit(solution)/shard_map/ppermute | solution.py:533
  7.0 13.0 %collective-permute-start.2 = (bf16[4,2,128,128]{3,2,1,0:T(8,128)(2,1)}, bf16[4,2,128,128]{3,2,1,0:T(8,128)(2,1)}, u32[]{:S(2)}, u32[]{:S(2)}) collective-permute-start(bf16[4,2,128,128]{3,2,1,0:T(8,128)(2,1)} %get-tuple-element.23), channel_id=1, source_target_pairs={{0,1},{1,0},{2,3},{3,2},{4,5},{5,4},{6,7},{7,6},{8,9},{9,8},{10,11... | collective-permute-start | bytes 786440 | tf_op jit(solution)/shard_map/ppermute | solution.py:526
  7.2 12.8 %collective-permute-start.3 = (bf16[4,2,128,128]{3,2,1,0:T(8,128)(2,1)}, bf16[4,2,128,128]{3,2,1,0:T(8,128)(2,1)}, u32[]{:S(2)}, u32[]{:S(2)}) collective-permute-start(bf16[4,2,128,128]{3,2,1,0:T(8,128)(2,1)} %get-tuple-element.24), channel_id=1, source_target_pairs={{4,8},{5,9},{6,10},{7,11},{8,4},{9,5},{10,6},{11,7},{20,24},{21,25... | collective-permute-start | bytes 786440 | tf_op jit(solution)/shard_map/ppermute | solution.py:537
  8.6 11.4 %collective-permute-start.4 = (bf16[4,2,128,128]{3,2,1,0:T(8,128)(2,1)}, bf16[4,2,128,128]{3,2,1,0:T(8,128)(2,1)}, u32[]{:S(2)}, u32[]{:S(2)}) collective-permute-start(bf16[4,2,128,128]{3,2,1,0:T(8,128)(2,1)} %get-tuple-element.25), channel_id=1, source_target_pairs={{4,9},{5,8},{6,11},{7,10},{8,5},{9,4},{10,7},{11,6},{20,25},{21,24... | collective-permute-start | bytes 786440 | tf_op jit(solution)/shard_map/ppermute | solution.py:537
  12.6 7.4 %copy-start = (bf16[4,2,128,128]{3,2,1,0:T(8,128)(2,1)S(1)}, bf16[4,2,128,128]{3,2,1,0:T(8,128)(2,1)}, u32[]{:S(2)}) copy-start(bf16[4,2,128,128]{3,2,1,0:T(8,128)(2,1)} %get-tuple-element.22.refs_2_) | copy-start | bytes 786436
  12.7 24.5 %all-to-all-start = ((bf16[8,4,128,128]{3,2,1,0:T(8,128)(2,1)}), bf16[8,4,128,128]{3,2,1,0:T(8,128)(2,1)S(1)}, u32[]{:S(2)}, u32[]{:S(2)}) async-start(bf16[8,4,128,128]{3,2,1,0:T(8,128)(2,1)} %shard_map.121), calls=%async_computation | async-start | bytes 2097152 | tf_op jit(solution)/shard_map/all_to_all | solution.py:541
  19.9 0.7 copy-start.2
  19.9 0.7 copy-start.3
  22.3 18.7 %collective-permute-start.6 = (bf16[2,2,128,128]{3,2,1,0:T(8,128)(2,1)S(1)}, bf16[2,2,128,128]{3,2,1,0:T(8,128)(2,1)S(1)}, u32[]{:S(2)}, u32[]{:S(2)}) collective-permute-start(bf16[2,2,128,128]{3,2,1,0:T(8,128)(2,1)S(1)} %get-tuple-element.27), channel_id=1, source_target_pairs={{0,10},{1,11},{2,8},{3,9},{4,14},{5,15},{6,12},{7,13},{8,2},{9,3},... | collective-permute-start | bytes 393224 | tf_op jit(solution)/shard_map/ppermute | solution.py:551
  28.0 13.8 %collective-permute-start.7 = (bf16[2,2,128,128]{3,2,1,0:T(8,128)(2,1)S(1)}, bf16[2,2,128,128]{3,2,1,0:T(8,128)(2,1)S(1)}, u32[]{:S(2)}, u32[]{:S(2)}) collective-permute-start(bf16[2,2,128,128]{3,2,1,0:T(8,128)(2,1)S(1)} %get-tuple-element.28), channel_id=1, source_target_pairs={{0,12},{1,13},{2,14},{3,15},{4,8},{5,9},{6,10},{7,11},{8,4},{9,5},... | collective-permute-start | bytes 393224 | tf_op jit(solution)/shard_map/ppermute | solution.py:551
  29.4 16.2 %collective-permute-start.8 = (bf16[2,2,128,128]{3,2,1,0:T(8,128)(2,1)S(1)}, bf16[2,2,128,128]{3,2,1,0:T(8,128)(2,1)S(1)}, u32[]{:S(2)}, u32[]{:S(2)}) collective-permute-start(bf16[2,2,128,128]{3,2,1,0:T(8,128)(2,1)S(1)} %get-tuple-element.29), channel_id=1, source_target_pairs={{0,14},{1,15},{2,12},{3,13},{4,10},{5,11},{6,8},{7,9},{8,6},{9,7},... | collective-permute-start | bytes 393224 | tf_op jit(solution)/shard_map/ppermute | solution.py:551
  31.8 19.3 %collective-permute-start.5 = (bf16[2,2,128,128]{3,2,1,0:T(8,128)(2,1)S(1)}, bf16[2,2,128,128]{3,2,1,0:T(8,128)(2,1)S(1)}, u32[]{:S(2)}, u32[]{:S(2)}) collective-permute-start(bf16[2,2,128,128]{3,2,1,0:T(8,128)(2,1)S(1)} %get-tuple-element.26._), channel_id=1, source_target_pairs={{0,8},{1,9},{2,10},{3,11},{4,12},{5,13},{6,14},{7,15},{8,0},{9,1},... | collective-permute-start | bytes 393224 | tf_op jit(solution)/shard_map/ppermute | solution.py:551
  37.2 21.0 %all-to-all-start.1 = ((bf16[4,2,512,128]{3,2,1,0:T(8,128)(2,1)}), bf16[4,2,512,128]{3,2,1,0:T(8,128)(2,1)S(1)}, u32[]{:S(2)}, u32[]{:S(2)}) async-start(bf16[4,2,512,128]{3,2,1,0:T(8,128)(2,1)} %shard_map.124), calls=%async_computation.1 | async-start | bytes 2097152 | tf_op jit(solution)/shard_map/all_to_all | solution.py:555
  40.9 17.3 %copy-start.1 = (s32[2]{0:T(128)S(1)}, s32[2]{0:T(128)}, u32[]{:S(2)}) copy-start(s32[2]{0:T(128)} %length_ref.9) | copy-start | bytes 28
  40.9 17.3 %copy-start.4 = (s32[2]{0:T(128)S(1)}, s32[2]{0:T(128)}, u32[]{:S(2)}) copy-start(s32[2]{0:T(128)} %count_ref.3) | copy-start | bytes 28
  62.9 6.7 %collective-permute-start.9 = (f32[2,8,256]{2,1,0:T(8,128)S(1)}, f32[2,8,256]{2,1,0:T(8,128)S(1)}, u32[]{:S(2)}, u32[]{:S(2)}) collective-permute-start(f32[2,8,256]{2,1,0:T(8,128)S(1)} %get-tuple-element.30), channel_id=1, source_target_pairs={{8,0},{9,1},{10,2},{11,3},{12,4},{13,5},{14,6},{15,7},{24,16},{25,... | collective-permute-start | bytes 49160 | tf_op jit(solution)/shard_map/ppermute | solution.py:559

commit v5 on v4

--- a/solution.py
+++ b/solution.py
@@ -292,6 +292,7 @@
 def attend_body(scale, depth, half, memories, length_ref, count_ref, _, ev_ref, near_ref, *refs):
     far_refs, refs = refs[:memories], refs[memories:]
     gq_ref, gk_ref, gv_ref = refs[:3]
+    k_all, v_all = refs[-2:]
     rows, hd = ev_ref.shape[2:]
     tile = 2 * rows
     tiles = WINDOW // tile
@@ -302,13 +303,18 @@
     slope = scale * LOG2E
 
     def events(part, chunk):
-        return ev_ref[2 * chunk : 2 * chunk + 2, part].reshape(tile, hd)
-
-    def window(part, chunk):
-        chunk += half * tiles
-        if chunk < 0:
-            return near_ref[tiles + chunk, part - 1, near:].reshape(tile, hd)
-        return events(part, chunk)
+        return ev_ref[pl.ds(2 * chunk, 2), part].reshape(tile, hd)
+
+    for chunk in range(2 * tiles):
+        where = slice(chunk * tile, (chunk + 1) * tile)
+        number = chunk + (half - 1) * tiles
+        for part, all_ref in ((1, k_all), (2, v_all)):
+            if number < 0:
+                all_ref[where] = near_ref[chunk, part - 1, near:].reshape(tile, hd)
+            else:
+                all_ref[where] = events(part, number)
+    gk_ref[...] = jnp.zeros_like(gk_ref)
+    gv_ref[...] = jnp.zeros_like(gv_ref)
 
     per = max(1, tile // near)
     memory = [
@@ -329,12 +335,12 @@
     which = lax.broadcasted_iota(jnp.int32, (1, per * near), 1)
     live = lax.rem(which, near // 2) // depth < count
 
-    sums = {}
-    for this in range(tiles):
+    def step(this, carry):
         q, g = events(0, half * tiles + this), events(3, half * tiles + this)
-        chunks = list(range(this - tiles, this + 1))
-        keys = [window(1, chunk) for chunk in chunks] + memory[0]
-        values = [window(2, chunk) for chunk in chunks] + memory[1]
+        chunks = [this - tiles + i for i in range(tiles + 1)]
+        spans = [pl.ds(pl.multiple_of((this + i) * tile, tile), tile) for i in range(tiles + 1)]
+        keys = [k_all[span] for span in spans] + memory[0]
+        values = [v_all[span] for span in spans] + memory[1]
         score = []
         for i, key in enumerate(keys):
             s = dot_nt(q, key)
@@ -378,18 +384,22 @@
             prob = expo[i] * inv
             dscore = (prob * (dprob[i] - delta)).astype(jnp.bfloat16)
             gq += dot_nn(dscore, keys[i])
-            if chunk + half * tiles >= 0:
-                owed = dot_tn(dscore, q), dot_tn(prob.astype(jnp.bfloat16), g)
-                old = sums.get(chunk)
-                sums[chunk] = owed if old is None else (old[0] + owed[0], old[1] + owed[1])
-        gq_ref[2 * this : 2 * this + 2] = (gq * scale).astype(gq_ref.dtype).reshape(2, rows, hd)
+            owed = dot_tn(dscore, q) * scale, dot_tn(prob.astype(jnp.bfloat16), g)
+            first = pl.multiple_of(jnp.maximum(chunk + half * tiles, 0) * tile, tile)
+
+            @pl.when(chunk + half * tiles >= 0)
+            def _():
+                gk_ref[pl.ds(first, tile)] += owed[0]
+                gv_ref[pl.ds(first, tile)] += owed[1]
+
+        gq_ref[pl.ds(2 * this, 2)] = (gq * scale).astype(gq_ref.dtype).reshape(2, rows, hd)
         if half == 0:
             lane = lax.broadcasted_iota(jnp.int32, (tile, hd), 1)
             both = jnp.where(lane == 0, top * slope + jnp.log2(total), delta)
             refs[3][this] = both.T[:8]
-    for i, chunk in enumerate(sorted(sums)):
-        gk_ref[i * tile : (i + 1) * tile] = sums[chunk][0] * scale
-        gv_ref[i * tile : (i + 1) * tile] = sums[chunk][1]
+        return carry
+
+    lax.fori_loop(0, tiles, step, 0)
 
 
 def attend(scale, depth, half, seq_lengths, mem_counts, after, events, near, far):
@@ -406,6 +416,7 @@
         in_specs=[smem] * 2 + [pl.BlockSpec(memory_space=pl.ANY)] + [vmem] * (2 + len(far)),
         out_specs=[vmem] * len(outs),
         out_shape=[jax.ShapeDtypeStruct(shape, dtype) for shape, dtype in outs],
+        scratch_shapes=[pltpu.VMEM((2 * WINDOW, hd), events.dtype)] * 2,
         cost_estimate=pl.CostEstimate(
             flops=10 * WINDOW * keys * hd,
             bytes_accessed=4 * keys * hd,

time: 87 us -> 89.2 us (1.025)
  Pallas kernels: 22.4 us -> 25.2 us
    pallas_call x2, Pallas kernels: 9.49 us -> 12.2 us  [attend(): call(functools.partial(attend_body, scale, depth, half, len(far)), in_spe...]
  transfers between devices with their start and end apart: 12 -> 12, of which waited for: 6 -> 5; matrix products, arithmetic and copies ran while one was open for 0% -> 0% of each run, Pallas kernels for 14% -> 15%
where the time goes in v5:
time: 89.2 us; the launch traced here: 88.8 us
  starting transfers between devices  27.7 us (31%)
  Pallas kernels  25.2 us (28%)
  waiting for transfers between devices  19.9 us (22%)
  blocking collectives  14.5 us (16%)
    all_to_all x1, blocking collectives, on_device(): return tuple(join_heads(swap(out, axis_index_groups=groups)))  14.5 us
    pallas_call x2, Pallas kernels, attend(): call(functools.partial(attend_body, scale, depth, half, len(far)), in_spe...  12.2 us
    ppermute x4, waiting for transfers between devices, on_device(): far.append(lax.ppermute(piece, 'seq', pairs))  10.1 us
    ppermute x4, starting transfers between devices, on_device(): far.append(lax.ppermute(piece, 'seq', pairs))  9.45 us
    all_to_all x1, starting transfers between devices, on_device(): events = swap(split_heads(seq_lengths, arrays), axis_index_groups=groups)  7.34 us
    all_to_all x1, waiting for transfers between devices, on_device(): near = swap(near, axis_index_groups=parities)  7.1 us
    all_to_all x1, starting transfers between devices, on_device(): near = swap(near, axis_index_groups=parities)  3.77 us
    pallas_call x1, Pallas kernels, pack(): call(functools.partial(pack_body, users), limit=VMEM_WHOLE, in_specs=[sme...  3.46 us
  transfers between devices with their start and end apart: 12, of which 5 were waited for; matrix products, arithmetic and copies ran while one was open for 0% of the time, Pallas kernels for 15%

profile of v5, /device:TPU:0, one launch (start us, length us, event | category | flops | bytes accessed | tf_op | source)
XLA Modules:
  0.0 88.8 jit_solution(6756919358349812782)
XLA Ops:
  0.6 3.5 %shard_map.122 = (bf16[4,2,128,128]{3,2,1,0:T(8,128)(2,1)}, bf16[4,2,128,128]{3,2,1,0:T(8,128)(2,1)}, bf16[4,2,128,128]{3,2,1,0:T(8,128)(2,1)}, bf16[4,2,128,128...) custom-call(s32[2]{0:T(128)} %length_ref.9, s32[16]{0:T(128)} %slots_ref.5, ...), custom_call_target="tpu_custom_call" | custom-call | tf_op jit(solution)/shard_map/pallas_call | solution.py:143
  4.1 3.0 %collective-permute-start = (bf16[4,2,128,128]{3,2,1,0:T(8,128)(2,1)}, bf16[4,2,128,128]{3,2,1,0:T(8,128)(2,1)}, u32[]{:S(2)}, u32[]{:S(2)}) collective-permute-start(bf16[4,2,128,128]{3,2,1,0:T(8,128)(2,1)} %get-tuple-element.20), channel_id=1, source_target_pairs={{0,16},{1,17},{2,18},{3,19},{4,20},{5,21},{6,22},{7,23},{8,24},{9,... | collective-permute-start | bytes 786440 | tf_op jit(solution)/shard_map/ppermute | solution.py:544
  7.1 0.2 collective-permute-start.2
  7.3 1.4 %collective-permute-start.3 = (bf16[4,2,128,128]{3,2,1,0:T(8,128)(2,1)}, bf16[4,2,128,128]{3,2,1,0:T(8,128)(2,1)}, u32[]{:S(2)}, u32[]{:S(2)}) collective-permute-start(bf16[4,2,128,128]{3,2,1,0:T(8,128)(2,1)} %get-tuple-element.24), channel_id=1, source_target_pairs={{4,8},{5,9},{6,10},{7,11},{8,4},{9,5},{10,6},{11,7},{20,24},{21,25... | collective-permute-start | bytes 786440 | tf_op jit(solution)/shard_map/ppermute | solution.py:548
  8.6 1.3 %collective-permute-start.4 = (bf16[4,2,128,128]{3,2,1,0:T(8,128)(2,1)}, bf16[4,2,128,128]{3,2,1,0:T(8,128)(2,1)}, u32[]{:S(2)}, u32[]{:S(2)}) collective-permute-start(bf16[4,2,128,128]{3,2,1,0:T(8,128)(2,1)} %get-tuple-element.25), channel_id=1, source_target_pairs={{4,9},{5,8},{6,11},{7,10},{8,5},{9,4},{10,7},{11,6},{20,25},{21,24... | collective-permute-start | bytes 786440 | tf_op jit(solution)/shard_map/ppermute | solution.py:548
  10.0 2.7 %shard_map.121 = bf16[8,4,128,128]{3,2,1,0:T(8,128)(2,1)} custom-call(s32[2]{0:T(128)} %length_ref.9, bf16[1,128,1024]{2,1,0:T(8,128)(2,1)} %refs_0_.3, bf16[1,128,1024]{2,1,0:T(8,128)(2,1)} %refs_1_.3, bf16[1,128,1024]{2,1,0:T(8,128)(2,1)} %refs_2_.3, bf16[1,128,1024]{2,1,0:T(8,128)(2,1)} %refs_3_.3), custom_call_target="tpu_custom_call" | custom-call | tf_op jit(solution)/shard_map/pallas_call | solution.py:187
  12.7 0.0 copy-start
  12.7 7.3 %all-to-all-start = ((bf16[8,4,128,128]{3,2,1,0:T(8,128)(2,1)}), bf16[8,4,128,128]{3,2,1,0:T(8,128)(2,1)S(1)}, u32[]{:S(2)}, u32[]{:S(2)}) async-start(bf16[8,4,128,128]{3,2,1,0:T(8,128)(2,1)} %shard_map.121), calls=%async_computation | async-start | bytes 2097152 | tf_op jit(solution)/shard_map/all_to_all | solution.py:552
  20.1 0.0 copy-start.3
  20.1 0.0 collective-permute-done.2.refs_3_
  20.1 0.0 collective-permute-done.3.refs_4_.refs_0_
  20.2 0.6 copy-done.2
  20.8 1.7 %shard_map.123 = (bf16[2,2,128,128]{3,2,1,0:T(8,128)(2,1)S(1)}, bf16[2,2,128,128]{3,2,1,0:T(8,128)(2,1)S(1)}, bf16[2,2,128,128]{3,2,1,0:T(8,128)(2,1)S(1)}, bf16[2,2,128,128]{3,2,1,0:T(8,128)(2,1)S(1)}) custom-call(s32[16]{0:T(128)S(1)} %copy-done.3, s32[2,4]{1,0:T(2,128)S(1)} %copy-done.2, bf16[4,2,128,128]{3,2,1,0:T(8,128)(2,1)} %collective-permute-done.refs_0_.refs_4_, ...), custom_call_target="tpu_custom_call" | custom-call | flops 99999997952 | tf_op jit(solution)/shard_map/pallas_call | solution.py:232
  22.4 5.7 %collective-permute-start.6 = (bf16[2,2,128,128]{3,2,1,0:T(8,128)(2,1)S(1)}, bf16[2,2,128,128]{3,2,1,0:T(8,128)(2,1)S(1)}, u32[]{:S(2)}, u32[]{:S(2)}) collective-permute-start(bf16[2,2,128,128]{3,2,1,0:T(8,128)(2,1)S(1)} %get-tuple-element.27), channel_id=1, source_target_pairs={{0,10},{1,11},{2,8},{3,9},{4,14},{5,15},{6,12},{7,13},{8,2},{9,3},... | collective-permute-start | bytes 393224 | tf_op jit(solution)/shard_map/ppermute | solution.py:562
  28.1 1.4 %collective-permute-start.7 = (bf16[2,2,128,128]{3,2,1,0:T(8,128)(2,1)S(1)}, bf16[2,2,128,128]{3,2,1,0:T(8,128)(2,1)S(1)}, u32[]{:S(2)}, u32[]{:S(2)}) collective-permute-start(bf16[2,2,128,128]{3,2,1,0:T(8,128)(2,1)S(1)} %get-tuple-element.28), channel_id=1, source_target_pairs={{0,12},{1,13},{2,14},{3,15},{4,8},{5,9},{6,10},{7,11},{8,4},{9,5},... | collective-permute-start | bytes 393224 | tf_op jit(solution)/shard_map/ppermute | solution.py:562
  29.5 2.4 %collective-permute-start.8 = (bf16[2,2,128,128]{3,2,1,0:T(8,128)(2,1)S(1)}, bf16[2,2,128,128]{3,2,1,0:T(8,128)(2,1)S(1)}, u32[]{:S(2)}, u32[]{:S(2)}) collective-permute-start(bf16[2,2,128,128]{3,2,1,0:T(8,128)(2,1)S(1)} %get-tuple-element.29), channel_id=1, source_target_pairs={{0,14},{1,15},{2,12},{3,13},{4,10},{5,11},{6,8},{7,9},{8,6},{9,7},... | collective-permute-start | bytes 393224 | tf_op jit(solution)/shard_map/ppermute | solution.py:562
  31.9 0.0 collective-permute-start.5
  31.9 2.8 %shard_map.124 = bf16[4,2,512,128]{3,2,1,0:T(8,128)(2,1)} custom-call(s32[16]{0:T(128)S(1)} %copy-done.3, s32[2,4]{1,0:T(2,128)S(1)} %copy-done.2, bf16[2,2,128,128]{3,2,1,0:T(8,128)(2,1)S(1)} %get-tuple-element.26._, bf16[4,2,128,128]{3,2,1,0:T(8,128)(2,1)} %collective-permute-done.3.refs_4_.refs_0_, ...), custom_call_target="tpu_custom_call" | custom-call | tf_op jit(solution)/shard_map/pallas_call | solution.py:267
  34.6 2.7 %all-to-all-done.ev_ref = bf16[8,4,128,128]{3,2,1,0:T(8,128)(2,1)S(1)} async-done(((bf16[8,4,128,128]{3,2,1,0:T(8,128)(2,1)}), bf16[8,4,128,128]{3,2,1,0:T(8,128)(2,1)S(1)}, u32[]{:S(2)}, u32[]{:S(2)}) %all-to-all-start) | async-done | bytes 1048608 | tf_op jit(solution)/shard_map/all_to_all | solution.py:552
  37.4 3.8 %all-to-all-start.1 = ((bf16[4,2,512,128]{3,2,1,0:T(8,128)(2,1)}), bf16[4,2,512,128]{3,2,1,0:T(8,128)(2,1)S(1)}, u32[]{:S(2)}, u32[]{:S(2)}) async-start(bf16[4,2,512,128]{3,2,1,0:T(8,128)(2,1)} %shard_map.124), calls=%async_computation.1 | async-start | bytes 2097152 | tf_op jit(solution)/shard_map/all_to_all | solution.py:566
  41.1 0.0 collective-permute-done.6.refs_1_
  41.1 0.8 collective-permute-done.7.refs_2_
  41.9 3.8 %collective-permute-done.8.refs_3_ = bf16[2,2,128,128]{3,2,1,0:T(8,128)(2,1)S(1)} collective-permute-done((bf16[2,2,128,128]{3,2,1,0:T(8,128)(2,1)S(1)}, bf16[2,2,128,128]{3,2,1,0:T(8,128)(2,1)S(1)}, u32[]{:S(2)}, u32[]{:S(2)}) %collective-permute-start.8) | collective-permute-done | bytes 131104 | tf_op jit(solution)/shard_map/ppermute | solution.py:562
  45.7 5.5 %collective-permute-done.5.refs_0_ = bf16[2,2,128,128]{3,2,1,0:T(8,128)(2,1)S(1)} collective-permute-done((bf16[2,2,128,128]{3,2,1,0:T(8,128)(2,1)S(1)}, bf16[2,2,128,128]{3,2,1,0:T(8,128)(2,1)S(1)}, u32[]{:S(2)}, u32[]{:S(2)}) %collective-permute-start.5) | collective-permute-done | bytes 131104 | tf_op jit(solution)/shard_map/ppermute | solution.py:562
  51.2 7.1 %all-to-all-done.1.near_ref = bf16[4,2,512,128]{3,2,1,0:T(8,128)(2,1)S(1)} async-done(((bf16[4,2,512,128]{3,2,1,0:T(8,128)(2,1)}), bf16[4,2,512,128]{3,2,1,0:T(8,128)(2,1)S(1)}, u32[]{:S(2)}, u32[]{:S(2)}) %all-to-all-start.1) | async-done | bytes 1048608 | tf_op jit(solution)/shard_map/all_to_all | solution.py:566
  58.3 6.1 %shard_map.126 = (bf16[4,128,128]{2,1,0:T(8,128)(2,1)S(1)}, f32[512,128]{1,0:T(8,128)S(1)}, f32[512,128]{1,0:T(8,128)S(1)}, f32[2,8,256]{2,1,0:T(8,128)S(1)}) custom-call(s32[2]{0:T(128)S(1)} %copy-done.1, s32[2]{0:T(128)S(1)} %copy-done.4, f32[8,128]{1,0:T(8,128)S(1)} %shard_map.125._, bf16[8,4,128,128]{3,2,1,0:T(8,128)(2,1)S(1)} %all-to-all-done.ev_ref, ...), custom_call_target="tpu_custom_call" | custom-call | flops 1677721600 | bytes 1310720 | tf_op jit(solution)/shard_map/pallas_call | solution.py:414
  64.5 1.3 %collective-permute-start.9 = (f32[2,8,256]{2,1,0:T(8,128)S(1)}, f32[2,8,256]{2,1,0:T(8,128)S(1)}, u32[]{:S(2)}, u32[]{:S(2)}) collective-permute-start(f32[2,8,256]{2,1,0:T(8,128)S(1)} %get-tuple-element.30), channel_id=1, source_target_pairs={{8,0},{9,1},{10,2},{11,3},{12,4},{13,5},{14,6},{15,7},{24,16},{25,... | collective-permute-start | bytes 49160 | tf_op jit(solution)/shard_map/ppermute | solution.py:570
  65.8 6.1 %shard_map.127 = (bf16[4,128,128]{2,1,0:T(8,128)(2,1)S(1)}, f32[1024,128]{1,0:T(8,128)S(1)}, f32[1024,128]{1,0:T(8,128)S(1)}) custom-call(s32[2]{0:T(128)S(1)} %copy-done.1, s32[2]{0:T(128)S(1)} %copy-done.4, f32[8,128]{1,0:T(8,128)S(1)} %shard_map.125._, bf16[8,4,128,128]{3,2,1,0:T(8,128)(2,1)S(1)} %all-to-all-done.ev_ref, ...), custom_call_target="tpu_custom_call" | custom-call | flops 1677721600 | bytes 1310720 | tf_op jit(solution)/shard_map/pallas_call | solution.py:414
  71.8 0.0 collective-permute-done.9.stats_ref
  71.9 1.4 %shard_map.128 = bf16[8,3,128,128]{3,2,1,0:T(8,128)(2,1)S(1)} custom-call(s32[2]{0:T(128)S(1)} %copy-done.1, bf16[8,4,128,128]{3,2,1,0:T(8,128)(2,1)S(1)} %all-to-all-done.ev_ref, bf16[4,2,512,128]{3,2,1,0:T(8,128)(2,1)S(1)} %all-to-all-done.1.near_ref, f32[2,8,256]{2,1,0:T(8,128)S(1)} %collective-permute-done.9.stats_ref, ...), custom_call_target="tpu_custom_call" | custom-call | tf_op jit(solution)/shard_map/pallas_call | solution.py:474
  73.3 14.5 %all_to_all.15.in_ref = bf16[8,3,128,128]{3,2,1,0:T(8,128)(2,1)S(1)} all-to-all(bf16[8,3,128,128]{3,2,1,0:T(8,128)(2,1)S(1)} %shard_map.128), channel_id=1, replica_groups={{0,1,2,3,4,5,6,7},{8,9,10,11,12,13,14,15},{16,17,18,19,20,21,22,23},{24..., dimensions={0} | all-to-all | bytes 1572864 | tf_op jit(solution)/shard_map/all_to_all | solution.py:573
  87.8 1.0 %shard_map.129 = (bf16[1,128,1024]{2,1,0:T(8,128)(2,1)}, bf16[1,128,1024]{2,1,0:T(8,128)(2,1)}, bf16[1,128,1024]{2,1,0:T(8,128)(2,1)}) custom-call(bf16[8,3,128,128]{3,2,1,0:T(8,128)(2,1)S(1)} %all_to_all.15.in_ref), custom_call_target="tpu_custom_call" | custom-call | tf_op jit(solution)/shard_map/pallas_call | solution.py:500
  (12 shorter events, 0.0 us)
Async XLA Ops:
  4.1 16.0 %collective-permute-start = (bf16[4,2,128,128]{3,2,1,0:T(8,128)(2,1)}, bf16[4,2,128,128]{3,2,1,0:T(8,128)(2,1)}, u32[]{:S(2)}, u32[]{:S(2)}) collective-permute-start(bf16[4,2,128,128]{3,2,1,0:T(8,128)(2,1)} %get-tuple-element.20), channel_id=1, source_target_pairs={{0,16},{1,17},{2,18},{3,19},{4,20},{5,21},{6,22},{7,23},{8,24},{9,... | collective-permute-start | bytes 786440 | tf_op jit(solution)/shard_map/ppermute | solution.py:544
  7.1 13.0 %collective-permute-start.1 = (bf16[4,2,128,128]{3,2,1,0:T(8,128)(2,1)}, bf16[4,2,128,128]{3,2,1,0:T(8,128)(2,1)}, u32[]{:S(2)}, u32[]{:S(2)}) collective-permute-start(bf16[4,2,128,128]{3,2,1,0:T(8,128)(2,1)} %get-tuple-element.21), channel_id=1, source_target_pairs={{0,17},{1,16},{2,19},{3,18},{4,21},{5,20},{6,23},{7,22},{8,25},{9,... | collective-permute-start | bytes 786440 | tf_op jit(solution)/shard_map/ppermute | solution.py:544
  7.1 13.0 %collective-permute-start.2 = (bf16[4,2,128,128]{3,2,1,0:T(8,128)(2,1)}, bf16[4,2,128,128]{3,2,1,0:T(8,128)(2,1)}, u32[]{:S(2)}, u32[]{:S(2)}) collective-permute-start(bf16[4,2,128,128]{3,2,1,0:T(8,128)(2,1)} %get-tuple-element.23), channel_id=1, source_target_pairs={{0,1},{1,0},{2,3},{3,2},{4,5},{5,4},{6,7},{7,6},{8,9},{9,8},{10,11... | collective-permute-start | bytes 786440 | tf_op jit(solution)/shard_map/ppermute | solution.py:537
  7.3 12.8 %collective-permute-start.3 = (bf16[4,2,128,128]{3,2,1,0:T(8,128)(2,1)}, bf16[4,2,128,128]{3,2,1,0:T(8,128)(2,1)}, u32[]{:S(2)}, u32[]{:S(2)}) collective-permute-start(bf16[4,2,128,128]{3,2,1,0:T(8,128)(2,1)} %get-tuple-element.24), channel_id=1, source_target_pairs={{4,8},{5,9},{6,10},{7,11},{8,4},{9,5},{10,6},{11,7},{20,24},{21,25... | collective-permute-start | bytes 786440 | tf_op jit(solution)/shard_map/ppermute | solution.py:548
  8.6 11.5 %collective-permute-start.4 = (bf16[4,2,128,128]{3,2,1,0:T(8,128)(2,1)}, bf16[4,2,128,128]{3,2,1,0:T(8,128)(2,1)}, u32[]{:S(2)}, u32[]{:S(2)}) collective-permute-start(bf16[4,2,128,128]{3,2,1,0:T(8,128)(2,1)} %get-tuple-element.25), channel_id=1, source_target_pairs={{4,9},{5,8},{6,11},{7,10},{8,5},{9,4},{10,7},{11,6},{20,25},{21,24... | collective-permute-start | bytes 786440 | tf_op jit(solution)/shard_map/ppermute | solution.py:548
  12.7 7.4 %copy-start = (bf16[4,2,128,128]{3,2,1,0:T(8,128)(2,1)S(1)}, bf16[4,2,128,128]{3,2,1,0:T(8,128)(2,1)}, u32[]{:S(2)}) copy-start(bf16[4,2,128,128]{3,2,1,0:T(8,128)(2,1)} %get-tuple-element.22.refs_2_) | copy-start | bytes 786436
  12.7 24.6 %all-to-all-start = ((bf16[8,4,128,128]{3,2,1,0:T(8,128)(2,1)}), bf16[8,4,128,128]{3,2,1,0:T(8,128)(2,1)S(1)}, u32[]{:S(2)}, u32[]{:S(2)}) async-start(bf16[8,4,128,128]{3,2,1,0:T(8,128)(2,1)} %shard_map.121), calls=%async_computation | async-start | bytes 2097152 | tf_op jit(solution)/shard_map/all_to_all | solution.py:552
  20.1 0.7 copy-start.2
  20.1 0.7 copy-start.3
  22.4 18.7 %collective-permute-start.6 = (bf16[2,2,128,128]{3,2,1,0:T(8,128)(2,1)S(1)}, bf16[2,2,128,128]{3,2,1,0:T(8,128)(2,1)S(1)}, u32[]{:S(2)}, u32[]{:S(2)}) collective-permute-start(bf16[2,2,128,128]{3,2,1,0:T(8,128)(2,1)S(1)} %get-tuple-element.27), channel_id=1, source_target_pairs={{0,10},{1,11},{2,8},{3,9},{4,14},{5,15},{6,12},{7,13},{8,2},{9,3},... | collective-permute-start | bytes 393224 | tf_op jit(solution)/shard_map/ppermute | solution.py:562
  28.1 13.8 %collective-permute-start.7 = (bf16[2,2,128,128]{3,2,1,0:T(8,128)(2,1)S(1)}, bf16[2,2,128,128]{3,2,1,0:T(8,128)(2,1)S(1)}, u32[]{:S(2)}, u32[]{:S(2)}) collective-permute-start(bf16[2,2,128,128]{3,2,1,0:T(8,128)(2,1)S(1)} %get-tuple-element.28), channel_id=1, source_target_pairs={{0,12},{1,13},{2,14},{3,15},{4,8},{5,9},{6,10},{7,11},{8,4},{9,5},... | collective-permute-start | bytes 393224 | tf_op jit(solution)/shard_map/ppermute | solution.py:562
  29.5 16.2 %collective-permute-start.8 = (bf16[2,2,128,128]{3,2,1,0:T(8,128)(2,1)S(1)}, bf16[2,2,128,128]{3,2,1,0:T(8,128)(2,1)S(1)}, u32[]{:S(2)}, u32[]{:S(2)}) collective-permute-start(bf16[2,2,128,128]{3,2,1,0:T(8,128)(2,1)S(1)} %get-tuple-element.29), channel_id=1, source_target_pairs={{0,14},{1,15},{2,12},{3,13},{4,10},{5,11},{6,8},{7,9},{8,6},{9,7},... | collective-permute-start | bytes 393224 | tf_op jit(solution)/shard_map/ppermute | solution.py:562
  31.9 19.3 %collective-permute-start.5 = (bf16[2,2,128,128]{3,2,1,0:T(8,128)(2,1)S(1)}, bf16[2,2,128,128]{3,2,1,0:T(8,128)(2,1)S(1)}, u32[]{:S(2)}, u32[]{:S(2)}) collective-permute-start(bf16[2,2,128,128]{3,2,1,0:T(8,128)(2,1)S(1)} %get-tuple-element.26._), channel_id=1, source_target_pairs={{0,8},{1,9},{2,10},{3,11},{4,12},{5,13},{6,14},{7,15},{8,0},{9,1},... | collective-permute-start | bytes 393224 | tf_op jit(solution)/shard_map/ppermute | solution.py:562
  37.4 21.0 %all-to-all-start.1 = ((bf16[4,2,512,128]{3,2,1,0:T(8,128)(2,1)}), bf16[4,2,512,128]{3,2,1,0:T(8,128)(2,1)S(1)}, u32[]{:S(2)}, u32[]{:S(2)}) async-start(bf16[4,2,512,128]{3,2,1,0:T(8,128)(2,1)} %shard_map.124), calls=%async_computation.1 | async-start | bytes 2097152 | tf_op jit(solution)/shard_map/all_to_all | solution.py:566
  41.1 17.2 %copy-start.1 = (s32[2]{0:T(128)S(1)}, s32[2]{0:T(128)}, u32[]{:S(2)}) copy-start(s32[2]{0:T(128)} %length_ref.9) | copy-start | bytes 28
  41.1 17.2 %copy-start.4 = (s32[2]{0:T(128)S(1)}, s32[2]{0:T(128)}, u32[]{:S(2)}) copy-start(s32[2]{0:T(128)} %count_ref.3) | copy-start | bytes 28
  64.5 7.4 %collective-permute-start.9 = (f32[2,8,256]{2,1,0:T(8,128)S(1)}, f32[2,8,256]{2,1,0:T(8,128)S(1)}, u32[]{:S(2)}, u32[]{:S(2)}) collective-permute-start(f32[2,8,256]{2,1,0:T(8,128)S(1)} %get-tuple-element.30), channel_id=1, source_target_pairs={{8,0},{9,1},{10,2},{11,3},{12,4},{13,5},{14,6},{15,7},{24,16},{25,... | collective-permute-start | bytes 49160 | tf_op jit(solution)/shard_map/ppermute | solution.py:570

commit v6 on v4

--- a/solution.py
+++ b/solution.py
@@ -13,7 +13,7 @@
 TILE = 256
 NEG = -1e30
 LOG2E = 1.4426950408889634
-FAR_COST = 10**11
+FAR_COST = 0
 ARRIVED_COST = 10**11
 NEAR_COST = 0
 VMEM_LIMIT = 32 * 1024 * 1024

time: 87 us -> 94 us (1.080)
  waiting for transfers between devices: 20.3 us -> 27.3 us
  starting transfers between devices: 27.9 us -> 25.6 us
  blocking collectives: 14.3 us -> 15.5 us
    ppermute x2, waiting for transfers between devices: 0.01 us -> 10.8 us  [on_device(): sources.append(lax.ppermute(packed[side][step], ('dp', 'seq'), pairs))]
    all_to_all x1, waiting for transfers between devices: 7.1 us -> 1.86 us  [on_device(): near = swap(near, axis_index_groups=parities)]
    ppermute x4, waiting for transfers between devices: 10.2 us -> 14.6 us  [on_device(): far.append(lax.ppermute(piece, 'seq', pairs))]
    all_to_all x1, waiting for transfers between devices: 2.66 us -> 0.01 us  [on_device(): events = swap(split_heads(seq_lengths, arrays), axis_index_groups=groups)]
    all_to_all x1, starting transfers between devices: 7.27 us -> 5.27 us  [on_device(): events = swap(split_heads(seq_lengths, arrays), axis_index_groups=groups)]
    ppermute x2, starting transfers between devices: 2.71 us -> 1.34 us  [on_device(): lax.ppermute(packed[side][users], 'seq', [(i, j ^ side) for i, j in pairs])]
    pallas_call x2, Pallas kernels: 9.49 us -> 10.8 us  [attend(): call(functools.partial(attend_body, scale, depth, half, len(far)), in_spe...]
    ppermute x4, starting transfers between devices: 9.51 us -> 10.8 us  [on_device(): far.append(lax.ppermute(piece, 'seq', pairs))]
  transfers between devices with their start and end apart: 12 -> 12, of which waited for: 6 -> 5; matrix products, arithmetic and copies ran while one was open for 0% -> 0% of each run, Pallas kernels for 14% -> 13%
where the time goes in v6:
time: 94 us; the launch traced here: 93.4 us
  waiting for transfers between devices  27.3 us (29%)
  starting transfers between devices  25.6 us (27%)
  Pallas kernels  23.2 us (25%)
  blocking collectives  15.5 us (16%)
  local copies, waits for them, and re-layouts  0.97 us (1%)
    all_to_all x1, blocking collectives, on_device(): return tuple(join_heads(swap(out, axis_index_groups=groups)))  15.5 us
    ppermute x4, waiting for transfers between devices, on_device(): far.append(lax.ppermute(piece, 'seq', pairs))  14.6 us
    pallas_call x2, Pallas kernels, attend(): call(functools.partial(attend_body, scale, depth, half, len(far)), in_spe...  10.8 us
    ppermute x4, starting transfers between devices, on_device(): far.append(lax.ppermute(piece, 'seq', pairs))  10.8 us
    ppermute x2, waiting for transfers between devices, on_device(): sources.append(lax.ppermute(packed[side][step], ('dp', 'seq'), pairs))  10.8 us
    all_to_all x1, starting transfers between devices, on_device(): events = swap(split_heads(seq_lengths, arrays), axis_index_groups=groups)  5.27 us
    all_to_all x1, starting transfers between devices, on_device(): near = swap(near, axis_index_groups=parities)  4.51 us
    pallas_call x1, Pallas kernels, pack(): call(functools.partial(pack_body, users), limit=VMEM_WHOLE, in_specs=[sme...  3.39 us
  transfers between devices with their start and end apart: 12, of which 5 were waited for; matrix products, arithmetic and copies ran while one was open for 0% of the time, Pallas kernels for 13%

profile of v6, /device:TPU:0, one launch (start us, length us, event | category | flops | bytes accessed | tf_op | source)
XLA Modules:
  0.0 93.4 jit_solution(9535726089482109042)
XLA Ops:
  0.6 2.7 %shard_map.121 = bf16[8,4,128,128]{3,2,1,0:T(8,128)(2,1)} custom-call(s32[2]{0:T(128)} %length_ref.9, bf16[1,128,1024]{2,1,0:T(8,128)(2,1)} %refs_0_.3, bf16[1,128,1024]{2,1,0:T(8,128)(2,1)} %refs_1_.3, bf16[1,128,1024]{2,1,0:T(8,128)(2,1)} %refs_2_.3, bf16[1,128,1024]{2,1,0:T(8,128)(2,1)} %refs_3_.3), custom_call_target="tpu_custom_call" | custom-call | tf_op jit(solution)/shard_map/pallas_call | solution.py:187
  3.3 5.3 %all-to-all-start = ((bf16[8,4,128,128]{3,2,1,0:T(8,128)(2,1)}), bf16[8,4,128,128]{3,2,1,0:T(8,128)(2,1)}, u32[]{:S(2)}, u32[]{:S(2)}) async-start(bf16[8,4,128,128]{3,2,1,0:T(8,128)(2,1)} %shard_map.121), calls=%async_computation | async-start | bytes 2097152 | tf_op jit(solution)/shard_map/all_to_all | solution.py:541
  8.6 3.4 %shard_map.122 = (bf16[4,2,128,128]{3,2,1,0:T(8,128)(2,1)}, bf16[4,2,128,128]{3,2,1,0:T(8,128)(2,1)}, bf16[4,2,128,128]{3,2,1,0:T(8,128)(2,1)}, bf16[4,2,128,128...) custom-call(s32[2]{0:T(128)} %length_ref.9, s32[16]{0:T(128)} %slots_ref.5, ...), custom_call_target="tpu_custom_call" | custom-call | tf_op jit(solution)/shard_map/pallas_call | solution.py:143
  12.0 2.0 %collective-permute-start = (bf16[4,2,128,128]{3,2,1,0:T(8,128)(2,1)}, bf16[4,2,128,128]{3,2,1,0:T(8,128)(2,1)S(1)}, u32[]{:S(2)}, u32[]{:S(2)}) collective-permute-start(bf16[4,2,128,128]{3,2,1,0:T(8,128)(2,1)} %get-tuple-element.20), channel_id=1, source_target_pairs={{0,16},{1,17},{2,18},{3,19},{4,20},{5,21},{6,22},{7,23},{8,24},{9,... | collective-permute-start | bytes 786440 | tf_op jit(solution)/shard_map/ppermute | solution.py:533
  14.0 0.0 collective-permute-start.1
  14.1 0.2 collective-permute-start.2
  14.2 0.7 collective-permute-start.3
  14.9 0.0 copy-start.1
  14.9 0.0 copy-start.3
  14.9 0.7 collective-permute-start.4
  15.6 5.8 %collective-permute-done.refs_0_.refs_4_ = bf16[4,2,128,128]{3,2,1,0:T(8,128)(2,1)S(1)} collective-permute-done((bf16[4,2,128,128]{3,2,1,0:T(8,128)(2,1)}, bf16[4,2,128,128]{3,2,1,0:T(8,128)(2,1)S(1)}, u32[]{:S(2)}, u32[]{:S(2)}) %collective-permute-start) | collective-permute-done | bytes 262176 | tf_op jit(solution)/shard_map/ppermute | solution.py:533
  21.4 5.0 %collective-permute-done.1.refs_1_.refs_5_ = bf16[4,2,128,128]{3,2,1,0:T(8,128)(2,1)S(1)} collective-permute-done((bf16[4,2,128,128]{3,2,1,0:T(8,128)(2,1)}, bf16[4,2,128,128]{3,2,1,0:T(8,128)(2,1)S(1)}, u32[]{:S(2)}, u32[]{:S(2)}) %collective-permute-start.1) | collective-permute-done | bytes 262176 | tf_op jit(solution)/shard_map/ppermute | solution.py:533
  26.4 0.0 collective-permute-done.2.refs_3_
  26.4 0.0 collective-permute-done.3.refs_4_.refs_0_
  26.4 0.0 collective-permute-done.4.refs_5_.refs_1_
  26.4 0.0 copy-start
  26.4 0.9 %copy-done = bf16[4,2,128,128]{3,2,1,0:T(8,128)(2,1)S(1)} copy-done((bf16[4,2,128,128]{3,2,1,0:T(8,128)(2,1)S(1)}, bf16[4,2,128,128]{3,2,1,0:T(8,128)(2,1)}, u32[]{:S(2)}) %copy-start) | copy-done | bytes 262168
  27.4 1.1 %shard_map.123 = (bf16[2,2,128,128]{3,2,1,0:T(8,128)(2,1)S(1)}, bf16[2,2,128,128]{3,2,1,0:T(8,128)(2,1)S(1)}, bf16[2,2,128,128]{3,2,1,0:T(8,128)(2,1)S(1)}, bf16[2,2,128,128]{3,2,1,0:T(8,128)(2,1)S(1)}) custom-call(s32[16]{0:T(128)S(1)} %copy-done.3, s32[2,4]{1,0:T(2,128)S(1)} %copy-done.1, ...), custom_call_target="tpu_custom_call" | custom-call | tf_op jit(solution)/shard_map/pallas_call | solution.py:232
  28.5 7.2 %collective-permute-start.6 = (bf16[2,2,128,128]{3,2,1,0:T(8,128)(2,1)S(1)}, bf16[2,2,128,128]{3,2,1,0:T(8,128)(2,1)S(1)}, u32[]{:S(2)}, u32[]{:S(2)}) collective-permute-start(bf16[2,2,128,128]{3,2,1,0:T(8,128)(2,1)S(1)} %get-tuple-element.27), channel_id=1, source_target_pairs={{0,10},{1,11},{2,8},{3,9},{4,14},{5,15},{6,12},{7,13},{8,2},{9,3},... | collective-permute-start | bytes 393224 | tf_op jit(solution)/shard_map/ppermute | solution.py:551
  35.7 1.5 %collective-permute-start.7 = (bf16[2,2,128,128]{3,2,1,0:T(8,128)(2,1)S(1)}, bf16[2,2,128,128]{3,2,1,0:T(8,128)(2,1)S(1)}, u32[]{:S(2)}, u32[]{:S(2)}) collective-permute-start(bf16[2,2,128,128]{3,2,1,0:T(8,128)(2,1)S(1)} %get-tuple-element.28), channel_id=1, source_target_pairs={{0,12},{1,13},{2,14},{3,15},{4,8},{5,9},{6,10},{7,11},{8,4},{9,5},... | collective-permute-start | bytes 393224 | tf_op jit(solution)/shard_map/ppermute | solution.py:551
  37.2 2.0 %collective-permute-start.8 = (bf16[2,2,128,128]{3,2,1,0:T(8,128)(2,1)S(1)}, bf16[2,2,128,128]{3,2,1,0:T(8,128)(2,1)S(1)}, u32[]{:S(2)}, u32[]{:S(2)}) collective-permute-start(bf16[2,2,128,128]{3,2,1,0:T(8,128)(2,1)S(1)} %get-tuple-element.29), channel_id=1, source_target_pairs={{0,14},{1,15},{2,12},{3,13},{4,10},{5,11},{6,8},{7,9},{8,6},{9,7},... | collective-permute-start | bytes 393224 | tf_op jit(solution)/shard_map/ppermute | solution.py:551
  39.2 2.1 %shard_map.124 = bf16[4,2,512,128]{3,2,1,0:T(8,128)(2,1)} custom-call(s32[16]{0:T(128)S(1)} %copy-done.3, s32[2,4]{1,0:T(2,128)S(1)} %copy-done.1, bf16[2,2,128,128]{3,2,1,0:T(8,128)(2,1)S(1)} %get-tuple-element.26._, bf16[4,2,128,128]{3,2,1,0:T(8,128)(2,1)S(1)} %collective-permute-done.3.refs_4_.refs_0_, ...), custom_call_target="tpu_custom_call" | custom-call | tf_op jit(solution)/shard_map/pallas_call | solution.py:267
  41.3 4.5 %all-to-all-start.1 = ((bf16[4,2,512,128]{3,2,1,0:T(8,128)(2,1)}), bf16[4,2,512,128]{3,2,1,0:T(8,128)(2,1)S(1)}, u32[]{:S(2)}, u32[]{:S(2)}) async-start(bf16[4,2,512,128]{3,2,1,0:T(8,128)(2,1)} %shard_map.124), calls=%async_computation.1 | async-start | bytes 2097152 | tf_op jit(solution)/shard_map/all_to_all | solution.py:555
  45.8 5.6 %collective-permute-done.6.refs_1_ = bf16[2,2,128,128]{3,2,1,0:T(8,128)(2,1)S(1)} collective-permute-done((bf16[2,2,128,128]{3,2,1,0:T(8,128)(2,1)S(1)}, bf16[2,2,128,128]{3,2,1,0:T(8,128)(2,1)S(1)}, u32[]{:S(2)}, u32[]{:S(2)}) %collective-permute-start.6) | collective-permute-done | bytes 131104 | tf_op jit(solution)/shard_map/ppermute | solution.py:551
  51.4 9.1 %collective-permute-done.5.refs_0_ = bf16[2,2,128,128]{3,2,1,0:T(8,128)(2,1)S(1)} collective-permute-done((bf16[2,2,128,128]{3,2,1,0:T(8,128)(2,1)S(1)}, bf16[2,2,128,128]{3,2,1,0:T(8,128)(2,1)S(1)}, u32[]{:S(2)}, u32[]{:S(2)}) %collective-permute-start.5) | collective-permute-done | bytes 131104 | tf_op jit(solution)/shard_map/ppermute | solution.py:551
  60.4 1.9 %all-to-all-done.1.near_ref = bf16[4,2,512,128]{3,2,1,0:T(8,128)(2,1)S(1)} async-done(((bf16[4,2,512,128]{3,2,1,0:T(8,128)(2,1)}), bf16[4,2,512,128]{3,2,1,0:T(8,128)(2,1)S(1)}, u32[]{:S(2)}, u32[]{:S(2)}) %all-to-all-start.1) | async-done | bytes 1048608 | tf_op jit(solution)/shard_map/all_to_all | solution.py:555
  62.3 5.3 %shard_map.126 = (bf16[4,128,128]{2,1,0:T(8,128)(2,1)S(1)}, f32[512,128]{1,0:T(8,128)S(1)}, f32[512,128]{1,0:T(8,128)S(1)}, f32[2,8,256]{2,1,0:T(8,128)S(1)}) custom-call(s32[2]{0:T(128)S(1)} %copy-done.2, s32[2]{0:T(128)S(1)} %copy-done.4, f32[8,128]{1,0:T(8,128)S(1)} %shard_map.125._, bf16[8,4,128,128]{3,2,1,0:T(8,128)(2,1)} %all-to-all-done.ev_ref, ...), custom_call_target="tpu_custom_call" | custom-call | flops 1677721600 | bytes 1310720 | tf_op jit(solution)/shard_map/pallas_call | solution.py:404
  67.6 1.5 %collective-permute-start.9 = (f32[2,8,256]{2,1,0:T(8,128)S(1)}, f32[2,8,256]{2,1,0:T(8,128)S(1)}, u32[]{:S(2)}, u32[]{:S(2)}) collective-permute-start(f32[2,8,256]{2,1,0:T(8,128)S(1)} %get-tuple-element.30), channel_id=1, source_target_pairs={{8,0},{9,1},{10,2},{11,3},{12,4},{13,5},{14,6},{15,7},{24,16},{25,... | collective-permute-start | bytes 49160 | tf_op jit(solution)/shard_map/ppermute | solution.py:559
  69.1 5.5 %shard_map.127 = (bf16[4,128,128]{2,1,0:T(8,128)(2,1)S(1)}, f32[1024,128]{1,0:T(8,128)S(1)}, f32[1024,128]{1,0:T(8,128)S(1)}) custom-call(s32[2]{0:T(128)S(1)} %copy-done.2, s32[2]{0:T(128)S(1)} %copy-done.4, f32[8,128]{1,0:T(8,128)S(1)} %shard_map.125._, bf16[8,4,128,128]{3,2,1,0:T(8,128)(2,1)} %all-to-all-done.ev_ref, ...), custom_call_target="tpu_custom_call" | custom-call | flops 1677721600 | bytes 1310720 | tf_op jit(solution)/shard_map/pallas_call | solution.py:404
  74.6 2.1 %shard_map.128 = bf16[8,3,128,128]{3,2,1,0:T(8,128)(2,1)S(1)} custom-call(s32[2]{0:T(128)S(1)} %copy-done.2, bf16[8,4,128,128]{3,2,1,0:T(8,128)(2,1)} %all-to-all-done.ev_ref, bf16[4,2,512,128]{3,2,1,0:T(8,128)(2,1)S(1)} %all-to-all-done.1.near_ref, f32[2,8,256]{2,1,0:T(8,128)S(1)} %collective-permute-done.9.stats_ref, ...), custom_call_target="tpu_custom_call" | custom-call | tf_op jit(solution)/shard_map/pallas_call | solution.py:463
  76.8 15.5 %all_to_all.15.in_ref = bf16[8,3,128,128]{3,2,1,0:T(8,128)(2,1)S(1)} all-to-all(bf16[8,3,128,128]{3,2,1,0:T(8,128)(2,1)S(1)} %shard_map.128), channel_id=1, replica_groups={{0,1,2,3,4,5,6,7},{8,9,10,11,12,13,14,15},{16,17,18,19,20,21,22,23},{24..., dimensions={0} | all-to-all | bytes 1572864 | tf_op jit(solution)/shard_map/all_to_all | solution.py:562
  92.3 1.0 %shard_map.129 = (bf16[1,128,1024]{2,1,0:T(8,128)(2,1)}, bf16[1,128,1024]{2,1,0:T(8,128)(2,1)}, bf16[1,128,1024]{2,1,0:T(8,128)(2,1)}) custom-call(bf16[8,3,128,128]{3,2,1,0:T(8,128)(2,1)S(1)} %all_to_all.15.in_ref), custom_call_target="tpu_custom_call" | custom-call | tf_op jit(solution)/shard_map/pallas_call | solution.py:489
  (12 shorter events, 0.0 us)
Async XLA Ops:
  3.3 37.9 %all-to-all-start = ((bf16[8,4,128,128]{3,2,1,0:T(8,128)(2,1)}), bf16[8,4,128,128]{3,2,1,0:T(8,128)(2,1)}, u32[]{:S(2)}, u32[]{:S(2)}) async-start(bf16[8,4,128,128]{3,2,1,0:T(8,128)(2,1)} %shard_map.121), calls=%async_computation | async-start | bytes 2097152 | tf_op jit(solution)/shard_map/all_to_all | solution.py:541
  12.0 9.4 %collective-permute-start = (bf16[4,2,128,128]{3,2,1,0:T(8,128)(2,1)}, bf16[4,2,128,128]{3,2,1,0:T(8,128)(2,1)S(1)}, u32[]{:S(2)}, u32[]{:S(2)}) collective-permute-start(bf16[4,2,128,128]{3,2,1,0:T(8,128)(2,1)} %get-tuple-element.20), channel_id=1, source_target_pairs={{0,16},{1,17},{2,18},{3,19},{4,20},{5,21},{6,22},{7,23},{8,24},{9,... | collective-permute-start | bytes 786440 | tf_op jit(solution)/shard_map/ppermute | solution.py:533
  14.0 12.3 %collective-permute-start.1 = (bf16[4,2,128,128]{3,2,1,0:T(8,128)(2,1)}, bf16[4,2,128,128]{3,2,1,0:T(8,128)(2,1)S(1)}, u32[]{:S(2)}, u32[]{:S(2)}) collective-permute-start(bf16[4,2,128,128]{3,2,1,0:T(8,128)(2,1)} %get-tuple-element.21), channel_id=1, source_target_pairs={{0,17},{1,16},{2,19},{3,18},{4,21},{5,20},{6,23},{7,22},{8,25},{9,... | collective-permute-start | bytes 786440 | tf_op jit(solution)/shard_map/ppermute | solution.py:533
  14.1 12.3 %collective-permute-start.2 = (bf16[4,2,128,128]{3,2,1,0:T(8,128)(2,1)}, bf16[4,2,128,128]{3,2,1,0:T(8,128)(2,1)S(1)}, u32[]{:S(2)}, u32[]{:S(2)}) collective-permute-start(bf16[4,2,128,128]{3,2,1,0:T(8,128)(2,1)} %get-tuple-element.23), channel_id=1, source_target_pairs={{0,1},{1,0},{2,3},{3,2},{4,5},{5,4},{6,7},{7,6},{8,9},{9,8},{10,11... | collective-permute-start | bytes 786440 | tf_op jit(solution)/shard_map/ppermute | solution.py:526
  14.2 12.1 %collective-permute-start.3 = (bf16[4,2,128,128]{3,2,1,0:T(8,128)(2,1)}, bf16[4,2,128,128]{3,2,1,0:T(8,128)(2,1)S(1)}, u32[]{:S(2)}, u32[]{:S(2)}) collective-permute-start(bf16[4,2,128,128]{3,2,1,0:T(8,128)(2,1)} %get-tuple-element.24), channel_id=1, source_target_pairs={{4,8},{5,9},{6,10},{7,11},{8,4},{9,5},{10,6},{11,7},{20,24},{21,25... | collective-permute-start | bytes 786440 | tf_op jit(solution)/shard_map/ppermute | solution.py:537
  14.9 11.5 %copy-start.1 = (s32[2,4]{1,0:T(2,128)S(1)}, s32[2,4]{1,0:T(2,128)}, u32[]{:S(2)}) copy-start(s32[2,4]{1,0:T(2,128)} %lists_ref.5) | copy-start | bytes 100
  14.9 11.5 %copy-start.3 = (s32[16]{0:T(128)S(1)}, s32[16]{0:T(128)}, u32[]{:S(2)}) copy-start(s32[16]{0:T(128)} %slots_ref.5) | copy-start | bytes 196
  14.9 11.5 %collective-permute-start.4 = (bf16[4,2,128,128]{3,2,1,0:T(8,128)(2,1)}, bf16[4,2,128,128]{3,2,1,0:T(8,128)(2,1)S(1)}, u32[]{:S(2)}, u32[]{:S(2)}) collective-permute-start(bf16[4,2,128,128]{3,2,1,0:T(8,128)(2,1)} %get-tuple-element.25), channel_id=1, source_target_pairs={{4,9},{5,8},{6,11},{7,10},{8,5},{9,4},{10,7},{11,6},{20,25},{21,24... | collective-permute-start | bytes 786440 | tf_op jit(solution)/shard_map/ppermute | solution.py:537
  26.4 1.0 %copy-start = (bf16[4,2,128,128]{3,2,1,0:T(8,128)(2,1)S(1)}, bf16[4,2,128,128]{3,2,1,0:T(8,128)(2,1)}, u32[]{:S(2)}) copy-start(bf16[4,2,128,128]{3,2,1,0:T(8,128)(2,1)} %get-tuple-element.22.refs_2_) | copy-start | bytes 786436
  28.5 22.9 %collective-permute-start.6 = (bf16[2,2,128,128]{3,2,1,0:T(8,128)(2,1)S(1)}, bf16[2,2,128,128]{3,2,1,0:T(8,128)(2,1)S(1)}, u32[]{:S(2)}, u32[]{:S(2)}) collective-permute-start(bf16[2,2,128,128]{3,2,1,0:T(8,128)(2,1)S(1)} %get-tuple-element.27), channel_id=1, source_target_pairs={{0,10},{1,11},{2,8},{3,9},{4,14},{5,15},{6,12},{7,13},{8,2},{9,3},... | collective-permute-start | bytes 393224 | tf_op jit(solution)/shard_map/ppermute | solution.py:551
  35.7 15.7 %collective-permute-start.7 = (bf16[2,2,128,128]{3,2,1,0:T(8,128)(2,1)S(1)}, bf16[2,2,128,128]{3,2,1,0:T(8,128)(2,1)S(1)}, u32[]{:S(2)}, u32[]{:S(2)}) collective-permute-start(bf16[2,2,128,128]{3,2,1,0:T(8,128)(2,1)S(1)} %get-tuple-element.28), channel_id=1, source_target_pairs={{0,12},{1,13},{2,14},{3,15},{4,8},{5,9},{6,10},{7,11},{8,4},{9,5},... | collective-permute-start | bytes 393224 | tf_op jit(solution)/shard_map/ppermute | solution.py:551
  37.2 14.2 %collective-permute-start.8 = (bf16[2,2,128,128]{3,2,1,0:T(8,128)(2,1)S(1)}, bf16[2,2,128,128]{3,2,1,0:T(8,128)(2,1)S(1)}, u32[]{:S(2)}, u32[]{:S(2)}) collective-permute-start(bf16[2,2,128,128]{3,2,1,0:T(8,128)(2,1)S(1)} %get-tuple-element.29), channel_id=1, source_target_pairs={{0,14},{1,15},{2,12},{3,13},{4,10},{5,11},{6,8},{7,9},{8,6},{9,7},... | collective-permute-start | bytes 393224 | tf_op jit(solution)/shard_map/ppermute | solution.py:551
  39.2 21.2 %collective-permute-start.5 = (bf16[2,2,128,128]{3,2,1,0:T(8,128)(2,1)S(1)}, bf16[2,2,128,128]{3,2,1,0:T(8,128)(2,1)S(1)}, u32[]{:S(2)}, u32[]{:S(2)}) collective-permute-start(bf16[2,2,128,128]{3,2,1,0:T(8,128)(2,1)S(1)} %get-tuple-element.26._), channel_id=1, source_target_pairs={{0,8},{1,9},{2,10},{3,11},{4,12},{5,13},{6,14},{7,15},{8,0},{9,1},... | collective-permute-start | bytes 393224 | tf_op jit(solution)/shard_map/ppermute | solution.py:551
  41.3 21.0 %all-to-all-start.1 = ((bf16[4,2,512,128]{3,2,1,0:T(8,128)(2,1)}), bf16[4,2,512,128]{3,2,1,0:T(8,128)(2,1)S(1)}, u32[]{:S(2)}, u32[]{:S(2)}) async-start(bf16[4,2,512,128]{3,2,1,0:T(8,128)(2,1)} %shard_map.124), calls=%async_computation.1 | async-start | bytes 2097152 | tf_op jit(solution)/shard_map/all_to_all | solution.py:555
  45.8 16.5 %copy-start.2 = (s32[2]{0:T(128)S(1)}, s32[2]{0:T(128)}, u32[]{:S(2)}) copy-start(s32[2]{0:T(128)} %length_ref.9) | copy-start | bytes 28
  45.8 16.5 %copy-start.4 = (s32[2]{0:T(128)S(1)}, s32[2]{0:T(128)}, u32[]{:S(2)}) copy-start(s32[2]{0:T(128)} %count_ref.3) | copy-start | bytes 28
  67.6 7.0 %collective-permute-start.9 = (f32[2,8,256]{2,1,0:T(8,128)S(1)}, f32[2,8,256]{2,1,0:T(8,128)S(1)}, u32[]{:S(2)}, u32[]{:S(2)}) collective-permute-start(f32[2,8,256]{2,1,0:T(8,128)S(1)} %get-tuple-element.30), channel_id=1, source_target_pairs={{8,0},{9,1},{10,2},{11,3},{12,4},{13,5},{14,6},{15,7},{24,16},{25,... | collective-permute-start | bytes 49160 | tf_op jit(solution)/shard_map/ppermute | solution.py:559

commit v7 on v4

--- a/solution.py
+++ b/solution.py
@@ -435,26 +435,33 @@
     out_ref[last, 0] = gq1[...]
     put(first, 1, gk0[...] + gk1[:WINDOW])
     put(first, 2, gv0[...] + gv1[:WINDOW])
-    k = ev_ref[early:, 1].reshape(WINDOW, hd)
-    v = ev_ref[early:, 2].reshape(WINDOW, hd)
-    gk = jnp.zeros((WINDOW, hd), jnp.float32)
-    gv = jnp.zeros((WINDOW, hd), jnp.float32)
-    kpos = base + span - WINDOW + lax.broadcasted_iota(jnp.int32, (WINDOW, TILE), 0)
-    for tile in range(WINDOW // TILE):
-        pairs = early // 2 + tile * TILE // (2 * rows)
-        pairs = slice(pairs, pairs + TILE // (2 * rows))
-        q = near_ref[pairs, 0, near:].reshape(TILE, hd)
-        g = near_ref[pairs, 1, near:].reshape(TILE, hd)
-        qpos = base + span + tile * TILE + lax.broadcasted_iota(jnp.int32, (WINDOW, TILE), 1)
-        allowed = (qpos - kpos < WINDOW) & (kpos < length) & follows
-        s = jnp.where(allowed, dot_nt(k, q) * slope - stats_ref[tile, 0:1], NEG)
-        p = jnp.exp2(s)
-        d = dot_nt(v, g)
-        ds = p * (d - stats_ref[tile, 1:2])
-        gk += dot_nn(ds.astype(jnp.bfloat16), q)
-        gv += dot_nn(p.astype(jnp.bfloat16), g)
-    put(last, 1, gk1[WINDOW:] + gk * scale)
-    put(last, 2, gv1[WINDOW:] + gv)
+    line = lax.broadcasted_iota(jnp.int32, (TILE, TILE), 0)
+    column = lax.broadcasted_iota(jnp.int32, (TILE, TILE), 1)
+    blocks = TILE // rows
+    for chunk in range(WINDOW // TILE):
+        mine = slice(early + chunk * blocks, early + (chunk + 1) * blocks)
+        k = ev_ref[mine, 1].reshape(TILE, hd)
+        v = ev_ref[mine, 2].reshape(TILE, hd)
+        gk = jnp.zeros((TILE, hd), jnp.float32)
+        gv = jnp.zeros((TILE, hd), jnp.float32)
+        kpos = base + span - WINDOW + chunk * TILE + line
+        for tile in range(chunk + 1):
+            pairs = early // 2 + tile * TILE // (2 * rows)
+            pairs = slice(pairs, pairs + TILE // (2 * rows))
+            q = near_ref[pairs, 0, near:].reshape(TILE, hd)
+            g = near_ref[pairs, 1, near:].reshape(TILE, hd)
+            allowed = (kpos < length) & follows
+            if tile == chunk:
+                allowed = allowed & (column < line)
+            s = jnp.where(allowed, dot_nt(k, q) * slope - stats_ref[tile, 0:1], NEG)
+            p = jnp.exp2(s)
+            d = dot_nt(v, g)
+            ds = p * (d - stats_ref[tile, 1:2])
+            gk += dot_nn(ds.astype(jnp.bfloat16), q)
+            gv += dot_nn(p.astype(jnp.bfloat16), g)
+        here = slice(WINDOW + chunk * TILE, WINDOW + (chunk + 1) * TILE)
+        for part, value in ((1, gk1[here] + gk * scale), (2, gv1[here] + gv)):
+            out_ref[mine, part] = value.astype(out_ref.dtype).reshape(blocks, rows, hd)
 
 
 def finish(scale, seq_lengths, events, near, stats, halves):

time: 87 us -> 86.8 us (level)
  no operation moved by 1% of the time
where the time goes in v7:
time: 86.8 us; the launch traced here: 86.3 us
  starting transfers between devices  27.9 us (32%)
  Pallas kernels  22.3 us (26%)
  waiting for transfers between devices  20.3 us (23%)
  blocking collectives  14.3 us (16%)
  between operations  0.92 us (1%)
    all_to_all x1, blocking collectives, on_device(): return tuple(join_heads(swap(out, axis_index_groups=groups)))  14.3 us
    ppermute x4, waiting for transfers between devices, on_device(): far.append(lax.ppermute(piece, 'seq', pairs))  10.2 us
    ppermute x4, starting transfers between devices, on_device(): far.append(lax.ppermute(piece, 'seq', pairs))  9.51 us
    pallas_call x2, Pallas kernels, attend(): call(functools.partial(attend_body, scale, depth, half, len(far)), in_spe...  9.49 us
    all_to_all x1, starting transfers between devices, on_device(): events = swap(split_heads(seq_lengths, arrays), axis_index_groups=groups)  7.27 us
    all_to_all x1, waiting for transfers between devices, on_device(): near = swap(near, axis_index_groups=parities)  7.1 us
    all_to_all x1, starting transfers between devices, on_device(): near = swap(near, axis_index_groups=parities)  3.72 us
    pallas_call x1, Pallas kernels, pack(): call(functools.partial(pack_body, users), limit=VMEM_WHOLE, in_specs=[sme...  3.37 us
  transfers between devices with their start and end apart: 12, of which 6 were waited for; matrix products, arithmetic and copies ran while one was open for 0% of the time, Pallas kernels for 14%

profile of v7, /device:TPU:0, one launch (start us, length us, event | category | flops | bytes accessed | tf_op | source)
XLA Modules:
  0.0 86.3 jit_solution(13311688037540281642)
XLA Ops:
  0.6 3.4 %shard_map.122 = (bf16[4,2,128,128]{3,2,1,0:T(8,128)(2,1)}, bf16[4,2,128,128]{3,2,1,0:T(8,128)(2,1)}, bf16[4,2,128,128]{3,2,1,0:T(8,128)(2,1)}, bf16[4,2,128,128...) custom-call(s32[2]{0:T(128)} %length_ref.9, s32[16]{0:T(128)} %slots_ref.5, ...), custom_call_target="tpu_custom_call" | custom-call | tf_op jit(solution)/shard_map/pallas_call | solution.py:143
  4.0 3.0 %collective-permute-start = (bf16[4,2,128,128]{3,2,1,0:T(8,128)(2,1)}, bf16[4,2,128,128]{3,2,1,0:T(8,128)(2,1)}, u32[]{:S(2)}, u32[]{:S(2)}) collective-permute-start(bf16[4,2,128,128]{3,2,1,0:T(8,128)(2,1)} %get-tuple-element.20), channel_id=1, source_target_pairs={{0,16},{1,17},{2,18},{3,19},{4,20},{5,21},{6,22},{7,23},{8,24},{9,... | collective-permute-start | bytes 786440 | tf_op jit(solution)/shard_map/ppermute | solution.py:540
  7.0 0.2 collective-permute-start.2
  7.2 1.4 %collective-permute-start.3 = (bf16[4,2,128,128]{3,2,1,0:T(8,128)(2,1)}, bf16[4,2,128,128]{3,2,1,0:T(8,128)(2,1)}, u32[]{:S(2)}, u32[]{:S(2)}) collective-permute-start(bf16[4,2,128,128]{3,2,1,0:T(8,128)(2,1)} %get-tuple-element.24), channel_id=1, source_target_pairs={{4,8},{5,9},{6,10},{7,11},{8,4},{9,5},{10,6},{11,7},{20,24},{21,25... | collective-permute-start | bytes 786440 | tf_op jit(solution)/shard_map/ppermute | solution.py:544
  8.6 1.3 %collective-permute-start.4 = (bf16[4,2,128,128]{3,2,1,0:T(8,128)(2,1)}, bf16[4,2,128,128]{3,2,1,0:T(8,128)(2,1)}, u32[]{:S(2)}, u32[]{:S(2)}) collective-permute-start(bf16[4,2,128,128]{3,2,1,0:T(8,128)(2,1)} %get-tuple-element.25), channel_id=1, source_target_pairs={{4,9},{5,8},{6,11},{7,10},{8,5},{9,4},{10,7},{11,6},{20,25},{21,24... | collective-permute-start | bytes 786440 | tf_op jit(solution)/shard_map/ppermute | solution.py:544
  9.9 2.7 %shard_map.121 = bf16[8,4,128,128]{3,2,1,0:T(8,128)(2,1)} custom-call(s32[2]{0:T(128)} %length_ref.9, bf16[1,128,1024]{2,1,0:T(8,128)(2,1)} %refs_0_.3, bf16[1,128,1024]{2,1,0:T(8,128)(2,1)} %refs_1_.3, bf16[1,128,1024]{2,1,0:T(8,128)(2,1)} %refs_2_.3, bf16[1,128,1024]{2,1,0:T(8,128)(2,1)} %refs_3_.3), custom_call_target="tpu_custom_call" | custom-call | tf_op jit(solution)/shard_map/pallas_call | solution.py:187
  12.6 0.0 copy-start
  12.7 7.3 %all-to-all-start = ((bf16[8,4,128,128]{3,2,1,0:T(8,128)(2,1)}), bf16[8,4,128,128]{3,2,1,0:T(8,128)(2,1)S(1)}, u32[]{:S(2)}, u32[]{:S(2)}) async-start(bf16[8,4,128,128]{3,2,1,0:T(8,128)(2,1)} %shard_map.121), calls=%async_computation | async-start | bytes 2097152 | tf_op jit(solution)/shard_map/all_to_all | solution.py:548
  19.9 0.0 copy-start.3
  20.0 0.0 collective-permute-done.refs_0_.refs_4_
  20.0 0.0 collective-permute-done.1.refs_1_.refs_5_
  20.0 0.0 collective-permute-done.3.refs_4_.refs_0_
  20.0 0.0 collective-permute-done.4.refs_5_.refs_1_
  20.0 0.6 copy-done.2
  20.6 1.7 %shard_map.123 = (bf16[2,2,128,128]{3,2,1,0:T(8,128)(2,1)S(1)}, bf16[2,2,128,128]{3,2,1,0:T(8,128)(2,1)S(1)}, bf16[2,2,128,128]{3,2,1,0:T(8,128)(2,1)S(1)}, bf16[2,2,128,128]{3,2,1,0:T(8,128)(2,1)S(1)}) custom-call(s32[16]{0:T(128)S(1)} %copy-done.3, s32[2,4]{1,0:T(2,128)S(1)} %copy-done.2, bf16[4,2,128,128]{3,2,1,0:T(8,128)(2,1)} %collective-permute-done.refs_0_.refs_4_, ...), custom_call_target="tpu_custom_call" | custom-call | flops 99999997952 | tf_op jit(solution)/shard_map/pallas_call | solution.py:232
  22.3 5.7 %collective-permute-start.6 = (bf16[2,2,128,128]{3,2,1,0:T(8,128)(2,1)S(1)}, bf16[2,2,128,128]{3,2,1,0:T(8,128)(2,1)S(1)}, u32[]{:S(2)}, u32[]{:S(2)}) collective-permute-start(bf16[2,2,128,128]{3,2,1,0:T(8,128)(2,1)S(1)} %get-tuple-element.27), channel_id=1, source_target_pairs={{0,10},{1,11},{2,8},{3,9},{4,14},{5,15},{6,12},{7,13},{8,2},{9,3},... | collective-permute-start | bytes 393224 | tf_op jit(solution)/shard_map/ppermute | solution.py:558
  28.0 1.4 %collective-permute-start.7 = (bf16[2,2,128,128]{3,2,1,0:T(8,128)(2,1)S(1)}, bf16[2,2,128,128]{3,2,1,0:T(8,128)(2,1)S(1)}, u32[]{:S(2)}, u32[]{:S(2)}) collective-permute-start(bf16[2,2,128,128]{3,2,1,0:T(8,128)(2,1)S(1)} %get-tuple-element.28), channel_id=1, source_target_pairs={{0,12},{1,13},{2,14},{3,15},{4,8},{5,9},{6,10},{7,11},{8,4},{9,5},... | collective-permute-start | bytes 393224 | tf_op jit(solution)/shard_map/ppermute | solution.py:558
  29.4 2.4 %collective-permute-start.8 = (bf16[2,2,128,128]{3,2,1,0:T(8,128)(2,1)S(1)}, bf16[2,2,128,128]{3,2,1,0:T(8,128)(2,1)S(1)}, u32[]{:S(2)}, u32[]{:S(2)}) collective-permute-start(bf16[2,2,128,128]{3,2,1,0:T(8,128)(2,1)S(1)} %get-tuple-element.29), channel_id=1, source_target_pairs={{0,14},{1,15},{2,12},{3,13},{4,10},{5,11},{6,8},{7,9},{8,6},{9,7},... | collective-permute-start | bytes 393224 | tf_op jit(solution)/shard_map/ppermute | solution.py:558
  31.8 2.8 %shard_map.124 = bf16[4,2,512,128]{3,2,1,0:T(8,128)(2,1)} custom-call(s32[16]{0:T(128)S(1)} %copy-done.3, s32[2,4]{1,0:T(2,128)S(1)} %copy-done.2, bf16[2,2,128,128]{3,2,1,0:T(8,128)(2,1)S(1)} %get-tuple-element.26._, bf16[4,2,128,128]{3,2,1,0:T(8,128)(2,1)} %collective-permute-done.3.refs_4_.refs_0_, ...), custom_call_target="tpu_custom_call" | custom-call | tf_op jit(solution)/shard_map/pallas_call | solution.py:267
  34.5 2.7 %all-to-all-done.ev_ref = bf16[8,4,128,128]{3,2,1,0:T(8,128)(2,1)S(1)} async-done(((bf16[8,4,128,128]{3,2,1,0:T(8,128)(2,1)}), bf16[8,4,128,128]{3,2,1,0:T(8,128)(2,1)S(1)}, u32[]{:S(2)}, u32[]{:S(2)}) %all-to-all-start) | async-done | bytes 1048608 | tf_op jit(solution)/shard_map/all_to_all | solution.py:548
  37.2 3.7 %all-to-all-start.1 = ((bf16[4,2,512,128]{3,2,1,0:T(8,128)(2,1)}), bf16[4,2,512,128]{3,2,1,0:T(8,128)(2,1)S(1)}, u32[]{:S(2)}, u32[]{:S(2)}) async-start(bf16[4,2,512,128]{3,2,1,0:T(8,128)(2,1)} %shard_map.124), calls=%async_computation.1 | async-start | bytes 2097152 | tf_op jit(solution)/shard_map/all_to_all | solution.py:562
  40.9 0.9 collective-permute-done.7.refs_2_
  41.8 3.8 %collective-permute-done.8.refs_3_ = bf16[2,2,128,128]{3,2,1,0:T(8,128)(2,1)S(1)} collective-permute-done((bf16[2,2,128,128]{3,2,1,0:T(8,128)(2,1)S(1)}, bf16[2,2,128,128]{3,2,1,0:T(8,128)(2,1)S(1)}, u32[]{:S(2)}, u32[]{:S(2)}) %collective-permute-start.8) | collective-permute-done | bytes 131104 | tf_op jit(solution)/shard_map/ppermute | solution.py:558
  45.6 5.5 %collective-permute-done.5.refs_0_ = bf16[2,2,128,128]{3,2,1,0:T(8,128)(2,1)S(1)} collective-permute-done((bf16[2,2,128,128]{3,2,1,0:T(8,128)(2,1)S(1)}, bf16[2,2,128,128]{3,2,1,0:T(8,128)(2,1)S(1)}, u32[]{:S(2)}, u32[]{:S(2)}) %collective-permute-start.5) | collective-permute-done | bytes 131104 | tf_op jit(solution)/shard_map/ppermute | solution.py:558
  51.1 7.1 %all-to-all-done.1.near_ref = bf16[4,2,512,128]{3,2,1,0:T(8,128)(2,1)S(1)} async-done(((bf16[4,2,512,128]{3,2,1,0:T(8,128)(2,1)}), bf16[4,2,512,128]{3,2,1,0:T(8,128)(2,1)S(1)}, u32[]{:S(2)}, u32[]{:S(2)}) %all-to-all-start.1) | async-done | bytes 1048608 | tf_op jit(solution)/shard_map/all_to_all | solution.py:562
  58.2 4.6 %shard_map.126 = (bf16[4,128,128]{2,1,0:T(8,128)(2,1)S(1)}, f32[512,128]{1,0:T(8,128)S(1)}, f32[512,128]{1,0:T(8,128)S(1)}, f32[2,8,256]{2,1,0:T(8,128)S(1)}) custom-call(s32[2]{0:T(128)S(1)} %copy-done.1, s32[2]{0:T(128)S(1)} %copy-done.4, f32[8,128]{1,0:T(8,128)S(1)} %shard_map.125._, bf16[8,4,128,128]{3,2,1,0:T(8,128)(2,1)S(1)} %all-to-all-done.ev_ref, ...), custom_call_target="tpu_custom_call" | custom-call | flops 1677721600 | bytes 1310720 | tf_op jit(solution)/shard_map/pallas_call | solution.py:404
  62.9 1.5 %collective-permute-start.9 = (f32[2,8,256]{2,1,0:T(8,128)S(1)}, f32[2,8,256]{2,1,0:T(8,128)S(1)}, u32[]{:S(2)}, u32[]{:S(2)}) collective-permute-start(f32[2,8,256]{2,1,0:T(8,128)S(1)} %get-tuple-element.30), channel_id=1, source_target_pairs={{8,0},{9,1},{10,2},{11,3},{12,4},{13,5},{14,6},{15,7},{24,16},{25,... | collective-permute-start | bytes 49160 | tf_op jit(solution)/shard_map/ppermute | solution.py:566
  64.4 4.8 %shard_map.127 = (bf16[4,128,128]{2,1,0:T(8,128)(2,1)S(1)}, f32[1024,128]{1,0:T(8,128)S(1)}, f32[1024,128]{1,0:T(8,128)S(1)}) custom-call(s32[2]{0:T(128)S(1)} %copy-done.1, s32[2]{0:T(128)S(1)} %copy-done.4, f32[8,128]{1,0:T(8,128)S(1)} %shard_map.125._, bf16[8,4,128,128]{3,2,1,0:T(8,128)(2,1)S(1)} %all-to-all-done.ev_ref, ...), custom_call_target="tpu_custom_call" | custom-call | flops 1677721600 | bytes 1310720 | tf_op jit(solution)/shard_map/pallas_call | solution.py:404
  69.2 0.4 collective-permute-done.9.stats_ref
  69.6 1.3 %shard_map.128 = bf16[8,3,128,128]{3,2,1,0:T(8,128)(2,1)S(1)} custom-call(s32[2]{0:T(128)S(1)} %copy-done.1, bf16[8,4,128,128]{3,2,1,0:T(8,128)(2,1)S(1)} %all-to-all-done.ev_ref, bf16[4,2,512,128]{3,2,1,0:T(8,128)(2,1)S(1)} %all-to-all-done.1.near_ref, f32[2,8,256]{2,1,0:T(8,128)S(1)} %collective-permute-done.9.stats_ref, ...), custom_call_target="tpu_custom_call" | custom-call | tf_op jit(solution)/shard_map/pallas_call | solution.py:470
  70.9 14.3 %all_to_all.15.in_ref = bf16[8,3,128,128]{3,2,1,0:T(8,128)(2,1)S(1)} all-to-all(bf16[8,3,128,128]{3,2,1,0:T(8,128)(2,1)S(1)} %shard_map.128), channel_id=1, replica_groups={{0,1,2,3,4,5,6,7},{8,9,10,11,12,13,14,15},{16,17,18,19,20,21,22,23},{24..., dimensions={0} | all-to-all | bytes 1572864 | tf_op jit(solution)/shard_map/all_to_all | solution.py:569
  85.2 1.0 %shard_map.129 = (bf16[1,128,1024]{2,1,0:T(8,128)(2,1)}, bf16[1,128,1024]{2,1,0:T(8,128)(2,1)}, bf16[1,128,1024]{2,1,0:T(8,128)(2,1)}) custom-call(bf16[8,3,128,128]{3,2,1,0:T(8,128)(2,1)S(1)} %all_to_all.15.in_ref), custom_call_target="tpu_custom_call" | custom-call | tf_op jit(solution)/shard_map/pallas_call | solution.py:496
  (12 shorter events, 0.0 us)
Async XLA Ops:
  4.0 15.9 %collective-permute-start = (bf16[4,2,128,128]{3,2,1,0:T(8,128)(2,1)}, bf16[4,2,128,128]{3,2,1,0:T(8,128)(2,1)}, u32[]{:S(2)}, u32[]{:S(2)}) collective-permute-start(bf16[4,2,128,128]{3,2,1,0:T(8,128)(2,1)} %get-tuple-element.20), channel_id=1, source_target_pairs={{0,16},{1,17},{2,18},{3,19},{4,20},{5,21},{6,22},{7,23},{8,24},{9,... | collective-permute-start | bytes 786440 | tf_op jit(solution)/shard_map/ppermute | solution.py:540
  7.0 13.0 %collective-permute-start.1 = (bf16[4,2,128,128]{3,2,1,0:T(8,128)(2,1)}, bf16[4,2,128,128]{3,2,1,0:T(8,128)(2,1)}, u32[]{:S(2)}, u32[]{:S(2)}) collective-permute-start(bf16[4,2,128,128]{3,2,1,0:T(8,128)(2,1)} %get-tuple-element.21), channel_id=1, source_target_pairs={{0,17},{1,16},{2,19},{3,18},{4,21},{5,20},{6,23},{7,22},{8,25},{9,... | collective-permute-start | bytes 786440 | tf_op jit(solution)/shard_map/ppermute | solution.py:540
  7.0 13.0 %collective-permute-start.2 = (bf16[4,2,128,128]{3,2,1,0:T(8,128)(2,1)}, bf16[4,2,128,128]{3,2,1,0:T(8,128)(2,1)}, u32[]{:S(2)}, u32[]{:S(2)}) collective-permute-start(bf16[4,2,128,128]{3,2,1,0:T(8,128)(2,1)} %get-tuple-element.23), channel_id=1, source_target_pairs={{0,1},{1,0},{2,3},{3,2},{4,5},{5,4},{6,7},{7,6},{8,9},{9,8},{10,11... | collective-permute-start | bytes 786440 | tf_op jit(solution)/shard_map/ppermute | solution.py:533
  7.2 12.8 %collective-permute-start.3 = (bf16[4,2,128,128]{3,2,1,0:T(8,128)(2,1)}, bf16[4,2,128,128]{3,2,1,0:T(8,128)(2,1)}, u32[]{:S(2)}, u32[]{:S(2)}) collective-permute-start(bf16[4,2,128,128]{3,2,1,0:T(8,128)(2,1)} %get-tuple-element.24), channel_id=1, source_target_pairs={{4,8},{5,9},{6,10},{7,11},{8,4},{9,5},{10,6},{11,7},{20,24},{21,25... | collective-permute-start | bytes 786440 | tf_op jit(solution)/shard_map/ppermute | solution.py:544
  8.6 11.4 %collective-permute-start.4 = (bf16[4,2,128,128]{3,2,1,0:T(8,128)(2,1)}, bf16[4,2,128,128]{3,2,1,0:T(8,128)(2,1)}, u32[]{:S(2)}, u32[]{:S(2)}) collective-permute-start(bf16[4,2,128,128]{3,2,1,0:T(8,128)(2,1)} %get-tuple-element.25), channel_id=1, source_target_pairs={{4,9},{5,8},{6,11},{7,10},{8,5},{9,4},{10,7},{11,6},{20,25},{21,24... | collective-permute-start | bytes 786440 | tf_op jit(solution)/shard_map/ppermute | solution.py:544
  12.6 7.4 %copy-start = (bf16[4,2,128,128]{3,2,1,0:T(8,128)(2,1)S(1)}, bf16[4,2,128,128]{3,2,1,0:T(8,128)(2,1)}, u32[]{:S(2)}) copy-start(bf16[4,2,128,128]{3,2,1,0:T(8,128)(2,1)} %get-tuple-element.22.refs_2_) | copy-start | bytes 786436
  12.7 24.5 %all-to-all-start = ((bf16[8,4,128,128]{3,2,1,0:T(8,128)(2,1)}), bf16[8,4,128,128]{3,2,1,0:T(8,128)(2,1)S(1)}, u32[]{:S(2)}, u32[]{:S(2)}) async-start(bf16[8,4,128,128]{3,2,1,0:T(8,128)(2,1)} %shard_map.121), calls=%async_computation | async-start | bytes 2097152 | tf_op jit(solution)/shard_map/all_to_all | solution.py:548
  19.9 0.7 copy-start.2
  19.9 0.7 copy-start.3
  22.3 18.7 %collective-permute-start.6 = (bf16[2,2,128,128]{3,2,1,0:T(8,128)(2,1)S(1)}, bf16[2,2,128,128]{3,2,1,0:T(8,128)(2,1)S(1)}, u32[]{:S(2)}, u32[]{:S(2)}) collective-permute-start(bf16[2,2,128,128]{3,2,1,0:T(8,128)(2,1)S(1)} %get-tuple-element.27), channel_id=1, source_target_pairs={{0,10},{1,11},{2,8},{3,9},{4,14},{5,15},{6,12},{7,13},{8,2},{9,3},... | collective-permute-start | bytes 393224 | tf_op jit(solution)/shard_map/ppermute | solution.py:558
  28.0 13.8 %collective-permute-start.7 = (bf16[2,2,128,128]{3,2,1,0:T(8,128)(2,1)S(1)}, bf16[2,2,128,128]{3,2,1,0:T(8,128)(2,1)S(1)}, u32[]{:S(2)}, u32[]{:S(2)}) collective-permute-start(bf16[2,2,128,128]{3,2,1,0:T(8,128)(2,1)S(1)} %get-tuple-element.28), channel_id=1, source_target_pairs={{0,12},{1,13},{2,14},{3,15},{4,8},{5,9},{6,10},{7,11},{8,4},{9,5},... | collective-permute-start | bytes 393224 | tf_op jit(solution)/shard_map/ppermute | solution.py:558
  29.4 16.2 %collective-permute-start.8 = (bf16[2,2,128,128]{3,2,1,0:T(8,128)(2,1)S(1)}, bf16[2,2,128,128]{3,2,1,0:T(8,128)(2,1)S(1)}, u32[]{:S(2)}, u32[]{:S(2)}) collective-permute-start(bf16[2,2,128,128]{3,2,1,0:T(8,128)(2,1)S(1)} %get-tuple-element.29), channel_id=1, source_target_pairs={{0,14},{1,15},{2,12},{3,13},{4,10},{5,11},{6,8},{7,9},{8,6},{9,7},... | collective-permute-start | bytes 393224 | tf_op jit(solution)/shard_map/ppermute | solution.py:558
  31.8 19.3 %collective-permute-start.5 = (bf16[2,2,128,128]{3,2,1,0:T(8,128)(2,1)S(1)}, bf16[2,2,128,128]{3,2,1,0:T(8,128)(2,1)S(1)}, u32[]{:S(2)}, u32[]{:S(2)}) collective-permute-start(bf16[2,2,128,128]{3,2,1,0:T(8,128)(2,1)S(1)} %get-tuple-element.26._), channel_id=1, source_target_pairs={{0,8},{1,9},{2,10},{3,11},{4,12},{5,13},{6,14},{7,15},{8,0},{9,1},... | collective-permute-start | bytes 393224 | tf_op jit(solution)/shard_map/ppermute | solution.py:558
  37.2 21.0 %all-to-all-start.1 = ((bf16[4,2,512,128]{3,2,1,0:T(8,128)(2,1)}), bf16[4,2,512,128]{3,2,1,0:T(8,128)(2,1)S(1)}, u32[]{:S(2)}, u32[]{:S(2)}) async-start(bf16[4,2,512,128]{3,2,1,0:T(8,128)(2,1)} %shard_map.124), calls=%async_computation.1 | async-start | bytes 2097152 | tf_op jit(solution)/shard_map/all_to_all | solution.py:562
  40.9 17.3 %copy-start.1 = (s32[2]{0:T(128)S(1)}, s32[2]{0:T(128)}, u32[]{:S(2)}) copy-start(s32[2]{0:T(128)} %length_ref.9) | copy-start | bytes 28
  40.9 17.3 %copy-start.4 = (s32[2]{0:T(128)S(1)}, s32[2]{0:T(128)}, u32[]{:S(2)}) copy-start(s32[2]{0:T(128)} %count_ref.3) | copy-start | bytes 28
  62.9 6.7 %collective-permute-start.9 = (f32[2,8,256]{2,1,0:T(8,128)S(1)}, f32[2,8,256]{2,1,0:T(8,128)S(1)}, u32[]{:S(2)}, u32[]{:S(2)}) collective-permute-start(f32[2,8,256]{2,1,0:T(8,128)S(1)} %get-tuple-element.30), channel_id=1, source_target_pairs={{8,0},{9,1},{10,2},{11,3},{12,4},{13,5},{14,6},{15,7},{24,16},{25,... | collective-permute-start | bytes 49160 | tf_op jit(solution)/shard_map/ppermute | solution.py:566
